TPU v7x, 32 devices: a whole 2x2x4 slice. The times are simulated.
32 devices in a mesh: dp: 8 (over z, x), tp: 4 (over y, core).
Axes of the slice: x: 2, y: 2, z: 4, core: 2. Of those that a mesh axis runs over, the one named last changes fastest.
Arguments:
- query_stream: bfloat16 [32, 1024, 512], P('dp', 'tp'), may hold values from -6 to 6
- token_embed: bfloat16 [32, 1024, 512], P('dp', 'tp'), may hold values from -6 to 6
- encoder_out: bfloat16 [32, 1024, 512], P('dp', 'tp'), may hold values from -6 to 6
- out_grad: bfloat16 [32, 1024, 512], P('dp', 'tp'), may hold values from -6 to 6
- attn_q: bfloat16 [512, 512], P('dp', 'tp'), may hold values from -0.25 to 0.25
- attn_k: bfloat16 [512, 512], P('dp', 'tp'), may hold values from -0.25 to 0.25
- attn_v: bfloat16 [512, 512], P('dp', 'tp'), may hold values from -0.25 to 0.25
- attn_o: bfloat16 [512, 512], P('tp', 'dp'), may hold values from -1 to 1
- cross_q: bfloat16 [512, 512], P('dp', 'tp'), may hold values from -0.25 to 0.25
- cross_k: bfloat16 [512, 512], P('dp', 'tp'), may hold values from -0.25 to 0.25
- cross_v: bfloat16 [512, 512], P('dp', 'tp'), may hold values from -0.25 to 0.25
- cross_o: bfloat16 [512, 512], P('tp', 'dp'), may hold values from -1 to 1
- ffn_in: bfloat16 [512, 2048], P('dp', 'tp'), may hold values from -0.25 to 0.25
- ffn_bias_in: bfloat16 [2048], P(('tp', 'dp')), may hold values from -3 to 3
- ffn_out: bfloat16 [2048, 512], P('tp', 'dp'), may hold values from -0.125 to 0.125
- ffn_bias_out: float32 [512], replicated, may hold values from -3 to 3
- norm_gain: float32 [3, 512], replicated, may hold values from 0.1 to 1.9
- norm_bias: float32 [3, 512], replicated, may hold values from -2 to 2
- doc_lengths: int32 [32, 8], P('dp'), may hold values from 1 to 1017, as said below
- src_lengths: int32 [32, 8], P('dp'), may hold values from 1 to 1017, as said below
- ctx_rank: int32 [32, 1024], P('dp'), may hold values from 0 to 1023
- ctx_limit: int32 [32, 1024], P('dp'), may hold values from 1 to 1024
Outputs:
- mixed: bfloat16 [32, 1024, 512], P('dp', 'tp')
- grad_query: float32 [32, 1024, 512], P('dp', 'tp')
- grad_embed: float32 [32, 1024, 512], P('dp', 'tp')
- grad_encoder: float32 [32, 1024, 512], P('dp', 'tp')
- grad_attn_q: float32 [512, 512], P('dp', 'tp')
- grad_attn_k: float32 [512, 512], P('dp', 'tp')
- grad_attn_v: float32 [512, 512], P('dp', 'tp')
- grad_attn_o: float32 [512, 512], P('tp', 'dp')
- grad_cross_q: float32 [512, 512], P('dp', 'tp')
- grad_cross_k: float32 [512, 512], P('dp', 'tp')
- grad_cross_v: float32 [512, 512], P('dp', 'tp')
- grad_cross_o: float32 [512, 512], P('tp', 'dp')
- grad_ffn_in: float32 [512, 2048], P('dp', 'tp')
- grad_ffn_bias_in: float32 [2048], P(('tp', 'dp'))
- grad_ffn_out: float32 [2048, 512], P('tp', 'dp')
- grad_ffn_bias_out: float32 [512], replicated
- grad_norm_gain: float32 [3, 512], replicated
- grad_norm_bias: float32 [3, 512], replicated
Inputs may be any that keep to these rules, and one draw needn't show every extreme that they name: `doc_lengths`: in every row the 8 lengths sum to 1024; one of them, at a slot drawn from the seed, is a document that takes the rest of the row, the others are sentences of at most 32 tokens; in one row drawn from the seed all those sentences have one token. `src_lengths`: in every row the 8 lengths sum to 1024; one of them, at a slot drawn from the seed, is a source document that takes the rest of the row, the others are sentences of at most 32 tokens; in one row drawn from the seed all those sentences have one token.
All inputs are finite; a program needn't handle non-finite values.
Results may differ from a plain program's by a relative error of at most 0.025.
Values may be sent and summed in bfloat16 or wider, within the bound.
A program may use at most 192 MiB of HBM per device.

v0:
```python
import jax
import jax.numpy as jnp
from jax import lax
from jax.sharding import PartitionSpec as P

HEADS = 8


EPSILON = 1e-05
score_tile = 512


def layer_norm(values, scale_vec, shift_vec):
    average = jnp.mean(values, axis=-1, keepdims=True)
    centred = values - average
    spread = jnp.mean(centred * centred, axis=-1, keepdims=True)
    return centred * lax.rsqrt(spread + EPSILON) * scale_vec + shift_vec


def gelu_exact(values):
    return 0.5 * values * (1.0 + lax.erf(values * 0.7071067811865476))


def project(inputs, matrix):
    return jnp.einsum("rld,de->rle", inputs, matrix, preferred_element_type=jnp.float32)


def project_back(cotangent, matrix):
    return jnp.einsum("rle,de->rld", cotangent, matrix, preferred_element_type=jnp.float32)


def outer_sum(inputs, cotangent):
    return jnp.einsum("rld,rle->de", inputs, cotangent, preferred_element_type=jnp.float32)


def layout(lengths, length):
    offsets = jnp.cumsum(lengths) - lengths
    positions = jnp.arange(length, dtype=jnp.int32)
    passed = positions[:, None] >= offsets[None, :]
    document = jnp.sum(passed.astype(jnp.int32), axis=1) - 1
    doc_start = jnp.max(jnp.where(passed, offsets[None, :], 0), axis=1)
    return (document, doc_start)


def self_visible(lengths, rank_row, limit_row, length, first_row, block_rows):
    document, doc_start = layout(lengths, length)
    positions = jnp.arange(length, dtype=jnp.int32)
    rows_pos = positions[first_row : first_row + block_rows]
    same_text = document[first_row : first_row + block_rows, None] == document[None, :]
    chosen = (rank_row[None, :] < limit_row[first_row : first_row + block_rows, None]) & (
        rows_pos[:, None] != positions[None, :]
    )
    opener = positions[None, :] == doc_start[first_row : first_row + block_rows, None]
    return same_text & (chosen | opener)


def cross_visible(lengths, src_lengths, length, src_length, first_row, block_rows):
    document, _ = layout(lengths, length)
    source_doc, _ = layout(src_lengths, src_length)
    return document[first_row : first_row + block_rows, None] == source_doc[None, :]


def attend_forward(queries, keys_all, values_all, visible_of, head_count):
    query_count = queries.shape[0]
    head_size = queries.shape[1] // head_count
    factor = head_size ** (-0.5)
    queries = queries.reshape(query_count, head_count, head_size)
    keys_all = keys_all.reshape(keys_all.shape[0], head_count, head_size)
    values_all = values_all.reshape(values_all.shape[0], head_count, head_size)
    block_rows = min(score_tile, query_count)
    outputs = []
    totals = []
    for first_row in range(0, query_count, block_rows):
        query_part = queries[first_row : first_row + block_rows]
        scores = (
            jnp.einsum("qhd,khd->hqk", query_part, keys_all, preferred_element_type=jnp.float32)
            * factor
        )
        scores = jnp.where(visible_of(first_row, block_rows)[None], scores, -1e30)
        highest = jnp.max(scores, axis=-1, keepdims=True)
        exponent = jnp.exp(scores - highest)
        denominator = jnp.sum(exponent, axis=-1, keepdims=True)
        weights_low = (exponent / denominator).astype(jnp.bfloat16)
        outputs.append(
            jnp.einsum("hqk,khd->qhd", weights_low, values_all, preferred_element_type=jnp.float32)
        )
        totals.append(highest[..., 0] + jnp.log(denominator[..., 0]))
    context = jnp.concatenate(outputs, axis=0).reshape(query_count, head_count * head_size)
    return (context, jnp.concatenate(totals, axis=1))


def attend_backward(queries, keys_all, values_all, visible_of, totals, grad_context, head_count):
    query_count = queries.shape[0]
    key_count = keys_all.shape[0]
    head_size = queries.shape[1] // head_count
    factor = head_size ** (-0.5)
    queries = queries.reshape(query_count, head_count, head_size)
    keys_all = keys_all.reshape(key_count, head_count, head_size)
    values_all = values_all.reshape(key_count, head_count, head_size)
    grad_context = grad_context.reshape(query_count, head_count, head_size)
    grad_keys = jnp.zeros((key_count, head_count, head_size), jnp.float32)
    grad_values = jnp.zeros((key_count, head_count, head_size), jnp.float32)
    grad_queries = []
    block_rows = min(score_tile, query_count)
    for first_row in range(0, query_count, block_rows):
        query_part = queries[first_row : first_row + block_rows]
        grad_part = grad_context[first_row : first_row + block_rows]
        scores = (
            jnp.einsum("qhd,khd->hqk", query_part, keys_all, preferred_element_type=jnp.float32)
            * factor
        )
        scores = jnp.where(visible_of(first_row, block_rows)[None], scores, -1e30)
        weights_full = jnp.exp(scores - totals[:, first_row : first_row + block_rows, None])
        grad_weights = jnp.einsum(
            "qhd,khd->hqk", grad_part, values_all, preferred_element_type=jnp.float32
        )
        inner = jnp.sum(grad_weights * weights_full, axis=-1, keepdims=True)
        grad_scores = (weights_full * (grad_weights - inner)).astype(jnp.bfloat16)
        grad_queries.append(
            jnp.einsum("hqk,khd->qhd", grad_scores, keys_all, preferred_element_type=jnp.float32)
            * factor
        )
        grad_keys = (
            grad_keys
            + jnp.einsum(
                "hqk,qhd->khd", grad_scores, query_part, preferred_element_type=jnp.float32
            )
            * factor
        )
        grad_values = grad_values + jnp.einsum(
            "hqk,qhd->khd",
            weights_full.astype(jnp.bfloat16),
            grad_part,
            preferred_element_type=jnp.float32,
        )
    grad_queries = jnp.concatenate(grad_queries, axis=0).reshape(
        query_count, head_count * head_size
    )
    return (
        grad_queries.astype(jnp.bfloat16),
        grad_keys.reshape(key_count, -1).astype(jnp.bfloat16),
        grad_values.reshape(key_count, -1).astype(jnp.bfloat16),
    )


def collect(piece):
    return lax.all_gather(piece, "tp", axis=1, tiled=True)


def spread_sum(partial_sum):
    return lax.psum_scatter(partial_sum, "tp", scatter_dimension=1, tiled=True)


def collect_grad(piece):
    return lax.all_gather(piece, "tp", axis=1, tiled=True)


def send_back(partial_sum):
    return lax.psum_scatter(partial_sum, "tp", scatter_dimension=1, tiled=True)


def local(
    query_stream,
    token_embed,
    encoder_out,
    out_grad,
    attn_q,
    attn_k,
    attn_v,
    attn_o,
    cross_q,
    cross_k,
    cross_v,
    cross_o,
    ffn_in,
    ffn_bias_in,
    ffn_out,
    ffn_bias_out,
    norm_gain,
    norm_bias,
    doc_lengths,
    src_lengths,
    ctx_rank,
    ctx_limit,
):
    head_count = HEADS // lax.axis_size("tp")
    (
        self_query,
        self_key,
        self_value,
        self_out,
        other_query,
        other_key,
        other_value,
        other_out,
        hidden_in,
        hidden_bias,
        hidden_out,
    ) = (
        lax.all_gather(attn_q, "dp", axis=0, tiled=True),
        lax.all_gather(attn_k, "dp", axis=0, tiled=True),
        lax.all_gather(attn_v, "dp", axis=0, tiled=True),
        lax.all_gather(attn_o, "dp", axis=1, tiled=True),
        lax.all_gather(cross_q, "dp", axis=0, tiled=True),
        lax.all_gather(cross_k, "dp", axis=0, tiled=True),
        lax.all_gather(cross_v, "dp", axis=0, tiled=True),
        lax.all_gather(cross_o, "dp", axis=1, tiled=True),
        lax.all_gather(ffn_in, "dp", axis=0, tiled=True),
        lax.all_gather(ffn_bias_in, "dp", axis=0, tiled=True),
        lax.all_gather(ffn_out, "dp", axis=1, tiled=True),
    )

    def self_forward(row_items):
        queries, keys_all, values_all, lengths, rank_row, limit_row = row_items

        def visible_of(first_row, block_rows):
            return self_visible(
                lengths, rank_row, limit_row, keys_all.shape[0], first_row, block_rows
            )

        return attend_forward(queries, keys_all, values_all, visible_of, head_count)

    def self_backward(row_items):
        queries, keys_all, values_all, lengths, rank_row, limit_row, totals, grad_context = (
            row_items
        )

        def visible_of(first_row, block_rows):
            return self_visible(
                lengths, rank_row, limit_row, keys_all.shape[0], first_row, block_rows
            )

        return attend_backward(
            queries, keys_all, values_all, visible_of, totals, grad_context, head_count
        )

    def cross_forward(row_items):
        queries, keys_all, values_all, lengths, source_lengths = row_items

        def visible_of(first_row, block_rows):
            return cross_visible(
                lengths, source_lengths, queries.shape[0], keys_all.shape[0], first_row, block_rows
            )

        return attend_forward(queries, keys_all, values_all, visible_of, head_count)

    def cross_backward(row_items):
        queries, keys_all, values_all, lengths, source_lengths, totals, grad_context = row_items

        def visible_of(first_row, block_rows):
            return cross_visible(
                lengths, source_lengths, queries.shape[0], keys_all.shape[0], first_row, block_rows
            )

        return attend_backward(
            queries, keys_all, values_all, visible_of, totals, grad_context, head_count
        )

    query_all = collect(query_stream)
    embed_all = collect(token_embed)
    source_all = collect(encoder_out)
    self_queries = project(query_all, self_query).astype(jnp.bfloat16)
    self_keys = project(embed_all, self_key).astype(jnp.bfloat16)
    self_values = project(embed_all, self_value).astype(jnp.bfloat16)
    self_context, self_totals = lax.map(
        self_forward, (self_queries, self_keys, self_values, doc_lengths, ctx_rank, ctx_limit)
    )
    self_low = self_context.astype(jnp.bfloat16)
    first_sum = query_stream.astype(jnp.float32) + spread_sum(project(self_low, self_out))
    hidden_one, first_back = jax.vjp(layer_norm, first_sum, norm_gain[0], norm_bias[0])
    hidden_one_all = collect(hidden_one.astype(jnp.bfloat16))
    cross_queries = project(hidden_one_all, other_query).astype(jnp.bfloat16)
    cross_keys = project(source_all, other_key).astype(jnp.bfloat16)
    cross_values = project(source_all, other_value).astype(jnp.bfloat16)
    cross_context, cross_totals = lax.map(
        cross_forward, (cross_queries, cross_keys, cross_values, doc_lengths, src_lengths)
    )
    cross_low = cross_context.astype(jnp.bfloat16)
    second_sum = hidden_one + spread_sum(project(cross_low, other_out))
    hidden_two, second_back = jax.vjp(layer_norm, second_sum, norm_gain[1], norm_bias[1])
    hidden_two_low = hidden_two.astype(jnp.bfloat16)
    ffn_inputs = lax.all_gather(hidden_two_low, "tp", axis=1, tiled=True)
    ffn_pre = project(ffn_inputs, hidden_in) + hidden_bias.astype(jnp.float32)
    ffn_gate, gelu_back = jax.vjp(gelu_exact, ffn_pre)
    ffn_act = ffn_gate.astype(jnp.bfloat16)
    ffn_branch = (
        lax.psum_scatter(project(ffn_act, hidden_out), "tp", scatter_dimension=1, tiled=True)
        + ffn_bias_out
    )
    third_sum = hidden_two + ffn_branch
    mixed_full, third_back = jax.vjp(layer_norm, third_sum, norm_gain[2], norm_bias[2])
    grad_third, gain_two, shift_two = third_back(out_grad.astype(jnp.float32))
    grad_ffn = grad_third.astype(jnp.bfloat16)
    grad_bias_out = jnp.sum(grad_ffn.astype(jnp.float32), axis=(0, 1))
    grad_ffn_all = lax.all_gather(grad_ffn, "tp", axis=1, tiled=True)
    grad_act = project_back(grad_ffn_all, hidden_out)
    grad_down = outer_sum(ffn_act, grad_ffn_all)
    grad_pre = gelu_back(grad_act)[0].astype(jnp.bfloat16)
    grad_up = outer_sum(ffn_inputs, grad_pre)
    grad_bias_in = jnp.sum(grad_pre.astype(jnp.float32), axis=(0, 1))
    grad_two = grad_third + lax.psum_scatter(
        project_back(grad_pre, hidden_in), "tp", scatter_dimension=1, tiled=True
    )
    grad_second, gain_one, shift_one = second_back(grad_two)
    grad_cross_all = collect_grad(grad_second.astype(jnp.bfloat16))
    grad_other_out = outer_sum(cross_low, grad_cross_all)
    grad_cross_ctx = project_back(grad_cross_all, other_out).astype(jnp.bfloat16)
    cross_dq, cross_dk, cross_dv = lax.map(
        cross_backward,
        (
            cross_queries,
            cross_keys,
            cross_values,
            doc_lengths,
            src_lengths,
            cross_totals,
            grad_cross_ctx,
        ),
    )
    grad_other_query = outer_sum(hidden_one_all, cross_dq)
    grad_other_key = outer_sum(source_all, cross_dk)
    grad_other_value = outer_sum(source_all, cross_dv)
    grad_encoder = send_back(
        project_back(cross_dk, other_key) + project_back(cross_dv, other_value)
    )
    grad_one = grad_second + send_back(project_back(cross_dq, other_query))
    grad_first, gain_zero, shift_zero = first_back(grad_one)
    grad_attn_all = collect_grad(grad_first.astype(jnp.bfloat16))
    grad_self_out = outer_sum(self_low, grad_attn_all)
    grad_self_ctx = project_back(grad_attn_all, self_out).astype(jnp.bfloat16)
    self_dq, self_dk, self_dv = lax.map(
        self_backward,
        (
            self_queries,
            self_keys,
            self_values,
            doc_lengths,
            ctx_rank,
            ctx_limit,
            self_totals,
            grad_self_ctx,
        ),
    )
    grad_self_query = outer_sum(query_all, self_dq)
    grad_self_key = outer_sum(embed_all, self_dk)
    grad_self_value = outer_sum(embed_all, self_dv)
    grad_embed = send_back(project_back(self_dk, self_key) + project_back(self_dv, self_value))
    grad_query = grad_first + send_back(project_back(self_dq, self_query))
    (
        grad_self_query,
        grad_self_key,
        grad_self_value,
        grad_self_out,
        grad_other_query,
        grad_other_key,
        grad_other_value,
        grad_other_out,
        grad_up,
        grad_bias_in,
        grad_down,
    ) = (
        lax.psum_scatter(
            grad_self_query.astype(jnp.bfloat16), "dp", scatter_dimension=0, tiled=True
        ).astype(jnp.float32),
        lax.psum_scatter(
            grad_self_key.astype(jnp.bfloat16), "dp", scatter_dimension=0, tiled=True
        ).astype(jnp.float32),
        lax.psum_scatter(
            grad_self_value.astype(jnp.bfloat16), "dp", scatter_dimension=0, tiled=True
        ).astype(jnp.float32),
        lax.psum_scatter(
            grad_self_out.astype(jnp.bfloat16), "dp", scatter_dimension=1, tiled=True
        ).astype(jnp.float32),
        lax.psum_scatter(
            grad_other_query.astype(jnp.bfloat16), "dp", scatter_dimension=0, tiled=True
        ).astype(jnp.float32),
        lax.psum_scatter(
            grad_other_key.astype(jnp.bfloat16), "dp", scatter_dimension=0, tiled=True
        ).astype(jnp.float32),
        lax.psum_scatter(
            grad_other_value.astype(jnp.bfloat16), "dp", scatter_dimension=0, tiled=True
        ).astype(jnp.float32),
        lax.psum_scatter(
            grad_other_out.astype(jnp.bfloat16), "dp", scatter_dimension=1, tiled=True
        ).astype(jnp.float32),
        lax.psum_scatter(
            grad_up.astype(jnp.bfloat16), "dp", scatter_dimension=0, tiled=True
        ).astype(jnp.float32),
        lax.psum_scatter(
            grad_bias_in.astype(jnp.bfloat16), "dp", scatter_dimension=0, tiled=True
        ).astype(jnp.float32),
        lax.psum_scatter(
            grad_down.astype(jnp.bfloat16), "dp", scatter_dimension=1, tiled=True
        ).astype(jnp.float32),
    )
    gain_grads = jnp.stack([gain_zero, gain_one, gain_two])
    shift_grads = jnp.stack([shift_zero, shift_one, shift_two])
    gain_grads, shift_grads, grad_bias_out = lax.psum(
        (gain_grads, shift_grads, grad_bias_out), ("dp", "tp")
    )
    return (
        mixed_full.astype(jnp.bfloat16),
        grad_query,
        grad_embed,
        grad_encoder,
        grad_self_query,
        grad_self_key,
        grad_self_value,
        grad_self_out,
        grad_other_query,
        grad_other_key,
        grad_other_value,
        grad_other_out,
        grad_up,
        grad_bias_in,
        grad_down,
        grad_bias_out,
        gain_grads,
        shift_grads,
    )


def solution(mesh):
    in_specs = (
        P("dp", "tp", None),
        P("dp", "tp", None),
        P("dp", "tp", None),
        P("dp", "tp", None),
        P("dp", "tp"),
        P("dp", "tp"),
        P("dp", "tp"),
        P("tp", "dp"),
        P("dp", "tp"),
        P("dp", "tp"),
        P("dp", "tp"),
        P("tp", "dp"),
        P("dp", "tp"),
        P(("tp", "dp")),
        P("tp", "dp"),
        P(),
        P(),
        P(),
        P("dp", None),
        P("dp", None),
        P("dp", None),
        P("dp", None),
    )
    out_specs = (
        P("dp", "tp", None),
        P("dp", "tp", None),
        P("dp", "tp", None),
        P("dp", "tp", None),
        P("dp", "tp"),
        P("dp", "tp"),
        P("dp", "tp"),
        P("tp", "dp"),
        P("dp", "tp"),
        P("dp", "tp"),
        P("dp", "tp"),
        P("tp", "dp"),
        P("dp", "tp"),
        P(("tp", "dp")),
        P("tp", "dp"),
        P(),
        P(),
        P(),
    )
    return jax.shard_map(local, mesh=mesh, in_specs=in_specs, out_specs=out_specs, check_vma=False)
```

profile of v0, /device:TPU:0, one launch (start us, length us, event | category | flops | bytes accessed | tf_op | source)
XLA Modules:
  0.0 1962.5 jit_solution(1660202006431707567)
XLA Ops:
  8.7 32.6 %all_gather.60 = bf16[512,128]{1,0:T(8,128)(2,1)S(1)} all-gather(bf16[64,128]{1,0:T(8,128)(2,1)} %param.34), channel_id=1, replica_groups=mesh['dp'=8,'tp'=4] {'dp'}, dimensions={0}, use_global_device_ids=true | all-gather | bytes 147456 | tf_op jit(solution)/shard_map/all_gather | solution.py:200
  41.3 30.8 %all_gather.61 = bf16[512,128]{1,0:T(8,128)(2,1)S(1)} all-gather(bf16[64,128]{1,0:T(8,128)(2,1)} %param.35), channel_id=1, replica_groups=mesh['dp'=8,'tp'=4] {'dp'}, dimensions={0}, use_global_device_ids=true | all-gather | bytes 147456 | tf_op jit(solution)/shard_map/all_gather | solution.py:201
  72.1 30.8 %all_gather.58 = bf16[512,128]{1,0:T(8,128)(2,1)S(1)} all-gather(bf16[64,128]{1,0:T(8,128)(2,1)} %param.36), channel_id=1, replica_groups=mesh['dp'=8,'tp'=4] {'dp'}, dimensions={0}, use_global_device_ids=true | all-gather | bytes 147456 | tf_op jit(solution)/shard_map/all_gather | solution.py:202
  102.9 30.7 %all_gather.62 = bf16[128,512]{0,1:T(8,128)(2,1)S(1)} all-gather(bf16[128,64]{0,1:T(8,128)(2,1)} %param.37), channel_id=1, replica_groups=mesh['dp'=8,'tp'=4] {'dp'}, dimensions={1}, use_global_device_ids=true | all-gather | bytes 147456 | tf_op jit(solution)/shard_map/all_gather | solution.py:203
  148.7 50.2 %while.62 = (s32[]{:T(128)}, bf16[4,1024,128]{1,2,0:T(8,128)(2,1)}, f32[4,2,1024]{2,1,0:T(2,128)S(1)}, bf16[4,1024,128]{1,2,0:T(8,128)(2,1)S(1)}, s32[4,8]{1,0:T...) while((s32[]{:T(128)}, bf16[4,1024,128]{1,2,0:T(8,128)(2,1)}, ...), condition=%wide.region_8.9_spmd, body=%wide.region_0.8_spmd.sunk | while | flops 569941056 | bytes 33726900 | solution.py:265
  199.0 6.5 fusion.119
  206.2 9.8 all-gather.15.cloned.1.call-start
  217.2 61.2 %reduce-scatter.29.cloned.1.call-done = f32[4,256,512]{2,1,0:T(8,128)} async-done(((f32[4,1024,512]{2,1,0:T(8,128)}), f32[4,256,512]{2,1,0:T(8,128)}) %reduce-scatter.29.cloned.1.call-update) | async-done | bytes 2097168 | tf_op jit(solution)/shard_map/reduce_scatter | solution.py:151
  282.3 30.6 %all_gather.66 = bf16[512,128]{1,0:T(8,128)(2,1)S(1)} all-gather(bf16[64,128]{1,0:T(8,128)(2,1)S(1)} %copy-done.59), channel_id=1, replica_groups=mesh['dp'=8,'tp'=4] {'dp'}, dimensions={0}, use_global_device_ids=true | all-gather | bytes 147456 | tf_op jit(solution)/shard_map/all_gather | solution.py:204
  312.9 30.5 %all_gather.67 = bf16[512,128]{1,0:T(8,128)(2,1)S(1)} all-gather(bf16[64,128]{1,0:T(8,128)(2,1)S(1)} %copy-done.60), channel_id=1, replica_groups=mesh['dp'=8,'tp'=4] {'dp'}, dimensions={0}, use_global_device_ids=true | all-gather | bytes 147456 | tf_op jit(solution)/shard_map/all_gather | solution.py:205
  343.4 30.5 %all_gather.64 = bf16[512,128]{1,0:T(8,128)(2,1)S(1)} all-gather(bf16[64,128]{1,0:T(8,128)(2,1)S(1)} %copy-done.61), channel_id=1, replica_groups=mesh['dp'=8,'tp'=4] {'dp'}, dimensions={0}, use_global_device_ids=true | all-gather | bytes 147456 | tf_op jit(solution)/shard_map/all_gather | solution.py:206
  373.9 32.5 %all_gather.68 = bf16[128,512]{0,1:T(8,128)(2,1)} all-gather(bf16[128,64]{0,1:T(8,128)(2,1)S(1)} %copy-done.62), channel_id=1, replica_groups=mesh['dp'=8,'tp'=4] {'dp'}, dimensions={1}, use_global_device_ids=true | all-gather | bytes 147456 | tf_op jit(solution)/shard_map/all_gather | solution.py:207
  423.0 42.6 %while.63 = (s32[]{:T(128)}, bf16[4,1024,128]{1,2,0:T(8,128)(2,1)}, f32[4,2,1024]{2,1,0:T(2,128)S(1)}, bf16[4,1024,128]{1,2,0:T(8,128)(2,1)}, s32[4,8]{1,0:T(4,1...) while((s32[]{:T(128)}, bf16[4,1024,128]{1,2,0:T(8,128)(2,1)}, ...), condition=%wide.region_21.22_spmd, body=%wide.region_12.21_spmd.sunk | while | flops 563658880 | bytes 33677984 | solution.py:275
  465.6 6.1 fusion.116
  472.0 71.7 %reduce-scatter.31.cloned.1.call-done = f32[4,256,512]{2,1,0:T(8,128)} async-done(((f32[4,1024,512]{2,1,0:T(8,128)}), f32[4,256,512]{2,1,0:T(8,128)}) %reduce-scatter.31.cloned.1.call-update) | async-done | bytes 2097168 | tf_op jit(solution)/shard_map/reduce_scatter | solution.py:151
  550.2 21.3 %all-reduce = bf16[512]{0:T(512)(128)(2,1)S(1)} all-reduce(bf16[512]{0:T(512)(128)(2,1)S(1)} %dynamic-update-slice), channel_id=1, replica_groups=mesh['dp'=8,'tp'=4] {'dp'}, use_global_device_ids=true, to_apply=%add | all-reduce | flops 512 | bytes 2048
  571.6 31.4 %all_gather.70 = bf16[512,512]{1,0:T(8,128)(2,1)S(1)} all-gather(bf16[64,512]{1,0:T(8,128)(2,1)S(1)} %copy-done.45), channel_id=1, replica_groups=mesh['dp'=8,'tp'=4] {'dp'}, dimensions={0}, use_global_device_ids=true | all-gather | bytes 589824 | tf_op jit(solution)/shard_map/all_gather | solution.py:208
  602.9 31.2 %all_gather.72 = bf16[512,512]{0,1:T(8,128)(2,1)S(1)} all-gather(bf16[512,64]{0,1:T(8,128)(2,1)S(1)} %copy-done.46), channel_id=1, replica_groups=mesh['dp'=8,'tp'=4] {'dp'}, dimensions={1}, use_global_device_ids=true | all-gather | bytes 589824 | tf_op jit(solution)/shard_map/all_gather | solution.py:210
  634.1 7.2 multiply_convert_fusion.4
  643.3 5.6 fusion.109
  649.1 68.1 %reduce-scatter.33.cloned.1.call-done = f32[4,256,512]{2,1,0:T(8,128)} async-done(((f32[4,1024,512]{2,1,0:T(8,128)}), f32[4,256,512]{2,1,0:T(8,128)}) %reduce-scatter.33.cloned.1.call-update) | async-done | bytes 2097168 | tf_op jit(solution)/shard_map/reduce_scatter | solution.py:287
  725.5 34.2 %all-gather.19.cloned.1.call-done = bf16[4,1024,512]{2,1,0:T(8,128)(2,1)} async-done(((bf16[4,256,512]{2,1,0:T(8,128)(2,1)}), bf16[4,1024,512]{2,1,0:T(8,128)(2,1)}) %all-gather.19.cloned.1.call-update) | async-done | bytes 4194320 | tf_op jit(solution)/shard_map/all_gather | solution.py:295
  759.6 9.6 fusion.162
  771.1 5.8 fusion.111
  777.0 71.8 %reduce-scatter.35.cloned.1.call-done = f32[4,256,512]{2,1,0:T(8,128)} async-done(((f32[4,1024,512]{2,1,0:T(8,128)}), f32[4,256,512]{2,1,0:T(8,128)}) %reduce-scatter.35.cloned.1.call-update) | async-done | bytes 2097168 | tf_op jit(solution)/shard_map/reduce_scatter | solution.py:301
  848.8 4.9 multiply_reduce_fusion.4
  857.2 34.6 %all-gather.21.cloned.1.call-done = bf16[4,1024,512]{2,1,0:T(8,128)(2,1)} async-done(((bf16[4,256,512]{2,1,0:T(8,128)(2,1)}), bf16[4,1024,512]{2,1,0:T(8,128)(2,1)}) %all-gather.21.cloned.1.call-update) | async-done | bytes 4194320 | tf_op jit(solution)/shard_map/all_gather | solution.py:155
  897.5 76.8 %while.64 = (s32[]{:T(128)}, bf16[4,1024,128]{1,2,0:T(8,128)(2,1)}, bf16[4,1024,128]{1,2,0:T(8,128)(2,1)S(1)}, bf16[4,1024,128]{1,2,0:T(8,128)(2,1)S(1)}, bf16[4...) while((s32[]{:T(128)}, bf16[4,1024,128]{1,2,0:T(8,128)(2,1)}, ...), condition=%wide.region_40.41_spmd, body=%wide.region_33.40_spmd.sunk | while | flops 1376172160 | bytes 77447896 | solution.py:308
  974.4 6.5 fusion.126
  981.0 71.8 %reduce-scatter.37.cloned.1.call-done = f32[4,256,512]{2,1,0:T(8,128)} async-done(((f32[4,1024,512]{2,1,0:T(8,128)}), f32[4,256,512]{2,1,0:T(8,128)}) %reduce-scatter.37.cloned.1.call-update) | async-done | bytes 2097168 | tf_op jit(solution)/shard_map/reduce_scatter | solution.py:159
  1059.8 6.6 fusion.94
  1066.5 7.6 fusion.93
  1100.2 91.7 %while.65 = (s32[]{:T(128)}, bf16[4,1024,128]{1,2,0:T(8,128)(2,1)}, bf16[4,1024,128]{1,2,0:T(8,128)(2,1)S(1)}, bf16[4,1024,128]{1,2,0:T(8,128)(2,1)S(1)}, bf16[4...) while((s32[]{:T(128)}, bf16[4,1024,128]{1,2,0:T(8,128)(2,1)}, ...), condition=%wide.region_50.51_spmd, body=%wide.region_44.50_spmd.sunk | while | flops 1382454272 | bytes 77496800 | solution.py:331
  1203.6 4.9 fusion.98
  1208.6 5.7 fusion.136
  1230.0 21.3 %all-reduce.1 = bf16[512]{0:T(512)(128)(2,1)S(1)} all-reduce(bf16[512]{0:T(512)(128)(2,1)S(1)} %copy-done.76), channel_id=19, replica_groups=mesh['dp'=8,'tp'=4] {'dp'}, use_global_device_ids=true, to_apply=%region_64.65.clone | all-reduce | flops 512 | bytes 2048
  1254.9 32.8 %reduce-scatter.61.cloned.1.call-done = bf16[64,128]{1,0:T(8,128)(2,1)} async-done(((bf16[512,128]{1,0:T(8,128)(2,1)}), bf16[64,128]{1,0:T(8,128)(2,1)}) %reduce-scatter.61.cloned.1.call-update) | async-done | bytes 16400
  1289.3 61.9 %reduce-scatter.63.cloned.1.call-done = bf16[64,128]{1,0:T(8,128)(2,1)} async-done(((bf16[512,128]{1,0:T(8,128)(2,1)}), bf16[64,128]{1,0:T(8,128)(2,1)}) %reduce-scatter.63.cloned.1.call-update) | async-done | bytes 16400
  1352.7 61.9 %reduce-scatter.49.cloned.1.call-done = bf16[128,64]{0,1:T(8,128)(2,1)} async-done(((bf16[128,512]{0,1:T(8,128)(2,1)}), bf16[128,64]{0,1:T(8,128)(2,1)}) %reduce-scatter.49.cloned.1.call-update) | async-done | bytes 16400 | tf_op jit(solution)/shard_map/reduce_scatter | solution.py:383
  1416.0 62.3 %reduce-scatter.47.cloned.1.call-done = bf16[64,128]{1,0:T(8,128)(2,1)} async-done(((bf16[512,128]{1,0:T(8,128)(2,1)}), bf16[64,128]{1,0:T(8,128)(2,1)}) %reduce-scatter.47.cloned.1.call-update) | async-done | bytes 16400 | tf_op jit(solution)/shard_map/reduce_scatter | solution.py:374
  1479.7 40.6 %all-reduce.2 = (f32[512]{0:T(512)}, f32[3,512]{1,0:T(4,128)}, f32[3,512]{1,0:T(4,128)}) all-reduce(f32[512]{0:T(512)S(1)} %copy-done.64, f32[3,512]{1,0:T(4,128)S(1)} %get-tuple-element.953, f32[3,512]{1,0:T(4,128)S(1)} %get-tuple-element.954), channel_id=1, replica_groups=mesh['dp'=8,'tp'=4] {'dp','tp'}, use_global_device_ids=true, to_apply=%region_67.68 | all-reduce | flops 3584 | bytes 28672 | tf_op jit(solution)/shard_map/psum | solution.py:398
  1520.3 21.5 %reduce-scatter.55.cloned.1.call-done = bf16[64,128]{1,0:T(8,128)(2,1)} async-done(((bf16[512,128]{1,0:T(8,128)(2,1)}), bf16[64,128]{1,0:T(8,128)(2,1)}) %reduce-scatter.55.cloned.1.call-update) | async-done | bytes 16400
  1543.3 62.0 %reduce-scatter.57.cloned.1.call-done = bf16[64,128]{1,0:T(8,128)(2,1)} async-done(((bf16[512,128]{1,0:T(8,128)(2,1)}), bf16[64,128]{1,0:T(8,128)(2,1)}) %reduce-scatter.57.cloned.1.call-update) | async-done | bytes 16400
  1606.9 62.1 %reduce-scatter.59.cloned.1.call-done = bf16[64,128]{1,0:T(8,128)(2,1)} async-done(((bf16[512,128]{1,0:T(8,128)(2,1)}), bf16[64,128]{1,0:T(8,128)(2,1)}) %reduce-scatter.59.cloned.1.call-update) | async-done | bytes 16400
  1670.5 62.0 %reduce-scatter.45.cloned.1.call-done = bf16[128,64]{0,1:T(8,128)(2,1)} async-done(((bf16[128,512]{0,1:T(8,128)(2,1)}), bf16[128,64]{0,1:T(8,128)(2,1)}) %reduce-scatter.45.cloned.1.call-update) | async-done | bytes 16400 | tf_op jit(solution)/shard_map/reduce_scatter | solution.py:371
  1733.8 72.1 %reduce-scatter.39.cloned.1.call-done = f32[4,256,512]{2,1,0:T(8,128)} async-done(((f32[4,1024,512]{2,1,0:T(8,128)}), f32[4,256,512]{2,1,0:T(8,128)}) %reduce-scatter.39.cloned.1.call-update) | async-done | bytes 2097168 | tf_op jit(solution)/shard_map/reduce_scatter | solution.py:159
  1809.1 71.7 %reduce-scatter.43.cloned.1.call-done = f32[4,256,512]{2,1,0:T(8,128)} async-done(((f32[4,1024,512]{2,1,0:T(8,128)}), f32[4,256,512]{2,1,0:T(8,128)}) %reduce-scatter.43.cloned.1.call-update) | async-done | bytes 2097168 | tf_op jit(solution)/shard_map/reduce_scatter | solution.py:159
  1880.8 74.9 %reduce-scatter.41.cloned.1.call-done = f32[4,256,512]{2,1,0:T(8,128)} async-done(((f32[4,1024,512]{2,1,0:T(8,128)}), f32[4,256,512]{2,1,0:T(8,128)}) %reduce-scatter.41.cloned.1.call-update) | async-done | bytes 2097168 | tf_op jit(solution)/shard_map/reduce_scatter | solution.py:159
  (793 shorter events, 402.6 us)
Async XLA Ops:
  7.2 126.4 %all-gather.9.cloned.1.call-start = ((), (), s32[]{:S(2)}) async-start(), calls=%async_computation.18 | async-start | bytes 5242880 | tf_op jit(solution)/shard_map/all_gather | solution.py:147
  7.9 133.8 %all-gather.11.cloned.1.call-start = ((), (), s32[]{:S(2)}) async-start(), calls=%async_computation.19 | async-start | bytes 5242880 | tf_op jit(solution)/shard_map/all_gather | solution.py:147
  8.7 269.7 %reduce-scatter.29.cloned.1.call-start = ((), (), s32[]{:S(2)}) async-start(), calls=%async_computation.20 | async-start | bytes 10485760 | tf_op jit(solution)/shard_map/reduce_scatter | solution.py:151
  41.3 100.4 %copy-start.29 = (bf16[512,128]{1,0:T(8,128)(2,1)}, bf16[512,128]{1,0:T(8,128)(2,1)S(1)}, u32[]{:S(2)}) copy-start(bf16[512,128]{1,0:T(8,128)(2,1)S(1)} %all_gather.60) | copy-start | bytes 393220
  205.6 200.8 %all-gather.13.cloned.1.call-start = ((), (), s32[]{:S(2)}) async-start(), calls=%async_computation.21 | async-start | bytes 5242880 | tf_op jit(solution)/shard_map/all_gather | solution.py:147
  206.2 209.8 %all-gather.15.cloned.1.call-start = ((), (), s32[]{:S(2)}) async-start(), calls=%async_computation.22 | async-start | bytes 5242880 | tf_op jit(solution)/shard_map/all_gather | solution.py:147
  216.6 327.1 %copy-start.47 = (f32[1,512]{1,0:T(1,128)}, f32[1,512]{1,0:T(1,128)S(1)}, u32[]{:S(2)}) copy-start(f32[1,512]{1,0:T(1,128)S(1)} %get-tuple-element.940) | copy-start | bytes 6148
  280.3 263.4 %copy-start = (f32[4,256,512]{2,1,0:T(8,128)}, f32[4,256,512]{2,1,0:T(8,128)S(1)}, u32[]{:S(2)}) copy-start(f32[4,256,512]{2,1,0:T(8,128)S(1)} %get-tuple-element.869) | copy-start | bytes 6291460
  280.3 93.6 %copy-start.62 = (bf16[128,64]{0,1:T(8,128)(2,1)S(1)}, bf16[128,64]{0,1:T(8,128)(2,1)}, u32[]{:S(2)}) copy-start(bf16[128,64]{0,1:T(8,128)(2,1)} %param.41) | copy-start | bytes 49156
  280.4 263.4 %copy-start.41 = (f32[4,256]{1,0:T(4,128)}, f32[4,256]{1,0:T(4,128)S(1)}, u32[]{:S(2)}) copy-start(f32[4,256]{1,0:T(4,128)S(1)} %broadcast_multiply_fusion.2) | copy-start | bytes 12292
  280.8 125.6 %copy-start.52 = (f32[4,256]{1,0:T(4,128)}, f32[4,256]{1,0:T(4,128)S(1)}, u32[]{:S(2)}) copy-start(f32[4,256]{1,0:T(4,128)S(1)} %multiply_reduce_fusion.10) | copy-start | bytes 12292
  280.8 262.9 %copy-start.43 = (f32[4,256]{1,0:T(4,128)}, f32[4,256]{1,0:T(4,128)S(1)}, u32[]{:S(2)}) copy-start(f32[4,256]{1,0:T(4,128)S(1)} %fusion.141) | copy-start | bytes 12292
  282.2 261.5 %reduce-scatter.31.cloned.1.call-start = ((), (), s32[]{:S(2)}) async-start(), calls=%async_computation.23 | async-start | bytes 10485760 | tf_op jit(solution)/shard_map/reduce_scatter | solution.py:151
  312.9 103.1 %copy-start.37 = (bf16[512,128]{1,0:T(8,128)(2,1)}, bf16[512,128]{1,0:T(8,128)(2,1)S(1)}, u32[]{:S(2)}) copy-start(bf16[512,128]{1,0:T(8,128)(2,1)S(1)} %all_gather.66) | copy-start | bytes 393220
  471.7 75.6 %copy-start.51 = (f32[1,512]{1,0:T(1,128)S(1)}, f32[1,512]{1,0:T(1,128)}, u32[]{:S(2)}) copy-start(f32[1,512]{1,0:T(1,128)} %get-tuple-element.941) | copy-start | bytes 6148
  471.7 75.5 %copy-start.56 = (f32[1,512]{1,0:T(1,128)S(1)}, f32[1,512]{1,0:T(1,128)}, u32[]{:S(2)}) copy-start(f32[1,512]{1,0:T(1,128)} %get-tuple-element.944) | copy-start | bytes 6148
  471.7 162.4 %all-gather.17.cloned.1.call-start = ((), (), s32[]{:S(2)}) async-start(), calls=%async_computation.24 | async-start | bytes 5242880 | tf_op jit(solution)/shard_map/all_gather | solution.py:282
  548.7 168.5 %reduce-scatter.33.cloned.1.call-start = ((), (), s32[]{:S(2)}) async-start(), calls=%async_computation.25 | async-start | bytes 10485760 | tf_op jit(solution)/shard_map/reduce_scatter | solution.py:287
  649.0 110.6 %all-gather.19.cloned.1.call-start = ((), (), s32[]{:S(2)}) async-start(), calls=%async_computation.26 | async-start | bytes 5242880 | tf_op jit(solution)/shard_map/all_gather | solution.py:295
  725.0 123.8 %reduce-scatter.35.cloned.1.call-start = ((), (), s32[]{:S(2)}) async-start(), calls=%async_computation.27 | async-start | bytes 10485760 | tf_op jit(solution)/shard_map/reduce_scatter | solution.py:301
  776.9 114.9 %all-gather.21.cloned.1.call-start = ((), (), s32[]{:S(2)}) async-start(), calls=%async_computation.28 | async-start | bytes 5242880 | tf_op jit(solution)/shard_map/all_gather | solution.py:155
  857.1 195.7 %reduce-scatter.37.cloned.1.call-start = ((), (), s32[]{:S(2)}) async-start(), calls=%async_computation.29 | async-start | bytes 10485760 | tf_op jit(solution)/shard_map/reduce_scatter | solution.py:159
  897.5 76.9 %copy-start.38 = (bf16[512,128]{1,0:T(8,128)(2,1)S(1)}, bf16[512,128]{1,0:T(8,128)(2,1)}, u32[]{:S(2)}) copy-start(bf16[512,128]{1,0:T(8,128)(2,1)} %copy-done.37) | copy-start | bytes 393220
  974.4 103.6 %copy-start.13 = (bf16[4,1024,128]{1,2,0:T(8,128)(2,1)}, bf16[4,1024,128]{1,2,0:T(8,128)(2,1)S(1)}, u32[]{:S(2)}) copy-start(bf16[4,1024,128]{1,2,0:T(8,128)(2,1)S(1)} %get-tuple-element.583) | copy-start | bytes 3145732
  980.9 75.5 %copy-start.53 = (f32[4,256]{1,0:T(4,128)S(1)}, f32[4,256]{1,0:T(4,128)}, u32[]{:S(2)}) copy-start(f32[4,256]{1,0:T(4,128)} %copy-done.52) | copy-start | bytes 12292
  981.0 113.4 %all-gather.23.cloned.1.call-start = ((), (), s32[]{:S(2)}) async-start(), calls=%async_computation.30 | async-start | bytes 5242880 | tf_op jit(solution)/shard_map/all_gather | solution.py:155
  1059.7 192.2 %reduce-scatter.53.cloned.1.call-start = ((), (), s32[]{:S(2)}) async-start(), calls=%async_computation.38 | async-start | bytes 589824 | tf_op jit(solution)/shard_map/reduce_scatter | solution.py:392
  1066.5 187.0 %reduce-scatter.51.cloned.1.call-start = ((), (), s32[]{:S(2)}) async-start(), calls=%async_computation.37 | async-start | bytes 589824 | tf_op jit(solution)/shard_map/reduce_scatter | solution.py:386
  1074.2 213.6 %reduce-scatter.61.cloned.1.call-start = ((), (), s32[]{:S(2)}) async-start(), calls=%async_computation.42 | async-start | bytes 147456
  1077.9 273.3 %reduce-scatter.63.cloned.1.call-start = ((), (), s32[]{:S(2)}) async-start(), calls=%async_computation.43 | async-start | bytes 147456
  1081.8 332.9 %reduce-scatter.49.cloned.1.call-start = ((), (), s32[]{:S(2)}) async-start(), calls=%async_computation.36 | async-start | bytes 147456 | tf_op jit(solution)/shard_map/reduce_scatter | solution.py:383
  1086.5 391.8 %reduce-scatter.47.cloned.1.call-start = ((), (), s32[]{:S(2)}) async-start(), calls=%async_computation.35 | async-start | bytes 147456 | tf_op jit(solution)/shard_map/reduce_scatter | solution.py:374
  1090.8 451.0 %reduce-scatter.55.cloned.1.call-start = ((), (), s32[]{:S(2)}) async-start(), calls=%async_computation.39 | async-start | bytes 147456
  1195.9 409.5 %reduce-scatter.57.cloned.1.call-start = ((), (), s32[]{:S(2)}) async-start(), calls=%async_computation.40 | async-start | bytes 147456
  1199.8 469.2 %reduce-scatter.59.cloned.1.call-start = ((), (), s32[]{:S(2)}) async-start(), calls=%async_computation.41 | async-start | bytes 147456
  1203.6 529.0 %reduce-scatter.45.cloned.1.call-start = ((), (), s32[]{:S(2)}) async-start(), calls=%async_computation.34 | async-start | bytes 147456 | tf_op jit(solution)/shard_map/reduce_scatter | solution.py:371
  1208.6 597.4 %reduce-scatter.39.cloned.1.call-start = ((), (), s32[]{:S(2)}) async-start(), calls=%async_computation.31 | async-start | bytes 10485760 | tf_op jit(solution)/shard_map/reduce_scatter | solution.py:159
  1214.4 666.4 %reduce-scatter.43.cloned.1.call-start = ((), (), s32[]{:S(2)}) async-start(), calls=%async_computation.33 | async-start | bytes 10485760 | tf_op jit(solution)/shard_map/reduce_scatter | solution.py:159
  1222.4 733.3 %reduce-scatter.41.cloned.1.call-start = ((), (), s32[]{:S(2)}) async-start(), calls=%async_computation.32 | async-start | bytes 10485760 | tf_op jit(solution)/shard_map/reduce_scatter | solution.py:159
  1229.1 250.5 %copy-start.65 = (f32[512]{0:T(512)S(1)}, f32[512]{0:T(512)}, u32[]{:S(2)}) copy-start(f32[512]{0:T(512)} %get-tuple-element.772) | copy-start | bytes 6148
  1229.1 250.5 %copy-start.66 = (f32[512]{0:T(512)S(1)}, f32[512]{0:T(512)}, u32[]{:S(2)}) copy-start(f32[512]{0:T(512)} %get-tuple-element.766) | copy-start | bytes 6148
  1229.1 250.5 %copy-start.67 = (f32[512]{0:T(512)S(1)}, f32[512]{0:T(512)}, u32[]{:S(2)}) copy-start(f32[512]{0:T(512)} %get-tuple-element.762) | copy-start | bytes 6148
  1229.1 250.5 %copy-start.68 = (f32[512]{0:T(512)S(1)}, f32[512]{0:T(512)}, u32[]{:S(2)}) copy-start(f32[512]{0:T(512)} %get-tuple-element.770) | copy-start | bytes 6148
  1229.1 250.5 %copy-start.69 = (f32[512]{0:T(512)S(1)}, f32[512]{0:T(512)}, u32[]{:S(2)}) copy-start(f32[512]{0:T(512)} %get-tuple-element.764) | copy-start | bytes 6148
  1229.1 250.5 %copy-start.70 = (f32[512]{0:T(512)S(1)}, f32[512]{0:T(512)}, u32[]{:S(2)}) copy-start(f32[512]{0:T(512)} %get-tuple-element.771) | copy-start | bytes 6148
  1229.1 250.6 %copy-start.64 = (f32[512]{0:T(512)S(1)}, f32[512]{0:T(512)}, u32[]{:S(2)}) copy-start(f32[512]{0:T(512)} %get-tuple-element.856) | copy-start | bytes 6148
  1229.1 576.8 %copy-start.6 = (f32[4,256,512]{2,1,0:T(8,128)S(1)}, f32[4,256,512]{2,1,0:T(8,128)}, u32[]{:S(2)}) copy-start(f32[4,256,512]{2,1,0:T(8,128)} %copy-done.5) | copy-start | bytes 6291460
  1229.2 576.8 %copy-start.55 = (f32[4,256]{1,0:T(4,128)S(1)}, f32[4,256]{1,0:T(4,128)}, u32[]{:S(2)}) copy-start(f32[4,256]{1,0:T(4,128)} %copy-done.54) | copy-start | bytes 12292
  (56 other events, 1539.3 us)
Sparse Core Ops, SparseCore 0:
  9.6 37.1 all-gather.8
  48.4 34.4 all-gather.10
  205.7 72.6 reduce-scatter.28
  279.9 34.4 all-gather.12
  316.5 34.4 all-gather.14
  471.8 71.8 reduce-scatter.30
  548.8 34.4 all-gather.16
  649.1 68.0 reduce-scatter.32
  725.1 34.4 all-gather.18
  777.1 71.6 reduce-scatter.34
  857.3 34.4 all-gather.20
  981.1 71.7 reduce-scatter.36
  1059.9 34.4 all-gather.22
  1097.9 62.0 reduce-scatter.52
  1163.2 61.0 reduce-scatter.50
  1227.8 59.9 reduce-scatter.60
  1291.3 59.8 reduce-scatter.62
  1354.7 59.8 reduce-scatter.48
  1418.3 59.8 reduce-scatter.46
  1481.8 59.8 reduce-scatter.54
  1545.4 59.8 reduce-scatter.56
  1609.0 59.8 reduce-scatter.58
  1672.6 59.8 reduce-scatter.44
  1735.1 70.7 reduce-scatter.38
  1809.1 71.7 reduce-scatter.42
  1884.0 71.6 reduce-scatter.40
where the time goes:
time: 1970 us; the launch traced here: 1960 us
  waiting for transfers between devices  1060 us (54%)
  blocking collectives  395 us (20%)
  matrix products  263 us (13%)
  other arithmetic  110 us (6%)
  local copies, waits for them, and re-layouts  99.7 us (5%)
    reduce_scatter x4, waiting for transfers between devices, send_back(): return lax.psum_scatter(partial_sum, 'tp', scatter_dimension=1, tiled=True)  291 us
    unnamed x31, waiting for transfers between devices  243 us
    reduce_scatter x2, waiting for transfers between devices, spread_sum(): return lax.psum_scatter(partial_sum, 'tp', scatter_dimension=1, tiled=True)  133 us
    reduce_scatter x1, waiting for transfers between devices, local(): lax.psum_scatter(project_back(grad_pre, hidden_in), 'tp', scatter_dimensi...  71.8 us
    reduce_scatter x1, waiting for transfers between devices, local(): lax.psum_scatter(project(ffn_act, hidden_out), 'tp', scatter_dimension=1,...  68.1 us
    reduce_scatter x1, waiting for transfers between devices, local(): lax.psum_scatter(grad_other_query.astype(jnp.bfloat16), 'dp', scatter_dim...  62.3 us
    reduce_scatter x1, waiting for transfers between devices, local(): lax.psum_scatter(grad_self_out.astype(jnp.bfloat16), 'dp', scatter_dimens...  62 us
    reduce_scatter x1, waiting for transfers between devices, local(): lax.psum_scatter(grad_other_out.astype(jnp.bfloat16), 'dp', scatter_dimen...  61.9 us
  transfers between devices with their start and end apart: 26, of which 19 were waited for; matrix products, arithmetic and copies ran while one was open for 10% of the time, Pallas kernels for 0%

commit v1 on v0

--- a/solution.py
+++ b/solution.py
@@ -159,7 +159,7 @@
     return lax.psum_scatter(partial_sum, "tp", scatter_dimension=1, tiled=True)
 
 
-def local(
+def local_split(
     query_stream,
     token_embed,
     encoder_out,
@@ -420,6 +420,193 @@
     )
 
 
+def to_row(piece):
+    return lax.all_to_all(piece, "tp", split_axis=0, concat_axis=1, tiled=True)
+
+
+def from_row(row):
+    return lax.all_to_all(row, "tp", split_axis=1, concat_axis=0, tiled=True)
+
+
+def own_row(per_row):
+    return lax.dynamic_slice_in_dim(per_row, lax.axis_index("tp"), 1, axis=0)
+
+
+def whole_weight(piece, rows_axis, cols_axis):
+    gathered = lax.all_gather(piece, rows_axis, axis=0, tiled=True)
+    return lax.all_gather(gathered, cols_axis, axis=1, tiled=True)
+
+
+def own_weight(partial_sum, rows_axis, cols_axis):
+    low = partial_sum.astype(jnp.bfloat16)
+    low = lax.psum_scatter(low, cols_axis, scatter_dimension=1, tiled=True)
+    return lax.psum_scatter(low, rows_axis, scatter_dimension=0, tiled=True).astype(jnp.float32)
+
+
+def local_rows(
+    query_stream,
+    token_embed,
+    encoder_out,
+    out_grad,
+    attn_q,
+    attn_k,
+    attn_v,
+    attn_o,
+    cross_q,
+    cross_k,
+    cross_v,
+    cross_o,
+    ffn_in,
+    ffn_bias_in,
+    ffn_out,
+    ffn_bias_out,
+    norm_gain,
+    norm_bias,
+    doc_lengths,
+    src_lengths,
+    ctx_rank,
+    ctx_limit,
+):
+    low = jnp.bfloat16
+    query_row, embed_row, source_row = to_row(query_stream), to_row(token_embed), to_row(encoder_out)
+    grad_row = to_row(out_grad)
+    lengths, source_lengths = own_row(doc_lengths)[0], own_row(src_lengths)[0]
+    rank_row, limit_row = own_row(ctx_rank)[0], own_row(ctx_limit)[0]
+    self_query, self_key, self_value, other_query, other_key, other_value, hidden_in = [
+        whole_weight(w, "dp", "tp")
+        for w in (attn_q, attn_k, attn_v, cross_q, cross_k, cross_v, ffn_in)
+    ]
+    self_out, other_out, hidden_out = [
+        whole_weight(w, "tp", "dp") for w in (attn_o, cross_o, ffn_out)
+    ]
+    hidden_bias = lax.all_gather(ffn_bias_in, ("tp", "dp"), axis=0, tiled=True)
+
+    def own_mask(first_row, block_rows):
+        return self_visible(
+            lengths, rank_row, limit_row, query_row.shape[1], first_row, block_rows
+        )
+
+    def other_mask(first_row, block_rows):
+        return cross_visible(
+            lengths,
+            source_lengths,
+            query_row.shape[1],
+            source_row.shape[1],
+            first_row,
+            block_rows,
+        )
+
+    self_queries = project(query_row, self_query).astype(low)
+    self_keys = project(embed_row, self_key).astype(low)
+    self_values = project(embed_row, self_value).astype(low)
+    self_context, self_totals = attend_forward(
+        self_queries[0], self_keys[0], self_values[0], own_mask, HEADS
+    )
+    self_low = self_context.astype(low)[None]
+    first_sum = query_row.astype(jnp.float32) + project(self_low, self_out)
+    hidden_one, first_back = jax.vjp(layer_norm, first_sum, norm_gain[0], norm_bias[0])
+    hidden_one_low = hidden_one.astype(low)
+    cross_queries = project(hidden_one_low, other_query).astype(low)
+    cross_keys = project(source_row, other_key).astype(low)
+    cross_values = project(source_row, other_value).astype(low)
+    cross_context, cross_totals = attend_forward(
+        cross_queries[0], cross_keys[0], cross_values[0], other_mask, HEADS
+    )
+    cross_low = cross_context.astype(low)[None]
+    second_sum = hidden_one + project(cross_low, other_out)
+    hidden_two, second_back = jax.vjp(layer_norm, second_sum, norm_gain[1], norm_bias[1])
+    hidden_two_low = hidden_two.astype(low)
+    ffn_pre = project(hidden_two_low, hidden_in) + hidden_bias.astype(jnp.float32)
+    ffn_gate, gelu_back = jax.vjp(gelu_exact, ffn_pre)
+    ffn_act = ffn_gate.astype(low)
+    third_sum = hidden_two + project(ffn_act, hidden_out) + ffn_bias_out
+    mixed, third_back = jax.vjp(layer_norm, third_sum, norm_gain[2], norm_bias[2])
+    grad_third, gain_two, shift_two = third_back(grad_row.astype(jnp.float32))
+    grad_ffn = grad_third.astype(low)
+    grad_bias_out = jnp.sum(grad_ffn.astype(jnp.float32), axis=(0, 1))
+    grad_down = outer_sum(ffn_act, grad_ffn)
+    grad_pre = gelu_back(project_back(grad_ffn, hidden_out))[0].astype(low)
+    grad_up = outer_sum(hidden_two_low, grad_pre)
+    grad_bias_in = jnp.sum(grad_pre.astype(jnp.float32), axis=(0, 1))
+    grad_two = grad_third + project_back(grad_pre, hidden_in)
+    grad_second, gain_one, shift_one = second_back(grad_two)
+    grad_cross = grad_second.astype(low)
+    grad_other_out = outer_sum(cross_low, grad_cross)
+    grad_cross_ctx = project_back(grad_cross, other_out).astype(low)
+    cross_dq, cross_dk, cross_dv = [
+        g[None]
+        for g in attend_backward(
+            cross_queries[0],
+            cross_keys[0],
+            cross_values[0],
+            other_mask,
+            cross_totals,
+            grad_cross_ctx[0],
+            HEADS,
+        )
+    ]
+    grad_other_query = outer_sum(hidden_one_low, cross_dq)
+    grad_other_key = outer_sum(source_row, cross_dk)
+    grad_other_value = outer_sum(source_row, cross_dv)
+    grad_encoder = project_back(cross_dk, other_key) + project_back(cross_dv, other_value)
+    grad_one = grad_second + project_back(cross_dq, other_query)
+    grad_first, gain_zero, shift_zero = first_back(grad_one)
+    grad_attn = grad_first.astype(low)
+    grad_self_out = outer_sum(self_low, grad_attn)
+    grad_self_ctx = project_back(grad_attn, self_out).astype(low)
+    self_dq, self_dk, self_dv = [
+        g[None]
+        for g in attend_backward(
+            self_queries[0],
+            self_keys[0],
+            self_values[0],
+            own_mask,
+            self_totals,
+            grad_self_ctx[0],
+            HEADS,
+        )
+    ]
+    grad_self_query = outer_sum(query_row, self_dq)
+    grad_self_key = outer_sum(embed_row, self_dk)
+    grad_self_value = outer_sum(embed_row, self_dv)
+    grad_embed = project_back(self_dk, self_key) + project_back(self_dv, self_value)
+    grad_query = grad_first + project_back(self_dq, self_query)
+    gain_grads = jnp.stack([gain_zero, gain_one, gain_two])
+    shift_grads = jnp.stack([shift_zero, shift_one, shift_two])
+    gain_grads, shift_grads, grad_bias_out = lax.psum(
+        (gain_grads, shift_grads, grad_bias_out), ("dp", "tp")
+    )
+    return (
+        from_row(mixed.astype(low)),
+        from_row(grad_query.astype(low)).astype(jnp.float32),
+        from_row(grad_embed.astype(low)).astype(jnp.float32),
+        from_row(grad_encoder.astype(low)).astype(jnp.float32),
+        own_weight(grad_self_query, "dp", "tp"),
+        own_weight(grad_self_key, "dp", "tp"),
+        own_weight(grad_self_value, "dp", "tp"),
+        own_weight(grad_self_out, "tp", "dp"),
+        own_weight(grad_other_query, "dp", "tp"),
+        own_weight(grad_other_key, "dp", "tp"),
+        own_weight(grad_other_value, "dp", "tp"),
+        own_weight(grad_other_out, "tp", "dp"),
+        own_weight(grad_up, "dp", "tp"),
+        lax.psum_scatter(
+            grad_bias_in.astype(low), ("tp", "dp"), scatter_dimension=0, tiled=True
+        ).astype(jnp.float32),
+        own_weight(grad_down, "tp", "dp"),
+        grad_bias_out,
+        gain_grads,
+        shift_grads,
+    )
+
+
+def local(*arrays):
+    rows_here = arrays[0].shape[0]
+    if rows_here == lax.axis_size("tp"):
+        return local_rows(*arrays)
+    return local_split(*arrays)
+
+
 def solution(mesh):
     in_specs = (
         P("dp", "tp", None),

time: 1970 us -> 1550 us (0.79)
  waiting for transfers between devices: 1060 us -> 550 us
  blocking collectives: 395 us -> 493 us
  matrix products: 263 us -> 221 us
  starting transfers between devices: 11.7 us -> 34.6 us
    reduce_scatter x13 -> x12, waiting for transfers between devices: 750 us -> 302 us  [the longest x9 156 us: own_weight(): low = lax.psum_scatter(low, cols_axis, scatter_dimension=1, tiled=True)]
    all_gather x8 -> x2, waiting for transfers between devices: 72.4 us -> 0.02 us  [whole_weight(): return lax.all_gather(gathered, cols_axis, axis=1, tiled=True)]
    unnamed x174 -> x323, local copies, waits for them, and re-layouts: 21.6 us -> 86.4 us
    all_gather x10 -> x18, blocking collectives: 312 us -> 368 us  [the longest x10 256 us: whole_weight(): gathered = lax.all_gather(piece, rows_axis, axis=0, tiled=True)]
    unnamed x2, blocking collectives: 42.7 us -> 80.1 us
    all_to_all x0 -> x8, starting transfers between devices: none -> 32.2 us  [the longest x4 16.6 us: from_row(): return lax.all_to_all(row, 'tp', split_axis=1, concat_axis=0, tiled=True)]
    unnamed x0 -> x7, other arithmetic: none -> 31.1 us
    convert_element_type x16 -> x4, other arithmetic: 21 us -> 51.6 us  [attend_backward(): grad_scores = (weights_full * (grad_weights - inner)).astype(jnp.bfloat16)]
  transfers between devices with their start and end apart: 26 -> 30, of which waited for: 19 -> 16; matrix products, arithmetic and copies ran while one was open for 10% -> 21% of each run, Pallas kernels for 0% -> 0%
where the time goes in v1:
time: 1550 us; the launch traced here: 1540 us
  waiting for transfers between devices  550 us (35%)
  blocking collectives  493 us (32%)
  matrix products  221 us (14%)
  other arithmetic  122 us (8%)
  local copies, waits for them, and re-layouts  104 us (7%)
  starting transfers between devices  34.6 us (2%)
  between operations  18.2 us (1%)
    all_gather x10, blocking collectives, whole_weight(): gathered = lax.all_gather(piece, rows_axis, axis=0, tiled=True)  256 us
    unnamed x30, waiting for transfers between devices  229 us
    reduce_scatter x9, waiting for transfers between devices, own_weight(): low = lax.psum_scatter(low, cols_axis, scatter_dimension=1, tiled=True)  156 us
    reduce_scatter x3, waiting for transfers between devices, own_weight(): lax.psum_scatter(low, rows_axis, scatter_dimension=0, tiled=True)  146 us
    all_gather x8, blocking collectives, whole_weight(): return lax.all_gather(gathered, cols_axis, axis=1, tiled=True)  112 us
    unnamed x323, local copies, waits for them, and re-layouts  86.4 us
    unnamed x2, blocking collectives  80.1 us
    convert_element_type x4, other arithmetic, attend_backward(): grad_scores = (weights_full * (grad_weights - inner)).astype(jnp.bfloat16)  51.6 us
  transfers between devices with their start and end apart: 30, of which 16 were waited for; matrix products, arithmetic and copies ran while one was open for 21% of the time, Pallas kernels for 0%

profile of v1, /device:TPU:0, one launch (start us, length us, event | category | flops | bytes accessed | tf_op | source)
XLA Modules:
  0.0 1543.1 jit_solution(7197807304585175408)
XLA Ops:
  7.3 35.5 %all_gather.79 = bf16[512,512]{1,0:T(8,128)(2,1)} all-gather(bf16[64,512]{1,0:T(8,128)(2,1)} %param.34), channel_id=1, replica_groups=mesh['dp'=8,'tp'=4] {'dp'}, dimensions={0}, use_global_device_ids=true | all-gather | bytes 589824 | tf_op jit(solution)/shard_map/all_gather | solution.py:436
  46.7 25.9 %all_gather.82 = bf16[2048,64]{0,1:T(8,128)(2,1)} all-gather(bf16[512,64]{0,1:T(8,128)(2,1)S(1)} %copy-done.80), channel_id=1, replica_groups=mesh['dp'=8,'tp'=4] {'tp'}, dimensions={0}, use_global_device_ids=true | all-gather | bytes 327680 | tf_op jit(solution)/shard_map/all_gather | solution.py:436
  75.4 39.2 %all-reduce = bf16[2048]{0:T(1024)(128)(2,1)S(1)} all-reduce(bf16[2048]{0:T(1024)(128)(2,1)S(1)} %dynamic-update-slice), channel_id=1, replica_groups=mesh['dp'=8,'tp'=4] {'tp','dp'}, use_global_device_ids=true, to_apply=%add | all-reduce | flops 2048 | bytes 8192
  127.0 30.5 %all_gather.65 = bf16[512,128]{1,0:T(8,128)(2,1)S(1)} all-gather(bf16[64,128]{1,0:T(8,128)(2,1)S(1)} %copy-done.95), channel_id=1, replica_groups=mesh['dp'=8,'tp'=4] {'dp'}, dimensions={0}, use_global_device_ids=true | all-gather | bytes 147456 | tf_op jit(solution)/shard_map/all_gather | solution.py:436
  157.5 30.5 %all_gather.67 = bf16[512,128]{1,0:T(8,128)(2,1)S(1)} all-gather(bf16[64,128]{1,0:T(8,128)(2,1)S(1)} %copy-done.96), channel_id=1, replica_groups=mesh['dp'=8,'tp'=4] {'dp'}, dimensions={0}, use_global_device_ids=true | all-gather | bytes 147456 | tf_op jit(solution)/shard_map/all_gather | solution.py:436
  188.0 30.5 %all_gather.63 = bf16[512,128]{1,0:T(8,128)(2,1)S(1)} all-gather(bf16[64,128]{1,0:T(8,128)(2,1)S(1)} %copy-done.97), channel_id=1, replica_groups=mesh['dp'=8,'tp'=4] {'dp'}, dimensions={0}, use_global_device_ids=true | all-gather | bytes 147456 | tf_op jit(solution)/shard_map/all_gather | solution.py:436
  218.6 30.5 %all_gather.73 = bf16[512,128]{1,0:T(8,128)(2,1)S(1)} all-gather(bf16[64,128]{1,0:T(8,128)(2,1)S(1)} %copy-done.98), channel_id=1, replica_groups=mesh['dp'=8,'tp'=4] {'dp'}, dimensions={0}, use_global_device_ids=true | all-gather | bytes 147456 | tf_op jit(solution)/shard_map/all_gather | solution.py:436
  249.1 30.7 %all_gather.75 = bf16[512,128]{1,0:T(8,128)(2,1)S(1)} all-gather(bf16[64,128]{1,0:T(8,128)(2,1)S(1)} %copy-done.99), channel_id=1, replica_groups=mesh['dp'=8,'tp'=4] {'dp'}, dimensions={0}, use_global_device_ids=true | all-gather | bytes 147456 | tf_op jit(solution)/shard_map/all_gather | solution.py:436
  279.8 30.5 %all_gather.71 = bf16[512,128]{1,0:T(8,128)(2,1)S(1)} all-gather(bf16[64,128]{1,0:T(8,128)(2,1)S(1)} %copy-done.100), channel_id=1, replica_groups=mesh['dp'=8,'tp'=4] {'dp'}, dimensions={0}, use_global_device_ids=true | all-gather | bytes 147456 | tf_op jit(solution)/shard_map/all_gather | solution.py:436
  310.3 8.1 all_gather.72
  318.3 7.7 all_gather.76
  326.1 7.7 all_gather.74
  333.8 7.7 all_gather.64
  357.6 33.3 %all_gather.78 = bf16[512,512]{0,1:T(8,128)(2,1)} all-gather(bf16[512,64]{0,1:T(8,128)(2,1)S(1)} %all_gather.77), channel_id=1, replica_groups=mesh['dp'=8,'tp'=4] {'dp'}, dimensions={1}, use_global_device_ids=true | all-gather | bytes 589824 | tf_op jit(solution)/shard_map/all_gather | solution.py:437
  390.9 33.3 %all_gather.70 = bf16[512,512]{0,1:T(8,128)(2,1)} all-gather(bf16[512,64]{0,1:T(8,128)(2,1)S(1)} %all_gather.69), channel_id=1, replica_groups=mesh['dp'=8,'tp'=4] {'dp'}, dimensions={1}, use_global_device_ids=true | all-gather | bytes 589824 | tf_op jit(solution)/shard_map/all_gather | solution.py:437
  434.1 8.0 all-to-all-done.1
  450.6 11.3 all-to-all-done.2
  538.1 8.7 multiply_convert_fusion.4
  560.9 8.0 fusion.101
  578.5 10.0 multiply_reduce_fusion.3
  588.5 16.0 %multiply_convert_fusion.3 = bf16[8,512,1024]{2,1,0:T(8,128)(2,1)} fusion(f32[8,512,1024]{2,1,0:T(8,128)} %get-tuple-element.160, f32[8,512,1024]{2,1,0:T(8,128)} %copy-done.5, f32[8,512]{1,0:T(8,128)} %get-tuple-element.159, f32[8,512]{1,0:T(8,128)} %log_add_fusion.3), kind=kLoop, calls=%fused_computation.9 | loop fusion | flops 16777216 | bytes 41975808 | tf_op jit(solution)/shard_map/convert_element_type | solution.py:118
  604.5 7.5 fusion.44
  622.4 9.9 multiply_reduce_fusion.2
  635.9 8.5 add_convert_fusion.2
  648.2 12.0 multiply_convert_fusion.2
  686.1 7.7 add_convert_fusion.4
  696.4 11.5 multiply_reduce_fusion.1
  708.0 11.5 multiply_reduce_fusion
  719.6 15.9 %multiply_convert_fusion.1 = bf16[8,512,1024]{2,1,0:T(8,128)(2,1)} fusion(f32[8,512,1024]{2,1,0:T(8,128)} %get-tuple-element.165, f32[8,512,1024]{2,1,0:T(8,128)} %copy-done.3, f32[8,512]{1,0:T(8,128)S(1)} %get-tuple-element.164, f32[8,512]{1,0:T(8,128)S(1)} %copy-done.71), kind=kLoop, calls=%fused_computation.3 | loop fusion | flops 16777216 | bytes 41975808 | tf_op jit(solution)/shard_map/convert_element_type | solution.py:118
  738.3 7.7 multiply_convert_fusion
  746.1 8.0 fusion.102
  793.0 16.5 %reduce-scatter.47.cloned.1.call-done = bf16[512,128]{0,1:T(8,128)(2,1)} async-done(((bf16[512,512]{0,1:T(8,128)(2,1)}), bf16[512,128]{0,1:T(8,128)(2,1)}) %reduce-scatter.47.cloned.1.call-update) | async-done | bytes 131088 | tf_op jit(solution)/shard_map/reduce_scatter | solution.py:442
  811.6 22.1 %reduce-scatter.41.cloned.1.call-done = bf16[512,128]{0,1:T(8,128)(2,1)} async-done(((bf16[512,512]{0,1:T(8,128)(2,1)}), bf16[512,128]{0,1:T(8,128)(2,1)}) %reduce-scatter.41.cloned.1.call-update) | async-done | bytes 131088 | tf_op jit(solution)/shard_map/reduce_scatter | solution.py:442
  837.7 8.0 reduce.41
  861.7 20.9 %reduce-scatter.37.cloned.1.call-done = bf16[512,128]{0,1:T(8,128)(2,1)} async-done(((bf16[512,512]{0,1:T(8,128)(2,1)}), bf16[512,128]{0,1:T(8,128)(2,1)}) %reduce-scatter.37.cloned.1.call-update) | async-done | bytes 131088 | tf_op jit(solution)/shard_map/reduce_scatter | solution.py:442
  888.0 8.0 reduce.44
  910.5 68.2 %reduce-scatter.57.cloned.1.call-done = bf16[2048,64]{0,1:T(8,128)(2,1)} async-done(((bf16[2048,512]{0,1:T(8,128)(2,1)}), bf16[2048,64]{0,1:T(8,128)(2,1)}) %reduce-scatter.57.cloned.1.call-update) | async-done | bytes 262160 | tf_op jit(solution)/shard_map/reduce_scatter | solution.py:442
  997.8 24.2 %reduce-scatter.53.cloned.1.call-done = bf16[512,512]{1,0:T(8,128)(2,1)} async-done(((bf16[512,2048]{1,0:T(8,128)(2,1)}), bf16[512,512]{1,0:T(8,128)(2,1)}) %reduce-scatter.53.cloned.1.call-update) | async-done | bytes 524304 | tf_op jit(solution)/shard_map/reduce_scatter | solution.py:442
  1029.7 8.0 reduce.42
  1048.1 44.6 %all-reduce.2 = (f32[512]{0:T(512)}, f32[3,512]{1,0:T(4,128)}, f32[3,512]{1,0:T(4,128)}) all-reduce(f32[512]{0:T(512)S(1)} %copy-done.110, f32[3,512]{1,0:T(4,128)S(1)} %pad_maximum_fusion.4, f32[3,512]{1,0:T(4,128)S(1)} %pad_maximum_fusion.5), channel_id=1, replica_groups=mesh['dp'=8,'tp'=4] {'dp','tp'}, use_global_device_ids=true, to_apply=%region_52.53 | all-reduce | flops 3584 | bytes 28672 | tf_op jit(solution)/shard_map/psum | solution.py:576
  1092.7 40.9 %all-reduce.1 = bf16[2048]{0:T(1024)(128)(2,1)S(1)} all-reduce(bf16[2048]{0:T(1024)(128)(2,1)S(1)} %copy-done.115), channel_id=20, replica_groups=mesh['dp'=8,'tp'=4] {'tp','dp'}, use_global_device_ids=true, to_apply=%region_48.49.clone | all-reduce | flops 2048 | bytes 8192
  1153.5 38.6 %reduce-scatter.71.cloned.1.call-done = bf16[64,128]{1,0:T(8,128)(2,1)} async-done(((bf16[512,128]{1,0:T(8,128)(2,1)}), bf16[64,128]{1,0:T(8,128)(2,1)}) %reduce-scatter.71.cloned.1.call-update) | async-done | bytes 16400
  1193.7 61.9 %reduce-scatter.65.cloned.1.call-done = bf16[64,128]{1,0:T(8,128)(2,1)} async-done(((bf16[512,128]{1,0:T(8,128)(2,1)}), bf16[64,128]{1,0:T(8,128)(2,1)}) %reduce-scatter.65.cloned.1.call-update) | async-done | bytes 16400
  1257.1 62.5 %reduce-scatter.63.cloned.1.call-done = bf16[64,128]{1,0:T(8,128)(2,1)} async-done(((bf16[512,128]{1,0:T(8,128)(2,1)}), bf16[64,128]{1,0:T(8,128)(2,1)}) %reduce-scatter.63.cloned.1.call-update) | async-done | bytes 16400
  1321.1 62.6 %reduce-scatter.61.cloned.1.call-done = bf16[64,128]{1,0:T(8,128)(2,1)} async-done(((bf16[512,128]{1,0:T(8,128)(2,1)}), bf16[64,128]{1,0:T(8,128)(2,1)}) %reduce-scatter.61.cloned.1.call-update) | async-done | bytes 16400
  1385.3 61.9 %reduce-scatter.45.cloned.1.call-done = bf16[64,128]{1,0:T(8,128)(2,1)} async-done(((bf16[512,128]{1,0:T(8,128)(2,1)}), bf16[64,128]{1,0:T(8,128)(2,1)}) %reduce-scatter.45.cloned.1.call-update) | async-done | bytes 16400 | tf_op jit(solution)/shard_map/reduce_scatter | solution.py:443
  1448.5 20.4 %reduce-scatter.59.cloned.1.call-done = bf16[512,64]{0,1:T(8,128)(2,1)} async-done(((bf16[2048,64]{0,1:T(8,128)(2,1)}), bf16[512,64]{0,1:T(8,128)(2,1)}) %reduce-scatter.59.cloned.1.call-update) | async-done | bytes 65552 | tf_op jit(solution)/shard_map/reduce_scatter | solution.py:443
  1470.5 63.8 %reduce-scatter.55.cloned.1.call-done = bf16[64,512]{1,0:T(8,128)(2,1)} async-done(((bf16[512,512]{1,0:T(8,128)(2,1)}), bf16[64,512]{1,0:T(8,128)(2,1)}) %reduce-scatter.55.cloned.1.call-update) | async-done | bytes 65552 | tf_op jit(solution)/shard_map/reduce_scatter | solution.py:443
  (516 shorter events, 347.6 us)
Async XLA Ops:
  7.2 67.9 %copy-start.129 = (bf16[64]{0:T(256)(128)(2,1)S(1)}, bf16[64]{0:T(256)(128)(2,1)}, u32[]{:S(2)}) copy-start(bf16[64]{0:T(256)(128)(2,1)} %param.35) | copy-start | bytes 388
  7.2 107.9 %copy-start.113 = (f32[3,512]{1,0:T(4,128)S(1)}, f32[3,512]{1,0:T(4,128)}, u32[]{:S(2)}) copy-start(f32[3,512]{1,0:T(4,128)} %param.38) | copy-start | bytes 18436
  7.3 108.7 %copy-start.93 = (bf16[128,64]{0,1:T(8,128)(2,1)S(1)}, bf16[128,64]{0,1:T(8,128)(2,1)}, u32[]{:S(2)}) copy-start(bf16[128,64]{0,1:T(8,128)(2,1)} %param.29) | copy-start | bytes 49156
  7.3 114.2 %copy-start.94 = (bf16[128,64]{0,1:T(8,128)(2,1)S(1)}, bf16[128,64]{0,1:T(8,128)(2,1)}, u32[]{:S(2)}) copy-start(bf16[128,64]{0,1:T(8,128)(2,1)} %param.33) | copy-start | bytes 49156
  7.3 119.7 %copy-start.95 = (bf16[64,128]{1,0:T(8,128)(2,1)S(1)}, bf16[64,128]{1,0:T(8,128)(2,1)}, u32[]{:S(2)}) copy-start(bf16[64,128]{1,0:T(8,128)(2,1)} %param.26) | copy-start | bytes 49156
  7.3 150.2 %copy-start.96 = (bf16[64,128]{1,0:T(8,128)(2,1)S(1)}, bf16[64,128]{1,0:T(8,128)(2,1)}, u32[]{:S(2)}) copy-start(bf16[64,128]{1,0:T(8,128)(2,1)} %param.27) | copy-start | bytes 49156
  7.3 180.8 %copy-start.97 = (bf16[64,128]{1,0:T(8,128)(2,1)S(1)}, bf16[64,128]{1,0:T(8,128)(2,1)}, u32[]{:S(2)}) copy-start(bf16[64,128]{1,0:T(8,128)(2,1)} %param.28) | copy-start | bytes 49156
  7.3 530.8 %all-gather.3.cloned.1.call-start = ((), (), s32[]{:S(2)}) async-start(), calls=%async_computation.28 | async-start | bytes 2621440 | tf_op jit(solution)/shard_map/all_gather | solution.py:437
  42.9 175.7 %copy-start.98 = (bf16[64,128]{1,0:T(8,128)(2,1)S(1)}, bf16[64,128]{1,0:T(8,128)(2,1)}, u32[]{:S(2)}) copy-start(bf16[64,128]{1,0:T(8,128)(2,1)} %param.30) | copy-start | bytes 49156
  42.9 206.2 %copy-start.99 = (bf16[64,128]{1,0:T(8,128)(2,1)S(1)}, bf16[64,128]{1,0:T(8,128)(2,1)}, u32[]{:S(2)}) copy-start(bf16[64,128]{1,0:T(8,128)(2,1)} %param.31) | copy-start | bytes 49156
  42.9 236.9 %copy-start.100 = (bf16[64,128]{1,0:T(8,128)(2,1)S(1)}, bf16[64,128]{1,0:T(8,128)(2,1)}, u32[]{:S(2)}) copy-start(bf16[64,128]{1,0:T(8,128)(2,1)} %param.32) | copy-start | bytes 49156
  42.9 381.3 %all-to-all-start = ((bf16[4,256,512]{2,1,0:T(8,128)(2,1)}), bf16[4,256,512]{2,1,0:T(8,128)(2,1)S(1)}, u32[]{:S(2)}, u32[]{:S(2)}) async-start(bf16[4,256,512]{2,1,0:T(8,128)(2,1)} %param.22), calls=%async_computation | async-start | bytes 2097152 | tf_op jit(solution)/shard_map/all_to_all | solution.py:424
  46.6 500.2 %all-gather.5.cloned.1.call-start = ((), (), s32[]{:S(2)}) async-start(), calls=%async_computation.29 | async-start | bytes 2359296 | tf_op jit(solution)/shard_map/all_gather | solution.py:437
  115.2 233.7 %copy-start.103 = (s32[1024]{0:T(1024)}, s32[1024]{0:T(1024)S(1)}, u32[]{:S(2)}) copy-start(s32[1024]{0:T(1024)S(1)} %iota.45) | copy-start | bytes 12292
  115.8 384.3 %copy-start.88 = (f32[1,512]{1,0:T(1,128)}, f32[1,512]{1,0:T(1,128)S(1)}, u32[]{:S(2)}) copy-start(f32[1,512]{1,0:T(1,128)S(1)} %get-tuple-element.123) | copy-start | bytes 6148
  249.1 108.0 %copy-start.114 = (f32[3,512]{1,0:T(4,128)S(1)}, f32[3,512]{1,0:T(4,128)}, u32[]{:S(2)}) copy-start(f32[3,512]{1,0:T(4,128)} %param.39) | copy-start | bytes 18436
  348.9 98.7 %copy-start.42 = (bf16[512,512]{1,0:T(8,128)(2,1)}, bf16[512,512]{1,0:T(8,128)(2,1)S(1)}, u32[]{:S(2)}) copy-start(bf16[512,512]{1,0:T(8,128)(2,1)S(1)} %all_gather.68) | copy-start | bytes 1572868
  356.2 76.2 %copy-start.66 = (bf16[512,512]{1,0:T(8,128)(2,1)}, bf16[512,512]{1,0:T(8,128)(2,1)S(1)}, u32[]{:S(2)}) copy-start(bf16[512,512]{1,0:T(8,128)(2,1)S(1)} %all_gather.66) | copy-start | bytes 1572868
  356.2 71.6 %slice-start.12 = ((s32[1024]{0:T(1024)}), s32[512]{0:T(512)S(1)}, s32[]{:S(2)}) async-start(s32[1024]{0:T(1024)} %copy-done.103), calls=%async_computation.62 | async-start | bytes 4096 | tf_op jit(solution)/shard_map/slice | solution.py:48
  357.6 142.4 %copy-start.123 = (f32[1,512]{1,0:T(1,128)}, f32[1,512]{1,0:T(1,128)S(1)}, u32[]{:S(2)}) copy-start(f32[1,512]{1,0:T(1,128)S(1)} %get-tuple-element.126) | copy-start | bytes 6148
  424.2 18.0 %all-to-all-start.1 = ((bf16[4,256,512]{2,1,0:T(8,128)(2,1)}), bf16[4,256,512]{2,1,0:T(8,128)(2,1)S(1)}, u32[]{:S(2)}, u32[]{:S(2)}) async-start(bf16[4,256,512]{2,1,0:T(8,128)(2,1)} %param.23), calls=%async_computation.1 | async-start | bytes 2097152 | tf_op jit(solution)/shard_map/all_to_all | solution.py:424
  443.1 18.8 %all-to-all-start.2 = ((bf16[4,256,512]{2,1,0:T(8,128)(2,1)}), bf16[4,256,512]{2,1,0:T(8,128)(2,1)}, u32[]{:S(2)}, u32[]{:S(2)}) async-start(bf16[4,256,512]{2,1,0:T(8,128)(2,1)} %param.24), calls=%async_computation.2 | async-start | bytes 2097152 | tf_op jit(solution)/shard_map/all_to_all | solution.py:424
  461.9 67.8 %all-to-all-start.4 = ((bf16[4,256,512]{2,1,0:T(8,128)(2,1)}), bf16[4,256,512]{2,1,0:T(8,128)(2,1)}, u32[]{:S(2)}, u32[]{:S(2)}) async-start(bf16[4,256,512]{2,1,0:T(8,128)(2,1)} %param.25), calls=%async_computation.4 | async-start | bytes 2097152 | tf_op jit(solution)/shard_map/all_to_all | solution.py:424
  466.2 321.6 %reduce-scatter.51.cloned.1.call-start = ((), (), s32[]{:S(2)}) async-start(), calls=%async_computation.37 | async-start | bytes 589824 | tf_op jit(solution)/shard_map/reduce_scatter | solution.py:442
  635.9 153.7 %reduce-scatter.43.cloned.1.call-start = ((), (), s32[]{:S(2)}) async-start(), calls=%async_computation.33 | async-start | bytes 589824 | tf_op jit(solution)/shard_map/reduce_scatter | solution.py:442
  678.5 112.7 %reduce-scatter.49.cloned.1.call-start = ((), (), s32[]{:S(2)}) async-start(), calls=%async_computation.36 | async-start | bytes 655360 | tf_op jit(solution)/shard_map/reduce_scatter | solution.py:442
  696.3 113.1 %reduce-scatter.47.cloned.1.call-start = ((), (), s32[]{:S(2)}) async-start(), calls=%async_computation.35 | async-start | bytes 655360 | tf_op jit(solution)/shard_map/reduce_scatter | solution.py:442
  707.9 125.7 %reduce-scatter.41.cloned.1.call-start = ((), (), s32[]{:S(2)}) async-start(), calls=%async_computation.32 | async-start | bytes 655360 | tf_op jit(solution)/shard_map/reduce_scatter | solution.py:442
  719.5 138.5 %reduce-scatter.39.cloned.1.call-start = ((), (), s32[]{:S(2)}) async-start(), calls=%async_computation.31 | async-start | bytes 655360 | tf_op jit(solution)/shard_map/reduce_scatter | solution.py:442
  758.2 124.4 %reduce-scatter.37.cloned.1.call-start = ((), (), s32[]{:S(2)}) async-start(), calls=%async_computation.30 | async-start | bytes 655360 | tf_op jit(solution)/shard_map/reduce_scatter | solution.py:442
  770.1 136.7 %reduce-scatter.69.cloned.1.call-start = ((), (), s32[]{:S(2)}) async-start(), calls=%async_computation.46 | async-start | bytes 655360
  773.9 204.9 %reduce-scatter.57.cloned.1.call-start = ((), (), s32[]{:S(2)}) async-start(), calls=%async_computation.40 | async-start | bytes 2359296 | tf_op jit(solution)/shard_map/reduce_scatter | solution.py:442
  780.1 241.8 %reduce-scatter.53.cloned.1.call-start = ((), (), s32[]{:S(2)}) async-start(), calls=%async_computation.38 | async-start | bytes 2621440 | tf_op jit(solution)/shard_map/reduce_scatter | solution.py:442
  787.7 361.3 %reduce-scatter.75.cloned.1.call-start = ((), (), s32[]{:S(2)}) async-start(), calls=%async_computation.49 | async-start | bytes 163840
  789.5 361.0 %reduce-scatter.67.cloned.1.call-start = ((), (), s32[]{:S(2)}) async-start(), calls=%async_computation.45 | async-start | bytes 163840
  791.2 360.8 %reduce-scatter.73.cloned.1.call-start = ((), (), s32[]{:S(2)}) async-start(), calls=%async_computation.48 | async-start | bytes 147456
  792.9 399.2 %reduce-scatter.71.cloned.1.call-start = ((), (), s32[]{:S(2)}) async-start(), calls=%async_computation.47 | async-start | bytes 147456
  811.1 444.5 %reduce-scatter.65.cloned.1.call-start = ((), (), s32[]{:S(2)}) async-start(), calls=%async_computation.44 | async-start | bytes 147456
  849.5 50.4 %all-to-all-start.3 = ((bf16[4,2,65536]{2,1,0:T(2,128)(2,1)}), bf16[4,2,65536]{2,1,0:T(2,128)(2,1)}, u32[]{:S(2)}, u32[]{:S(2)}) async-start(bf16[4,2,65536]{2,1,0:T(2,128)(2,1)} %reshape.867), calls=%async_computation.3 | async-start | bytes 2097152 | tf_op jit(solution)/shard_map/all_to_all | solution.py:428
  853.8 465.8 %reduce-scatter.63.cloned.1.call-start = ((), (), s32[]{:S(2)}) async-start(), calls=%async_computation.43 | async-start | bytes 147456
  859.7 524.1 %reduce-scatter.61.cloned.1.call-start = ((), (), s32[]{:S(2)}) async-start(), calls=%async_computation.42 | async-start | bytes 147456
  899.9 91.7 %all-to-all-start.7 = ((bf16[4,2,65536]{2,1,0:T(2,128)(2,1)}), bf16[4,2,65536]{2,1,0:T(2,128)(2,1)}, u32[]{:S(2)}, u32[]{:S(2)}) async-start(bf16[4,2,65536]{2,1,0:T(2,128)(2,1)} %reshape.865), calls=%async_computation.7 | async-start | bytes 2097152 | tf_op jit(solution)/shard_map/all_to_all | solution.py:428
  904.1 543.1 %reduce-scatter.45.cloned.1.call-start = ((), (), s32[]{:S(2)}) async-start(), calls=%async_computation.34 | async-start | bytes 147456 | tf_op jit(solution)/shard_map/reduce_scatter | solution.py:443
  908.5 560.5 %reduce-scatter.59.cloned.1.call-start = ((), (), s32[]{:S(2)}) async-start(), calls=%async_computation.41 | async-start | bytes 327680 | tf_op jit(solution)/shard_map/reduce_scatter | solution.py:443
  991.5 50.0 %all-to-all-start.6 = ((bf16[4,2,65536]{2,1,0:T(2,128)(2,1)}), bf16[4,2,65536]{2,1,0:T(2,128)(2,1)S(1)}, u32[]{:S(2)}, u32[]{:S(2)}) async-start(bf16[4,2,65536]{2,1,0:T(2,128)(2,1)} %reshape.863), calls=%async_computation.6 | async-start | bytes 2097152 | tf_op jit(solution)/shard_map/all_to_all | solution.py:428
  995.2 539.1 %reduce-scatter.55.cloned.1.call-start = ((), (), s32[]{:S(2)}) async-start(), calls=%async_computation.39 | async-start | bytes 589824 | tf_op jit(solution)/shard_map/reduce_scatter | solution.py:443
  1041.5 103.3 %all-to-all-start.5 = ((bf16[4,2,65536]{2,1,0:T(2,128)(2,1)}), bf16[4,2,65536]{2,1,0:T(2,128)(2,1)}, u32[]{:S(2)}, u32[]{:S(2)}) async-start(bf16[4,2,65536]{2,1,0:T(2,128)(2,1)} %reshape.861), calls=%async_computation.5 | async-start | bytes 2097152 | tf_op jit(solution)/shard_map/all_to_all | solution.py:428
  1147.5 388.3 %copy-start.1 = (s32[4,1024]{1,0:T(4,128)S(1)}, s32[4,1024]{1,0:T(4,128)}, u32[]{:S(2)}) copy-start(s32[4,1024]{1,0:T(4,128)} %param.42) | copy-start | bytes 49156
  (126 other events, 1279.6 us)
Sparse Core Ops, SparseCore 0:
  43.1 32.1 all-gather.2
  77.3 50.4 all-gather.4
  636.0 61.6 reduce-scatter.50
  701.2 60.8 reduce-scatter.42
  764.5 20.7 reduce-scatter.48
  787.7 21.6 reduce-scatter.46
  811.9 21.6 reduce-scatter.40
  836.3 21.6 reduce-scatter.38
  860.5 22.0 reduce-scatter.36
  885.1 21.6 reduce-scatter.68
  910.9 67.7 reduce-scatter.56
  981.7 40.2 reduce-scatter.52
  1024.5 17.6 reduce-scatter.74
  1044.5 19.5 reduce-scatter.66
  1067.7 60.8 reduce-scatter.72
  1132.1 59.9 reduce-scatter.70
  1195.7 59.8 reduce-scatter.64
  1259.7 59.8 reduce-scatter.62
  1323.8 59.8 reduce-scatter.60
  1387.3 59.8 reduce-scatter.44
  1449.8 19.1 reduce-scatter.58
  1472.3 61.9 reduce-scatter.54

commit v2 on v1

--- a/solution.py
+++ b/solution.py
@@ -1,6 +1,8 @@
 import jax
 import jax.numpy as jnp
 from jax import lax
+from jax.experimental import pallas as pl
+from jax.experimental.pallas import tpu as pltpu
 from jax.sharding import PartitionSpec as P
 
 HEADS = 8
@@ -420,27 +422,395 @@
     )
 
 
-def to_row(piece):
-    return lax.all_to_all(piece, "tp", split_axis=0, concat_axis=1, tiled=True)
-
-
-def from_row(row):
-    return lax.all_to_all(row, "tp", split_axis=1, concat_axis=0, tiled=True)
+MESH = pl.DeviceIdType.MESH
+LOW = jnp.bfloat16
+WIDE = jnp.float32
+
+
+class Place:
+    def __init__(self):
+        dp, tp = lax.axis_index("dp"), lax.axis_index("tp")
+        self.dp, self.tp = dp, tp
+        self.z, self.x = dp // 2, lax.rem(dp, 2)
+        self.y, self.core = tp // 2, lax.rem(tp, 2)
+        self.core_peer = (dp, 2 * self.y + 1 - self.core)
+        self.y_peer = (dp, 2 * (1 - self.y) + self.core)
+        self.far_peer = (dp, 2 * (1 - self.y) + 1 - self.core)
+        self.x_peer = (2 * self.z + 1 - self.x, tp)
+
+    def z_at(self, step):
+        return lax.rem(self.z + step, 4)
+
+    def z_peer(self, step):
+        return (2 * self.z_at(step) + self.x, self.tp)
+
+    def meet(self):
+        peers = [self.core_peer, self.y_peer, self.far_peer, self.x_peer]
+        peers += [self.z_peer(step) for step in (1, 2, 3)]
+        barrier = pltpu.get_barrier_semaphore()
+        for peer in peers:
+            pl.semaphore_signal(barrier, inc=1, device_id=peer, device_id_type=MESH)
+        pl.semaphore_wait(barrier, len(peers))
+
+
+def send(source, target, send_sem, recv_sem, peer):
+    copy = pltpu.make_async_remote_copy(
+        src_ref=source,
+        dst_ref=target,
+        send_sem=send_sem,
+        recv_sem=recv_sem,
+        device_id=peer,
+        device_id_type=MESH,
+    )
+    copy.start()
+    return copy
+
+
+def cols(index, width):
+    return pl.ds(pl.multiple_of(index * width, width), width)
+
+
+class Gather:
+    def __init__(self, place, local, full, first, count, sends, recvs, own_sem):
+        self.place, self.local, self.full = place, local, full
+        self.items = pl.ds(first, count)
+        self.width = local.shape[-1]
+        self.sends, self.recvs, self.own_sem = sends, recvs, own_sem
+        self.pending = []
+        self.sent = []
+
+    def _send(self, source, target, slot, peer):
+        copy = send(source, target, self.sends.at[slot], self.recvs.at[slot], peer)
+        self.pending.append(copy)
+        self.sent.append(copy)
+
+    def _arrive(self):
+        for copy in self.pending:
+            copy.wait_recv()
+        self.pending = []
+
+    def stage(self, number):
+        p = self.place
+        mine, other = cols(p.tp, self.width), cols(2 * (1 - p.y) + p.core, self.width)
+        if number == 0:
+            source = self.local.at[self.items]
+            target = self.full.at[self.items, p.z, p.x, :, mine]
+            self.own = pltpu.make_async_copy(source, target, self.own_sem)
+            self.own.start()
+            for step in (1, 2, 3):
+                self._send(source, target, step - 1, p.z_peer(step))
+            return
+        self._arrive()
+        if number == 1:
+            self.own.wait()
+            block = self.full.at[self.items, :, p.x, :, mine]
+            self._send(block, block, 3, p.y_peer)
+        elif number == 2:
+            for slot, side in ((4, mine), (5, other)):
+                block = self.full.at[self.items, :, p.x, :, side]
+                self._send(block, block, slot, p.x_peer)
+        elif number == 3:
+            for slot, side in ((6, mine), (7, other)):
+                block = self.full.at[self.items, :, :, :, side]
+                self._send(block, block, slot, p.core_peer)
+        else:
+            for copy in self.sent:
+                copy.wait_send()
+
+
+GATHER_SLOTS = 8
+
+
+class ToRow:
+    def __init__(self, place, local, row, sends, recvs, own_sem):
+        size = local.shape[1]
+        p = place
+        here = pl.ds(pl.multiple_of(p.tp * size, size), size)
+        self.own = pltpu.make_async_copy(local.at[p.tp], row.at[here], own_sem)
+        self.own.start()
+        self.copies = [
+            send(local.at[peer[1]], row.at[here], sends.at[slot], recvs.at[slot], peer)
+            for slot, peer in enumerate((p.y_peer, p.far_peer, p.core_peer))
+        ]
+
+    def arrive(self):
+        self.own.wait()
+        for copy in self.copies:
+            copy.wait_recv()
+
+    def finish(self):
+        for copy in self.copies:
+            copy.wait_send()
+
+
+class FromRow:
+    def __init__(self, place, row, blocks, sends, recvs, own_sem):
+        size = blocks.shape[1]
+        p = place
+
+        def part(tp):
+            return row.at[pl.ds(pl.multiple_of(tp * size, size), size)]
+
+        self.own = pltpu.make_async_copy(part(p.tp), blocks.at[p.tp], own_sem)
+        self.own.start()
+        self.copies = [
+            send(part(peer[1]), blocks.at[p.tp], sends.at[slot], recvs.at[slot], peer)
+            for slot, peer in enumerate((p.y_peer, p.far_peer, p.core_peer))
+        ]
+
+    def finish(self):
+        self.own.wait()
+        for copy in self.copies:
+            copy.wait()
+
+
+def gather_kernel(
+    query, embed, source, cotangent, squares, wides, biases,
+    query_row, embed_row, source_row, cotangent_row, all_squares, all_wides, all_biases,
+    row_sends, row_recvs, row_own, sends, recvs, own,
+):
+    place = Place()
+    place.meet()
+    groups = [
+        (squares, all_squares, 0, 2),
+        (squares, all_squares, 2, 2),
+        (squares, all_squares, 4, 4),
+        (wides, all_wides, 0, 1),
+        (biases, all_biases, 0, 1),
+        (wides, all_wides, 1, 1),
+    ]
+    gathers = [
+        Gather(place, *group, sends.at[i], recvs.at[i], own.at[i])
+        for i, group in enumerate(groups)
+    ]
+    streams = [
+        (embed, embed_row),
+        (query, query_row),
+        (source, source_row),
+        (cotangent, cotangent_row),
+    ]
+    rows = []
+    for tick in range(len(gathers) + 4):
+        if tick < len(streams):
+            rows.append(
+                ToRow(place, *streams[tick], row_sends.at[tick], row_recvs.at[tick], row_own.at[tick])
+            )
+        for stage in range(5):
+            if 0 <= tick - stage < len(gathers):
+                gathers[tick - stage].stage(stage)
+    for row in rows:
+        row.arrive()
+        row.finish()
+
+
+def gather_all(query, embed, source, cotangent, squares, wides, biases):
+    hbm = pl.BlockSpec(memory_space=pl.ANY)
+    shape = jax.ShapeDtypeStruct
+    row = shape((4 * query.shape[1], query.shape[2]), LOW)
+    dma = pltpu.SemaphoreType.DMA
+    full = [shape((n, 4, 2, h, 4 * w), LOW) for n, h, w in (a.shape for a in (squares, wides, biases))]
+    outs = pl.pallas_call(
+        gather_kernel,
+        out_shape=[row] * 4 + full,
+        in_specs=[hbm] * 7,
+        out_specs=[hbm] * 7,
+        scratch_shapes=[
+            dma((4, 3)), dma((4, 3)), dma((4,)),
+            dma((6, GATHER_SLOTS)), dma((6, GATHER_SLOTS)), dma((6,)),
+        ],
+        compiler_params=pltpu.CompilerParams(collective_id=0, has_side_effects=True),
+        name="gather_all",
+    )(query, embed, source, cotangent, squares, wides, biases)
+    rows, full = outs[:4], outs[4:]
+    return rows, [w.reshape(w.shape[0], -1, w.shape[-1]) for w in full]
+
+
+class Scatter:
+    def __init__(self, place, parts, half, quarter, eighth, last, out, first, count, sends, recvs):
+        self.place, self.parts = place, parts
+        self.half, self.quarter, self.eighth, self.last = half, quarter, eighth, last
+        self.out = out
+        self.first, self.count = first, count
+        self.items = pl.ds(first, count)
+        self.width = out.shape[-1]
+        self.sends, self.recvs = sends, recvs
+        self.pending = []
+        self.sent = []
+
+    def _send(self, source, target, slot, peer):
+        copy = send(source, target, self.sends.at[slot], self.recvs.at[slot], peer)
+        self.pending.append(copy)
+        self.sent.append(copy)
+
+    def _arrive(self):
+        for copy in self.pending:
+            copy.wait_recv()
+        self.pending = []
+
+    def stage(self, number):
+        p = self.place
+        width = self.width
+        mine = cols(p.tp, width)
+        other = cols(2 * (1 - p.y) + p.core, width)
+        if number == 0:
+            for side, column in ((0, p.core_peer[1]), (1, p.far_peer[1])):
+                source = self.parts.at[self.items, :, :, :, cols(column, width)]
+                self._send(source, self.half.at[self.items, side], side, p.core_peer)
+            return
+        self._arrive()
+        if number == 1:
+            for item in range(self.first, self.first + self.count):
+                for side, column in ((0, mine), (1, other)):
+
+                    @pl.loop(0, 4)
+                    def _(z):
+                        total = self.parts[item, z, :, :, column].astype(WIDE)
+                        total = total + self.half[item, side, z].astype(WIDE)
+                        self.half[item, side, z] = total.astype(LOW)
+
+            for side in (0, 1):
+                source = self.half.at[self.items, side, :, 1 - p.x]
+                self._send(source, self.quarter.at[self.items, side], 2 + side, p.x_peer)
+        elif number == 2:
+            for item in range(self.first, self.first + self.count):
+                for side in (0, 1):
+
+                    @pl.loop(0, 4)
+                    def _(z):
+                        total = self.half[item, side, z, p.x].astype(WIDE)
+                        total = total + self.quarter[item, side, z].astype(WIDE)
+                        self.quarter[item, side, z] = total.astype(LOW)
+
+            self._send(self.quarter.at[self.items, 1], self.eighth.at[self.items], 4, p.y_peer)
+        elif number == 3:
+            for item in range(self.first, self.first + self.count):
+
+                @pl.loop(0, 4)
+                def _(z):
+                    total = self.quarter[item, 0, z].astype(WIDE)
+                    total = total + self.eighth[item, z].astype(WIDE)
+                    self.eighth[item, z] = total.astype(LOW)
+
+            for step in (1, 2, 3):
+                source = self.eighth.at[self.items, p.z_at(step)]
+                target = self.last.at[self.items, step - 1]
+                self._send(source, target, 4 + step, p.z_peer(step))
+        else:
+            for item in range(self.first, self.first + self.count):
+                total = self.eighth[item, p.z].astype(WIDE)
+                for step in range(3):
+                    total = total + self.last[item, step].astype(WIDE)
+                self.out[item] = total
+            for copy in self.sent:
+                copy.wait_send()
+
+
+SCATTER_SLOTS = 8
+
+
+class SumAll:
+    def __init__(self, place, values, arrived, sends, recvs):
+        self.place, self.values, self.arrived = place, values, arrived
+        self.sends, self.recvs = sends, recvs
+        self.copy = None
+
+    def stage(self, number):
+        p = self.place
+        if self.copy is not None:
+            self.copy.wait()
+            self.values[...] = self.values[...] + self.arrived[number - 1]
+        if number < 5:
+            z_one = (2 * (p.z + 1 - 2 * lax.rem(p.z, 2)) + p.x, p.tp)
+            z_two = (2 * lax.rem(p.z + 2, 4) + p.x, p.tp)
+            peer = (p.core_peer, p.x_peer, p.y_peer, z_one, z_two)[number]
+            self.copy = send(
+                self.values, self.arrived.at[number], self.sends.at[number], self.recvs.at[number], peer
+            )
+
+
+def scatter_kernel(
+    squares, wides, small, mixed, grad_query, grad_embed, grad_encoder,
+    own_squares, own_wides, small_sum, mixed_blocks, query_blocks, embed_blocks, encoder_blocks,
+    half_s, quarter_s, eighth_s, last_s, half_w, quarter_w, eighth_w, last_w, arrived,
+    row_sends, row_recvs, row_own, sends, recvs, small_sends, small_recvs,
+):
+    place = Place()
+    place.meet()
+    rows = [
+        FromRow(place, row, blocks, row_sends.at[i], row_recvs.at[i], row_own.at[i])
+        for i, (row, blocks) in enumerate(
+            (
+                (mixed, mixed_blocks),
+                (grad_encoder, encoder_blocks),
+                (grad_embed, embed_blocks),
+                (grad_query, query_blocks),
+            )
+        )
+    ]
+    small_sum[...] = small[...]
+    sum_all = SumAll(place, small_sum, arrived, small_sends, small_recvs)
+    square = (squares, half_s, quarter_s, eighth_s, last_s, own_squares)
+    wide = (wides, half_w, quarter_w, eighth_w, last_w, own_wides)
+    groups = [(wide, 0, 1), (wide, 1, 1), (square, 4, 4), (square, 2, 2), (square, 0, 2)]
+    scatters = [
+        Scatter(place, *buffers, first, count, sends.at[i], recvs.at[i])
+        for i, (buffers, first, count) in enumerate(groups)
+    ]
+    for tick in range(len(scatters) + 4):
+        for stage in range(5):
+            if 0 <= tick - stage < len(scatters):
+                scatters[tick - stage].stage(stage)
+        if tick < 6:
+            sum_all.stage(tick)
+    for row in rows:
+        row.finish()
+
+
+def scatter_all(squares, wides, small, rows):
+    hbm = pl.BlockSpec(memory_space=pl.ANY)
+    vmem = pl.BlockSpec(memory_space=pltpu.VMEM)
+    shape = jax.ShapeDtypeStruct
+    squares = squares.reshape(squares.shape[0], 4, 2, -1, squares.shape[-1])
+    wides = wides.reshape(wides.shape[0], 4, 2, -1, wides.shape[-1])
+    dma = pltpu.SemaphoreType.DMA
+    length, features = rows[0].shape
+    blocks = shape((4, length // 4, features), LOW)
+
+    def steps(a):
+        n, _, _, h, w = a.shape
+        w = w // 4
+        return [
+            pltpu.VMEM((n, 2, 4, 2, h, w), LOW),
+            pltpu.VMEM((n, 2, 4, h, w), LOW),
+            pltpu.VMEM((n, 4, h, w), LOW),
+            pltpu.VMEM((n, 3, h, w), LOW),
+        ]
+
+    def own(a):
+        n, _, _, h, w = a.shape
+        return shape((n, h, w // 4), WIDE)
+
+    return pl.pallas_call(
+        scatter_kernel,
+        out_shape=[own(squares), own(wides), shape(small.shape, WIDE)] + [blocks] * 4,
+        in_specs=[vmem] * 3 + [hbm] * 4,
+        out_specs=[vmem] * 3 + [hbm] * 4,
+        scratch_shapes=steps(squares)
+        + steps(wides)
+        + [
+            pltpu.VMEM((5,) + small.shape, WIDE),
+            dma((4, 3)), dma((4, 3)), dma((4,)),
+            dma((5, SCATTER_SLOTS)), dma((5, SCATTER_SLOTS)), dma((5,)), dma((5,)),
+        ],
+        compiler_params=pltpu.CompilerParams(
+            collective_id=1, has_side_effects=True, vmem_limit_bytes=56 * 2**20
+        ),
+        name="scatter_all",
+    )(squares, wides, small, *rows)
 
 
 def own_row(per_row):
     return lax.dynamic_slice_in_dim(per_row, lax.axis_index("tp"), 1, axis=0)
-
-
-def whole_weight(piece, rows_axis, cols_axis):
-    gathered = lax.all_gather(piece, rows_axis, axis=0, tiled=True)
-    return lax.all_gather(gathered, cols_axis, axis=1, tiled=True)
-
-
-def own_weight(partial_sum, rows_axis, cols_axis):
-    low = partial_sum.astype(jnp.bfloat16)
-    low = lax.psum_scatter(low, cols_axis, scatter_dimension=1, tiled=True)
-    return lax.psum_scatter(low, rows_axis, scatter_dimension=0, tiled=True).astype(jnp.float32)
 
 
 def local_rows(
@@ -468,18 +838,23 @@
     ctx_limit,
 ):
     low = jnp.bfloat16
-    query_row, embed_row, source_row = to_row(query_stream), to_row(token_embed), to_row(encoder_out)
-    grad_row = to_row(out_grad)
+    squares = jnp.stack(
+        [attn_q, attn_k, attn_v, attn_o.T, cross_q, cross_k, cross_v, cross_o.T]
+    )
+    wides = jnp.stack([ffn_in, ffn_out.T])
+    biases = jnp.pad(ffn_bias_in[None, None], ((0, 0), (0, 15), (0, 64)))
+    rows, (squares, wides, biases) = gather_all(
+        query_stream, token_embed, encoder_out, out_grad, squares, wides, biases
+    )
+    query_row, embed_row, source_row, grad_row = [row[None] for row in rows]
     lengths, source_lengths = own_row(doc_lengths)[0], own_row(src_lengths)[0]
     rank_row, limit_row = own_row(ctx_rank)[0], own_row(ctx_limit)[0]
-    self_query, self_key, self_value, other_query, other_key, other_value, hidden_in = [
-        whole_weight(w, "dp", "tp")
-        for w in (attn_q, attn_k, attn_v, cross_q, cross_k, cross_v, ffn_in)
-    ]
-    self_out, other_out, hidden_out = [
-        whole_weight(w, "tp", "dp") for w in (attn_o, cross_o, ffn_out)
-    ]
-    hidden_bias = lax.all_gather(ffn_bias_in, ("tp", "dp"), axis=0, tiled=True)
+    self_query, self_key, self_value, other_query, other_key, other_value = (
+        squares[i] for i in (0, 1, 2, 4, 5, 6)
+    )
+    self_out, other_out = squares[3].T, squares[7].T
+    hidden_in, hidden_out = wides[0], wides[1].T
+    hidden_bias = biases.reshape(8, 16, 4, 128)[:, 0, :, :64].transpose(1, 0, 2).reshape(-1)
 
     def own_mask(first_row, block_rows):
         return self_visible(
@@ -571,38 +946,47 @@
     grad_self_value = outer_sum(embed_row, self_dv)
     grad_embed = project_back(self_dk, self_key) + project_back(self_dv, self_value)
     grad_query = grad_first + project_back(self_dq, self_query)
-    gain_grads = jnp.stack([gain_zero, gain_one, gain_two])
-    shift_grads = jnp.stack([shift_zero, shift_one, shift_two])
-    gain_grads, shift_grads, grad_bias_out = lax.psum(
-        (gain_grads, shift_grads, grad_bias_out), ("dp", "tp")
-    )
+    small = jnp.concatenate(
+        [grad_bias_in, gain_zero, gain_one, gain_two, shift_zero, shift_one, shift_two]
+        + [grad_bias_out, jnp.zeros((8 * 2048 - 2048 - 7 * 512,), jnp.float32)]
+    ).reshape(8, 2048)
+    squares = jnp.stack(
+        [grad_self_query, grad_self_key, grad_self_value, grad_self_out.T]
+        + [grad_other_query, grad_other_key, grad_other_value, grad_other_out.T]
+    ).astype(low)
+    wides = jnp.stack([grad_up, grad_down.T]).astype(low)
+    rows = [g[0].astype(low) for g in (mixed, grad_query, grad_embed, grad_encoder)]
+    squares, wides, small, mixed, grad_query, grad_embed, grad_encoder = scatter_all(
+        squares, wides, small, rows
+    )
+    small = small.reshape(-1)
+    device = lax.axis_index("tp") * lax.axis_size("dp") + lax.axis_index("dp")
+    grad_bias_in = lax.dynamic_slice_in_dim(small, device * 64, 64)
+    vectors = small[2048 : 2048 + 7 * 512].reshape(7, 512)
     return (
-        from_row(mixed.astype(low)),
-        from_row(grad_query.astype(low)).astype(jnp.float32),
-        from_row(grad_embed.astype(low)).astype(jnp.float32),
-        from_row(grad_encoder.astype(low)).astype(jnp.float32),
-        own_weight(grad_self_query, "dp", "tp"),
-        own_weight(grad_self_key, "dp", "tp"),
-        own_weight(grad_self_value, "dp", "tp"),
-        own_weight(grad_self_out, "tp", "dp"),
-        own_weight(grad_other_query, "dp", "tp"),
-        own_weight(grad_other_key, "dp", "tp"),
-        own_weight(grad_other_value, "dp", "tp"),
-        own_weight(grad_other_out, "tp", "dp"),
-        own_weight(grad_up, "dp", "tp"),
-        lax.psum_scatter(
-            grad_bias_in.astype(low), ("tp", "dp"), scatter_dimension=0, tiled=True
-        ).astype(jnp.float32),
-        own_weight(grad_down, "tp", "dp"),
-        grad_bias_out,
-        gain_grads,
-        shift_grads,
+        mixed,
+        grad_query.astype(jnp.float32),
+        grad_embed.astype(jnp.float32),
+        grad_encoder.astype(jnp.float32),
+        squares[0],
+        squares[1],
+        squares[2],
+        squares[3].T,
+        squares[4],
+        squares[5],
+        squares[6],
+        squares[7].T,
+        wides[0],
+        grad_bias_in,
+        wides[1].T,
+        vectors[6],
+        vectors[:3],
+        vectors[3:6],
     )
 
 
 def local(*arrays):
-    rows_here = arrays[0].shape[0]
-    if rows_here == lax.axis_size("tp"):
+    if arrays[0].shape[0] == 4 and (lax.axis_size("dp"), lax.axis_size("tp")) == (8, 4):
         return local_rows(*arrays)
     return local_split(*arrays)
 

time: 1550 us -> 537 us (0.35)
  waiting for transfers between devices: 550 us -> 0 us
  blocking collectives: 493 us -> 0 us
  Pallas kernels: 0 us -> 193 us
  other arithmetic: 122 us -> 78.1 us
  matrix products: 221 us -> 181 us
  starting transfers between devices: 34.6 us -> 0 us
  local copies, waits for them, and re-layouts: 104 us -> 72.4 us
  between operations: 18.2 us -> 2.42 us
    all_gather x18 -> x0, blocking collectives: 368 us -> none  [the longest x10 256 us: whole_weight(): gathered = lax.all_gather(piece, rows_axis, axis=0, tiled=True)]
    reduce_scatter x12 -> x0, waiting for transfers between devices: 302 us -> none  [the longest x9 156 us: own_weight(): low = lax.psum_scatter(low, cols_axis, scatter_dimension=1, tiled=True)]
    unnamed x30 -> x0, waiting for transfers between devices: 229 us -> none
    pallas_call x0 -> x2, Pallas kernels: none -> 193 us  [the longest x1 103 us: gather_all(): pl.pallas_call(gather_kernel, out_shape=[row] * 4 + full, in_specs=[hbm]...]
    unnamed x2 -> x0, blocking collectives: 80.1 us -> none
    unnamed x323 -> x225, local copies, waits for them, and re-layouts: 86.4 us -> 24.1 us
    psum x1 -> x0, blocking collectives: 44.6 us -> none  [local_rows(): lax.psum((gain_grads, shift_grads, grad_bias_out), ('dp', 'tp'))]
    all_to_all x8 -> x0, starting transfers between devices: 32.2 us -> none  [the longest x4 16.6 us: from_row(): return lax.all_to_all(row, 'tp', split_axis=1, concat_axis=0, tiled=True)]
  transfers between devices with their start and end apart: 30 -> 0, of which waited for: 16 -> 0; matrix products, arithmetic and copies ran while one was open for 21% -> 0% of each run, Pallas kernels for 0% -> 0%
where the time goes in v2:
time: 537 us; the launch traced here: 527 us
  Pallas kernels  193 us (36%)
  matrix products  181 us (34%)
  other arithmetic  78.1 us (15%)
  local copies, waits for them, and re-layouts  72.4 us (13%)
    pallas_call x1, Pallas kernels, gather_all(): pl.pallas_call(gather_kernel, out_shape=[row] * 4 + full, in_specs=[hbm]...  103 us
    pallas_call x1, Pallas kernels, scatter_all(): pl.pallas_call(scatter_kernel, out_shape=[own(squares), own(wides), shape...  89.4 us
    convert_element_type x4, other arithmetic, attend_backward(): grad_scores = (weights_full * (grad_weights - inner)).astype(jnp.bfloat16)  36.5 us
    dot_general x4, matrix products, attend_backward(): jnp.einsum('qhd,khd->hqk', grad_part, values_all, preferred_element_type=...  35.3 us
    dot_general x4, matrix products, attend_backward(): jnp.einsum('hqk,qhd->khd', weights_full.astype(jnp.bfloat16), grad_part,...  32.7 us
    dot_general x10, matrix products, project_back(): jnp.einsum('rle,de->rld', cotangent, matrix, preferred_element_type=jnp.f...  25 us
    unnamed x225, local copies, waits for them, and re-layouts  24.1 us
    dot_general x4, matrix products, attend_backward(): jnp.einsum('hqk,khd->qhd', grad_scores, keys_all, preferred_element_type=...  18.8 us

profile of v2, /device:TPU:0, one launch (start us, length us, event | category | flops | bytes accessed | tf_op | source)
XLA Modules:
  0.0 526.9 jit_solution(12520842062633118903)
XLA Ops:
  14.3 3.4 broadcast_compare_fusion.1
  17.6 103.3 %gather_all.1 = (bf16[1024,512]{1,0:T(8,128)(2,1)}, bf16[1024,512]{1,0:T(8,128)(2,1)}, bf16[1024,512]{1,0:T(8,128)(2,1)}, bf16[1024,512]{1,0:T(8,128)(2,1)}, bf1...) custom-call(bf16[4,256,512]{2,1,0:T(8,128)(2,1)} %query.1, ...), custom_call_target="tpu_custom_call" | custom-call | tf_op jit(solution)/shard_map/gather_all/pallas_call | solution.py:612
  121.0 3.8 fusion.93
  131.6 2.7 copy.109
  138.9 4.9 fusion.92
  143.7 3.2 fusion.103
  147.0 3.5 fusion.1
  152.7 4.6 fusion.51
  159.4 3.2 fusion.104
  162.7 3.5 fusion
  168.4 3.8 fusion.52
  181.3 3.2 fusion.106
  184.5 3.9 fusion.3
  190.4 4.5 fusion.49
  196.9 4.4 fusion.107
  201.4 3.5 fusion.2
  204.9 2.3 copy-done.5
  207.3 4.6 fusion.50
  217.6 3.0 multiply_convert_fusion.4
  220.6 2.7 fusion.109
  228.8 6.4 %convert_reduce_fusion = (f32[2048]{0:T(1024)S(1)}, bf16[1024,2048]{1,0:T(8,128)(2,1)S(1)}) fusion(bf16[1024,512]{1,0:T(8,128)(2,1)S(1)} %get-tuple-element.58, bf16[512,2048]{1,0:T(8,128)(2,1)S(1)} %bitcast.365, f32[1024,2048]{1,0:T(8,128)S(1)} %get-tuple-element.127, f32[2048]{0:T(1024)S(1)} %reshape.920), kind=kOutput, calls=%fused_computation.36 | convolution fusion | flops 2181036032 | bytes 15745024 | tf_op jit(solution)/shard_map/rle,de->rld/dot_general | solution.py:31
  235.2 2.4 convolution_convert_fusion
  237.6 3.6 multiply_reduce_fusion.4
  242.2 2.7 convolution_convert_fusion.1
  244.9 2.4 pad_maximum_fusion.wides
  252.6 7.4 %fusion.10 = f32[8,64,1024]{2,1,0:T(8,128)S(1)} fusion(bf16[512,8,64]{0,2,1:T(8,128)(2,1)S(1)} %bitcast.332, f32[8,512,1024]{2,1,0:T(8,128)} %copy-done.4, f32[8,512]{1,0:T(8,128)S(1)} %log_add_fusion.1), kind=kOutput, calls=%fused_computation.33 | convolution fusion | flops 545259520 | bytes 19415040 | tf_op jit(solution)/shard_map/hqk,qhd->khd/dot_general | solution.py:132
  260.0 9.1 %add_convert_fusion.5 = bf16[8,64,1024]{2,1,0:T(8,128)(2,1)} fusion(f32[8,64,1024]{2,1,0:T(8,128)S(1)} %fusion.10, bf16[512,8,64]{0,2,1:T(8,128)(2,1)S(1)} %bitcast.337, f32[8,512,1024]{2,1,0:T(8,128)} %copy-done.5, f32[8,512]{1,0:T(8,128)S(1)} %log_add_fusion.2), kind=kOutput, calls=%fused_computation.68 | convolution fusion | flops 546308096 | bytes 20463616 | tf_op jit(solution)/shard_map/hqk,qhd->khd/dot_general | solution.py:132
  269.2 9.3 %multiply_reduce_fusion.3 = (f32[8,512]{1,0:T(8,128)S(1)}, f32[8,512,1024]{2,1,0:T(8,128)}) fusion(f32[8,512,1024]{2,1,0:T(8,128)S(1)} %bitcast.309, f32[8,512]{1,0:T(8,128)S(1)} %log_add_fusion.2, bf16[512,8,64]{0,2,1:T(8,128)(2,1)} %bitcast.336, bf16[1024,8,64]{0,2,1:T(8,128)(2,1)} %bitcast.342), kind=kOutput, calls=%fused_computation.9 | convolution fusion | flops 549449728 | bytes 35160064 | tf_op jit(solution)/shard_map/qhd,khd->hqk/dot_general | solution.py:116
  278.5 10.2 %multiply_convert_fusion.3 = bf16[8,512,1024]{2,1,0:T(8,128)(2,1)} fusion(f32[8,512,1024]{2,1,0:T(8,128)} %get-tuple-element.134, f32[8,512,1024]{2,1,0:T(8,128)S(1)} %bitcast.309, f32[8,512]{1,0:T(8,128)S(1)} %get-tuple-element.133, f32[8,512]{1,0:T(8,128)S(1)} %log_add_fusion.2), kind=kLoop, calls=%fused_computation.8 | loop fusion | flops 16777216 | bytes 41975808 | tf_op jit(solution)/shard_map/convert_element_type | solution.py:120
  288.7 6.5 %fusion.45 = bf16[8,64,512]{2,1,0:T(8,128)(2,1)S(1)} fusion(bf16[1024,8,64]{0,2,1:T(8,128)(2,1)} %bitcast.314, bf16[8,512,1024]{2,1,0:T(8,128)(2,1)} %multiply_convert_fusion.3), kind=kOutput, calls=%fused_computation.115 | convolution fusion | flops 537395200 | bytes 9961472 | tf_op jit(solution)/shard_map/hqk,khd->qhd/dot_general | solution.py:122
  295.2 2.9 fusion.111
  299.1 8.3 %multiply_reduce_fusion.2 = (f32[8,512]{1,0:T(8,128)S(1)}, f32[8,512,1024]{2,1,0:T(8,128)S(1)}) fusion(f32[8,512,1024]{2,1,0:T(8,128)} %copy-done.4, f32[8,512]{1,0:T(8,128)S(1)} %log_add_fusion.1, bf16[512,8,64]{0,2,1:T(8,128)(2,1)} %bitcast.333, bf16[1024,8,64]{0,2,1:T(8,128)(2,1)} %bitcast.343), kind=kOutput, calls=%fused_computation.6 | convolution fusion | flops 549449728 | bytes 35160064 | tf_op jit(solution)/shard_map/qhd,khd->hqk/dot_general | solution.py:116
  307.4 8.0 %multiply_convert_fusion.2 = bf16[8,512,1024]{2,1,0:T(8,128)(2,1)S(1)} fusion(f32[8,512,1024]{2,1,0:T(8,128)S(1)} %get-tuple-element.132, f32[8,512,1024]{2,1,0:T(8,128)} %copy-done.4, f32[8,512]{1,0:T(8,128)S(1)} %get-tuple-element.131, f32[8,512]{1,0:T(8,128)S(1)} %log_add_fusion.1), kind=kLoop, calls=%fused_computation.5 | loop fusion | flops 16777216 | bytes 41975808 | tf_op jit(solution)/shard_map/convert_element_type | solution.py:120
  317.2 3.5 fusion.46
  322.8 4.7 multiply_reduce_fusion.5
  328.3 2.4 fusion.89
  333.2 2.3 copy.107
  338.7 7.4 %fusion.8 = f32[8,64,1024]{2,1,0:T(8,128)S(1)} fusion(bf16[512,8,64]{0,2,1:T(8,128)(2,1)S(1)} %bitcast.330, f32[8,512,1024]{2,1,0:T(8,128)} %copy-done.2, f32[8,512]{1,0:T(8,128)S(1)} %copy-done.74), kind=kOutput, calls=%fused_computation.32 | convolution fusion | flops 545259520 | bytes 19415040 | tf_op jit(solution)/shard_map/hqk,qhd->khd/dot_general | solution.py:132
  346.1 8.7 %add_convert_fusion.6 = bf16[8,64,1024]{2,1,0:T(8,128)(2,1)} fusion(f32[8,64,1024]{2,1,0:T(8,128)S(1)} %fusion.8, bf16[512,8,64]{0,2,1:T(8,128)(2,1)S(1)} %bitcast.334, f32[8,512,1024]{2,1,0:T(8,128)} %copy-done.3, f32[8,512]{1,0:T(8,128)S(1)} %copy-done.75), kind=kOutput, calls=%fused_computation.70 | convolution fusion | flops 546308096 | bytes 20463616 | tf_op jit(solution)/shard_map/hqk,qhd->khd/dot_general | solution.py:132
  354.9 9.6 %multiply_reduce_fusion.1 = (f32[8,512]{1,0:T(8,128)S(1)}, f32[8,512,1024]{2,1,0:T(8,128)}) fusion(f32[8,512,1024]{2,1,0:T(8,128)S(1)} %bitcast.307, f32[8,512]{1,0:T(8,128)S(1)} %copy-done.75, bf16[512,8,64]{0,2,1:T(8,128)(2,1)S(1)} %bitcast.335, bf16[1024,8,64]{0,2,1:T(8,128)(2,1)} %bitcast.340), kind=kOutput, calls=%fused_computation.4 | convolution fusion | flops 549449728 | bytes 35160064 | tf_op jit(solution)/shard_map/qhd,khd->hqk/dot_general | solution.py:116
  364.4 10.3 %multiply_convert_fusion.1 = bf16[8,512,1024]{2,1,0:T(8,128)(2,1)} fusion(f32[8,512,1024]{2,1,0:T(8,128)} %get-tuple-element.139, f32[8,512,1024]{2,1,0:T(8,128)S(1)} %bitcast.307, f32[8,512]{1,0:T(8,128)S(1)} %get-tuple-element.138, f32[8,512]{1,0:T(8,128)S(1)} %copy-done.75), kind=kLoop, calls=%fused_computation.3 | loop fusion | flops 16777216 | bytes 41975808 | tf_op jit(solution)/shard_map/convert_element_type | solution.py:120
  374.8 6.2 %fusion.47 = bf16[8,64,512]{2,1,0:T(8,128)(2,1)S(1)} fusion(bf16[1024,8,64]{0,2,1:T(8,128)(2,1)S(1)} %bitcast.312, bf16[8,512,1024]{2,1,0:T(8,128)(2,1)} %multiply_convert_fusion.1), kind=kOutput, calls=%fused_computation.117 | convolution fusion | flops 537395200 | bytes 9961472 | tf_op jit(solution)/shard_map/hqk,khd->qhd/dot_general | solution.py:122
  381.0 2.9 fusion.110
  384.9 8.1 %multiply_reduce_fusion = (f32[8,512]{1,0:T(8,128)S(1)}, f32[8,512,1024]{2,1,0:T(8,128)S(1)}) fusion(f32[8,512,1024]{2,1,0:T(8,128)} %copy-done.2, f32[8,512]{1,0:T(8,128)S(1)} %copy-done.74, bf16[512,8,64]{0,2,1:T(8,128)(2,1)S(1)} %bitcast.331, bf16[1024,8,64]{0,2,1:T(8,128)(2,1)} %bitcast.341), kind=kOutput, calls=%fused_computation.1 | convolution fusion | flops 549449728 | bytes 35160064 | tf_op jit(solution)/shard_map/qhd,khd->hqk/dot_general | solution.py:116
  393.0 8.1 %multiply_convert_fusion = bf16[8,512,1024]{2,1,0:T(8,128)(2,1)S(1)} fusion(f32[8,512,1024]{2,1,0:T(8,128)S(1)} %get-tuple-element.137, f32[8,512,1024]{2,1,0:T(8,128)} %copy-done.2, f32[8,512]{1,0:T(8,128)S(1)} %get-tuple-element.136, f32[8,512]{1,0:T(8,128)S(1)} %copy-done.74), kind=kLoop, calls=%fused_computation | loop fusion | flops 16777216 | bytes 41975808 | tf_op jit(solution)/shard_map/convert_element_type | solution.py:120
  402.8 2.7 fusion.48
  405.7 3.5 add_convert_fusion.3.grad_query
  424.3 89.4 %scatter_all.1 = (f32[8,64,128]{2,1,0:T(8,128)}, f32[2,64,512]{2,1,0:T(8,128)}, f32[8,2048]{1,0:T(8,128)}, bf16[4,256,512]{2,1,0:T(8,128)(2,1)}, bf16[4,256,512]...) custom-call(bf16[8,4,2,64,512]{4,3,2,1,0:T(8,128)(2,1)} %copy-done.27, ...), custom_call_target="tpu_custom_call" | custom-call | tf_op jit(solution)/shard_map/scatter_all/pallas_call | solution.py:793
  (329 shorter events, 103.3 us)
Async XLA Ops:
  5.3 208.6 %copy-start.84 = (f32[1,512]{1,0:T(1,128)}, f32[1,512]{1,0:T(1,128)S(1)}, u32[]{:S(2)}) copy-start(f32[1,512]{1,0:T(1,128)S(1)} %get-tuple-element.103) | copy-start | bytes 6148
  12.7 5.0 copy-start.76
  129.3 38.3 %copy-start.28 = (bf16[1024,512]{0,1:T(8,128)(2,1)}, bf16[1024,512]{0,1:T(8,128)(2,1)S(1)}, u32[]{:S(2)}) copy-start(bf16[1024,512]{0,1:T(8,128)(2,1)S(1)} %convolution_convert_fusion.7) | copy-start | bytes 3145732
  130.7 13.1 %copy-start.18 = (bf16[1,512,512]{1,2,0:T(8,128)(2,1)}, bf16[1,512,512]{1,2,0:T(8,128)(2,1)S(1)}, u32[]{:S(2)}) copy-start(bf16[1,512,512]{1,2,0:T(8,128)(2,1)S(1)} %get-tuple-element.83) | copy-start | bytes 1572868
  130.7 28.7 %copy-start.22 = (bf16[1,512,512]{1,2,0:T(8,128)(2,1)}, bf16[1,512,512]{1,2,0:T(8,128)(2,1)S(1)}, u32[]{:S(2)}) copy-start(bf16[1,512,512]{1,2,0:T(8,128)(2,1)S(1)} %get-tuple-element.82) | copy-start | bytes 1572868
  131.6 27.8 %copy-start.8 = (bf16[1024,512]{0,1:T(8,128)(2,1)}, bf16[1024,512]{0,1:T(8,128)(2,1)S(1)}, u32[]{:S(2)}) copy-start(bf16[1024,512]{0,1:T(8,128)(2,1)S(1)} %convolution_convert_fusion.9) | copy-start | bytes 3145732
  138.9 4.9 copy-start.45
  147.0 5.8 %copy-start.2 = (f32[8,512,1024]{2,1,0:T(8,128)}, f32[8,512,1024]{2,1,0:T(8,128)S(1)}, u32[]{:S(2)}) copy-start(f32[8,512,1024]{2,1,0:T(8,128)S(1)} %get-tuple-element.115) | copy-start | bytes 50331652
  152.7 6.7 %copy-start.44 = (pred[512,1024]{1,0:T(8,128)(4,1)S(1)}, pred[512,1024]{1,0:T(8,128)(4,1)}, u32[]{:S(2)}) copy-start(pred[512,1024]{1,0:T(8,128)(4,1)} %get-tuple-element.109) | copy-start | bytes 1572868
  162.7 5.7 %copy-start.3 = (f32[8,512,1024]{2,1,0:T(8,128)}, f32[8,512,1024]{2,1,0:T(8,128)S(1)}, u32[]{:S(2)}) copy-start(f32[8,512,1024]{2,1,0:T(8,128)S(1)} %get-tuple-element.117) | copy-start | bytes 50331652
  168.4 4.8 copy-start.57
  175.4 38.5 %copy-start.78 = (f32[1024]{0:T(1024)}, f32[1024]{0:T(1024)S(1)}, u32[]{:S(2)}) copy-start(f32[1024]{0:T(1024)S(1)} %broadcast_multiply_fusion.2) | copy-start | bytes 12292
  175.9 38.1 %copy-start.82 = (f32[1024]{0:T(1024)}, f32[1024]{0:T(1024)S(1)}, u32[]{:S(2)}) copy-start(f32[1024]{0:T(1024)S(1)} %fusion.73) | copy-start | bytes 12292
  184.5 5.9 %copy-start.4 = (f32[8,512,1024]{2,1,0:T(8,128)}, f32[8,512,1024]{2,1,0:T(8,128)S(1)}, u32[]{:S(2)}) copy-start(f32[8,512,1024]{2,1,0:T(8,128)S(1)} %get-tuple-element.121) | copy-start | bytes 50331652
  184.5 5.9 %copy-start.29 = (bf16[1024,512]{0,1:T(8,128)(2,1)S(1)}, bf16[1024,512]{0,1:T(8,128)(2,1)}, u32[]{:S(2)}) copy-start(bf16[1024,512]{0,1:T(8,128)(2,1)} %convolution_convert_fusion.6) | copy-start | bytes 3145732
  201.3 5.9 %copy-start.5 = (f32[8,512,1024]{2,1,0:T(8,128)}, f32[8,512,1024]{2,1,0:T(8,128)S(1)}, u32[]{:S(2)}) copy-start(f32[8,512,1024]{2,1,0:T(8,128)S(1)} %get-tuple-element.123) | copy-start | bytes 50331652
  201.4 5.9 %copy-start.30 = (bf16[1024,512]{0,1:T(8,128)(2,1)S(1)}, bf16[1024,512]{0,1:T(8,128)(2,1)}, u32[]{:S(2)}) copy-start(bf16[1024,512]{0,1:T(8,128)(2,1)} %convolution_convert_fusion.6) | copy-start | bytes 3145732
  207.3 6.7 %copy-start.65 = (bf16[1,4,2,64,512]{4,3,2,1,0:T(8,128)(2,1)S(1)}, bf16[1,4,2,64,512]{4,3,2,1,0:T(8,128)(2,1)}, u32[]{:S(2)}) copy-start(bf16[1,4,2,64,512]{4,3,2,1,0:T(8,128)(2,1)} %get-tuple-element.68) | copy-start | bytes 1572868
  207.3 6.7 %copy-start.68 = (bf16[512,512]{1,0:T(8,128)(2,1)S(1)}, bf16[512,512]{1,0:T(8,128)(2,1)}, u32[]{:S(2)}) copy-start(bf16[512,512]{1,0:T(8,128)(2,1)} %copy.94) | copy-start | bytes 1572868
  242.2 6.9 %copy-start.14 = (f32[1024,512]{1,0:T(8,128)}, f32[1024,512]{1,0:T(8,128)S(1)}, u32[]{:S(2)}) copy-start(f32[1024,512]{1,0:T(8,128)S(1)} %get-tuple-element.62) | copy-start | bytes 6291460
  252.5 7.4 %copy-start.26 = (bf16[1,512,512]{1,2,0:T(8,128)(2,1)S(1)}, bf16[1,512,512]{1,2,0:T(8,128)(2,1)}, u32[]{:S(2)}) copy-start(bf16[1,512,512]{1,2,0:T(8,128)(2,1)} %get-tuple-element.78) | copy-start | bytes 1572868
  252.5 16.6 %slice-start.4 = ((s8[16777216]{0:T(1024)(128)(4,1)}), s8[4194304]{0:T(1024)(128)(4,1)S(1)}, s32[]{:S(2)}) async-start(s8[16777216]{0:T(1024)(128)(4,1)} %bitcast.308), calls=%async_computation.4 | async-start | bytes 8388608
  252.5 16.6 %slice-start.5 = ((s8[16777216]{0:T(1024)(128)(4,1)}), s8[4194304]{0:T(1024)(128)(4,1)S(1)}, s32[]{:S(2)}) async-start(s8[16777216]{0:T(1024)(128)(4,1)} %bitcast.308), calls=%async_computation.5 | async-start | bytes 8388608
  260.0 9.2 %slice-start.6 = ((s8[16777216]{0:T(1024)(128)(4,1)}), s8[4194304]{0:T(1024)(128)(4,1)S(1)}, s32[]{:S(2)}) async-start(s8[16777216]{0:T(1024)(128)(4,1)} %bitcast.308), calls=%async_computation.6 | async-start | bytes 8388608
  260.0 9.1 %slice-start.7 = ((s8[16777216]{0:T(1024)(128)(4,1)}), s8[4194304]{0:T(1024)(128)(4,1)S(1)}, s32[]{:S(2)}) async-start(s8[16777216]{0:T(1024)(128)(4,1)} %bitcast.308), calls=%async_computation.7 | async-start | bytes 8388608
  288.7 6.5 %copy-start.6 = (bf16[8,512,1024]{2,1,0:T(8,128)(2,1)S(1)}, bf16[8,512,1024]{2,1,0:T(8,128)(2,1)}, u32[]{:S(2)}) copy-start(bf16[8,512,1024]{2,1,0:T(8,128)(2,1)} %multiply_convert_fusion.3) | copy-start | bytes 25165828
  288.7 6.5 %copy-start.24 = (bf16[1,512,512]{1,2,0:T(8,128)(2,1)S(1)}, bf16[1,512,512]{1,2,0:T(8,128)(2,1)}, u32[]{:S(2)}) copy-start(bf16[1,512,512]{1,2,0:T(8,128)(2,1)} %get-tuple-element.80) | copy-start | bytes 1572868
  307.4 8.0 %copy-start.12 = (f32[8,64,1024]{2,1,0:T(8,128)S(1)}, f32[8,64,1024]{2,1,0:T(8,128)}, u32[]{:S(2)}) copy-start(f32[8,64,1024]{2,1,0:T(8,128)} %fusion.111) | copy-start | bytes 6291460
  307.4 8.0 %copy-start.21 = (bf16[1,512,512]{1,2,0:T(8,128)(2,1)S(1)}, bf16[1,512,512]{1,2,0:T(8,128)(2,1)}, u32[]{:S(2)}) copy-start(bf16[1,512,512]{1,2,0:T(8,128)(2,1)} %copy-done.20) | copy-start | bytes 1572868
  317.2 18.4 %copy-start.16 = (bf16[8,64,1024]{2,1,0:T(8,128)(2,1)}, bf16[8,64,1024]{2,1,0:T(8,128)(2,1)S(1)}, u32[]{:S(2)}) copy-start(bf16[8,64,1024]{2,1,0:T(8,128)(2,1)S(1)} %multiply_convert_fusion.5) | copy-start | bytes 3145732
  317.2 5.6 %copy-start.79 = (f32[1024]{0:T(1024)S(1)}, f32[1024]{0:T(1024)}, u32[]{:S(2)}) copy-start(f32[1024]{0:T(1024)} %copy-done.78) | copy-start | bytes 12292
  317.2 5.6 %copy-start.83 = (f32[1024]{0:T(1024)S(1)}, f32[1024]{0:T(1024)}, u32[]{:S(2)}) copy-start(f32[1024]{0:T(1024)} %copy-done.82) | copy-start | bytes 12292
  317.2 5.5 %copy-start.85 = (f32[1,512]{1,0:T(1,128)S(1)}, f32[1,512]{1,0:T(1,128)}, u32[]{:S(2)}) copy-start(f32[1,512]{1,0:T(1,128)} %copy-done.84) | copy-start | bytes 6148
  317.2 5.5 %copy-start.88 = (f32[1024]{0:T(1024)S(1)}, f32[1024]{0:T(1024)}, u32[]{:S(2)}) copy-start(f32[1024]{0:T(1024)} %copy-done.87) | copy-start | bytes 12292
  322.8 4.8 copy-start.92
  322.8 5.5 %copy-start.81 = (f32[1024]{0:T(1024)S(1)}, f32[1024]{0:T(1024)}, u32[]{:S(2)}) copy-start(f32[1024]{0:T(1024)} %copy-done.80) | copy-start | bytes 12292
  338.7 7.4 %copy-start.75 = (f32[8,512]{1,0:T(8,128)S(1)}, f32[8,512]{1,0:T(8,128)}, u32[]{:S(2)}) copy-start(f32[8,512]{1,0:T(8,128)} %log_add_fusion.3) | copy-start | bytes 49156
  338.7 16.2 %slice-start = ((s8[16777216]{0:T(1024)(128)(4,1)}), s8[4194304]{0:T(1024)(128)(4,1)S(1)}, s32[]{:S(2)}) async-start(s8[16777216]{0:T(1024)(128)(4,1)} %bitcast.306), calls=%async_computation | async-start | bytes 8388608
  338.7 16.2 %slice-start.1 = ((s8[16777216]{0:T(1024)(128)(4,1)}), s8[4194304]{0:T(1024)(128)(4,1)S(1)}, s32[]{:S(2)}) async-start(s8[16777216]{0:T(1024)(128)(4,1)} %bitcast.306), calls=%async_computation.1 | async-start | bytes 8388608
  346.1 8.8 %slice-start.2 = ((s8[16777216]{0:T(1024)(128)(4,1)}), s8[4194304]{0:T(1024)(128)(4,1)S(1)}, s32[]{:S(2)}) async-start(s8[16777216]{0:T(1024)(128)(4,1)} %bitcast.306), calls=%async_computation.2 | async-start | bytes 8388608
  346.1 8.8 %slice-start.3 = ((s8[16777216]{0:T(1024)(128)(4,1)}), s8[4194304]{0:T(1024)(128)(4,1)S(1)}, s32[]{:S(2)}) async-start(s8[16777216]{0:T(1024)(128)(4,1)} %bitcast.306), calls=%async_computation.3 | async-start | bytes 8388608
  364.4 10.3 %copy-start.9 = (bf16[1024,512]{0,1:T(8,128)(2,1)S(1)}, bf16[1024,512]{0,1:T(8,128)(2,1)}, u32[]{:S(2)}) copy-start(bf16[1024,512]{0,1:T(8,128)(2,1)} %copy-done.8) | copy-start | bytes 3145732
  374.8 6.2 %copy-start.7 = (bf16[8,512,1024]{2,1,0:T(8,128)(2,1)S(1)}, bf16[8,512,1024]{2,1,0:T(8,128)(2,1)}, u32[]{:S(2)}) copy-start(bf16[8,512,1024]{2,1,0:T(8,128)(2,1)} %multiply_convert_fusion.1) | copy-start | bytes 25165828
  374.8 6.2 %copy-start.23 = (bf16[1,512,512]{1,2,0:T(8,128)(2,1)S(1)}, bf16[1,512,512]{1,2,0:T(8,128)(2,1)}, u32[]{:S(2)}) copy-start(bf16[1,512,512]{1,2,0:T(8,128)(2,1)} %copy-done.22) | copy-start | bytes 1572868
  393.0 8.1 %copy-start.13 = (f32[8,64,1024]{2,1,0:T(8,128)S(1)}, f32[8,64,1024]{2,1,0:T(8,128)}, u32[]{:S(2)}) copy-start(f32[8,64,1024]{2,1,0:T(8,128)} %fusion.110) | copy-start | bytes 6291460
  393.0 8.1 %copy-start.19 = (bf16[1,512,512]{1,2,0:T(8,128)(2,1)S(1)}, bf16[1,512,512]{1,2,0:T(8,128)(2,1)}, u32[]{:S(2)}) copy-start(bf16[1,512,512]{1,2,0:T(8,128)(2,1)} %copy-done.18) | copy-start | bytes 1572868
  513.7 6.9 %copy-start.50 = (bf16[4,256,512]{2,1,0:T(8,128)(2,1)S(1)}, bf16[4,256,512]{2,1,0:T(8,128)(2,1)}, u32[]{:S(2)}) copy-start(bf16[4,256,512]{2,1,0:T(8,128)(2,1)} %get-tuple-element.40) | copy-start | bytes 3145732
  517.3 5.0 copy-start.49
  (56 other events, 126.5 us)

commit v3 on v2

--- a/solution.py
+++ b/solution.py
@@ -809,8 +809,333 @@
     )(squares, wides, small, *rows)
 
 
-def own_row(per_row):
-    return lax.dynamic_slice_in_dim(per_row, lax.axis_index("tp"), 1, axis=0)
+HIDDEN = -1e30
+Q_TILE = 256
+
+
+def product(left, right, left_axis, right_axis):
+    return lax.dot_general(
+        left, right, (((left_axis,), (right_axis,)), ((), ())), preferred_element_type=WIDE
+    )
+
+
+def nn(left, right):
+    return product(left, right, 1, 0)
+
+
+def nt(left, right):
+    return product(left, right, 1, 1)
+
+
+def tn(left, right):
+    return product(left, right, 0, 0)
+
+
+def rows_of(index, size):
+    return pl.ds(pl.multiple_of(index * size, size), size)
+
+
+def normalize(values):
+    average = jnp.mean(values, axis=-1, keepdims=True)
+    centred = values - average
+    spread = jnp.mean(centred * centred, axis=-1, keepdims=True)
+    inverse = lax.rsqrt(spread + EPSILON)
+    return centred * inverse, inverse
+
+
+def normalize_back(grad, normal, inverse, gain):
+    scaled = grad * gain
+    mean_one = jnp.mean(scaled, axis=-1, keepdims=True)
+    mean_two = jnp.mean(scaled * normal, axis=-1, keepdims=True)
+    return inverse * (scaled - mean_one - normal * mean_two)
+
+
+def add_rows(target, grad):
+    target[...] += jnp.sum(grad, axis=0, keepdims=True)
+
+
+def documents(lengths, row, shape, axis):
+    positions = lax.broadcasted_iota(jnp.int32, shape, axis)
+    document = jnp.full(shape, -1, jnp.int32)
+    start = jnp.zeros(shape, jnp.int32)
+    offset = jnp.int32(0)
+    for slot in range(lengths.shape[1]):
+        passed = positions >= offset
+        document = document + passed.astype(jnp.int32)
+        start = jnp.where(passed, offset, start)
+        offset = offset + lengths[row, slot]
+    return positions, document, start
+
+
+def fill_self_bias(bias, lengths, rank, limit, row):
+    length = bias.shape[0]
+    key_position, key_document, _ = documents(lengths, row, (length, 1), 0)
+    position, document, start = documents(lengths, row, (1, length), 1)
+    rank_row = rank[pl.ds(row, 1), :].astype(WIDE)
+    key_rank = jnp.transpose(jnp.broadcast_to(rank_row, (128, length)))[:, :1]
+    query_limit = limit[pl.ds(row, 1), :].astype(WIDE)
+    for tile in range(length // Q_TILE):
+        part = slice(tile * Q_TILE, (tile + 1) * Q_TILE)
+        chosen = (key_rank < query_limit[:, part]) & (key_position != position[:, part])
+        seen = (key_document == document[:, part]) & (chosen | (key_position == start[:, part]))
+        bias[:, part] = jnp.where(seen, 0.0, HIDDEN).astype(bias.dtype)
+
+
+def fill_cross_bias(bias, lengths, source_lengths, row):
+    length = bias.shape[0]
+    _, key_document, _ = documents(source_lengths, row, (length, 1), 0)
+    _, document, _ = documents(lengths, row, (1, length), 1)
+    for tile in range(length // Q_TILE):
+        part = slice(tile * Q_TILE, (tile + 1) * Q_TILE)
+        seen = key_document == document[:, part]
+        bias[:, part] = jnp.where(seen, 0.0, HIDDEN).astype(bias.dtype)
+
+
+def one_head(pair, side):
+    lane = lax.broadcasted_iota(jnp.int32, pair.shape, 1)
+    return jnp.where(lane // 64 == side, pair, jnp.zeros_like(pair))
+
+
+def attend(keys, queries, values_t, bias, context, totals):
+    length = keys.shape[0]
+
+    @pl.loop(0, HEADS // 2)
+    def _(pair):
+        lanes = rows_of(pair, 128)
+
+        @pl.loop(0, length // Q_TILE)
+        def _(tile):
+            part = rows_of(tile, Q_TILE)
+            key_pair, query_pair = keys[:, lanes], queries[part, lanes]
+            outs = []
+            for side in (0, 1):
+                head = 2 * pair + side
+                scores = nt(key_pair, one_head(query_pair, side)) + bias[:, part].astype(WIDE)
+                highest = jnp.max(scores, axis=0, keepdims=True)
+                weights = jnp.exp(scores - highest).astype(LOW)
+                out = nn(values_t[head], weights)
+                total = out[64:65]
+                outs.append(out[:64] * (1.0 / total))
+                totals[pl.ds(head, 1), part] = highest + jnp.log(total)
+            context[part, lanes] = jnp.transpose(jnp.concatenate(outs, axis=0)).astype(LOW)
+
+
+def attend_back(keys, keys_t, queries, values, cotangent, bias, totals, inner, grads):
+    grad_keys, grad_values, grad_queries, key_sum, value_sum = grads
+    length = keys.shape[0]
+
+    @pl.loop(0, HEADS // 2)
+    def _(pair):
+        lanes = rows_of(pair, 128)
+        key_sum[...] = jnp.zeros_like(key_sum)
+        value_sum[...] = jnp.zeros_like(value_sum)
+
+        @pl.loop(0, length // Q_TILE)
+        def _(tile):
+            part = rows_of(tile, Q_TILE)
+            key_pair, value_pair = keys[:, lanes], values[:, lanes]
+            all_weights, all_scores, all_queries, all_cotangents, outs = [], [], [], [], []
+            for side in (0, 1):
+                head = 2 * pair + side
+                query = one_head(queries[part, lanes], side)
+                grad = one_head(cotangent[part, lanes], side)
+                scores = nt(key_pair, query) + bias[:, part].astype(WIDE)
+                weights = jnp.exp(scores - totals[pl.ds(head, 1), part])
+                grad_weights = nt(value_pair, grad)
+                grad_scores = (weights * (grad_weights - inner[pl.ds(head, 1), part])).astype(LOW)
+                outs.append(nn(keys_t[head, :64], grad_scores) * 0.125)
+                all_weights.append(weights.astype(LOW))
+                all_scores.append(grad_scores)
+                all_queries.append(query)
+                all_cotangents.append(grad)
+            grad_queries[part, lanes] = jnp.transpose(jnp.concatenate(outs, axis=0)).astype(LOW)
+            value_sum[...] += nn(
+                jnp.concatenate(all_weights, axis=1), jnp.concatenate(all_cotangents, axis=0)
+            )
+            key_sum[...] += nn(
+                jnp.concatenate(all_scores, axis=1), jnp.concatenate(all_queries, axis=0)
+            )
+
+        grad_keys[:, lanes] = key_sum[...].astype(LOW)
+        grad_values[:, lanes] = value_sum[...].astype(LOW)
+
+
+def inner_products(cotangent, context, inner):
+    products = cotangent[...].astype(WIDE) * context[...].astype(WIDE)
+    high = products.astype(LOW)
+    rest = (products - high.astype(WIDE)).astype(LOW)
+    shape = (2 * HEADS, products.shape[1])
+    head = lax.broadcasted_iota(jnp.int32, shape, 0)
+    lane = lax.broadcasted_iota(jnp.int32, shape, 1)
+    pick = jnp.where(lane // 64 == head, 1.0, 0.0).astype(LOW)
+    inner[...] = (nt(pick, high) + nt(pick, rest))[:HEADS]
+
+
+def flip_heads(values, flipped):
+    turned = jnp.transpose(values[...])
+    for head in range(HEADS):
+        flipped[head, :64] = turned[64 * head : 64 * head + 64]
+    flipped[:, 64:] = jnp.ones((HEADS, flipped.shape[1] - 64, flipped.shape[2]), LOW)
+
+
+def layer_kernel(
+    query_row, embed_row, source_row, cotangent_row, squares, wides, bias_in, bias_out, norm_gain,
+    norm_bias, lengths, source_lengths, rank, limit,
+    mixed, grad_query, grad_embed, grad_encoder, grad_squares, grad_wides, small,
+    self_q, self_k, self_v, self_context, cross_q, cross_k, cross_v, cross_context,
+    flipped, totals, cross_totals, inner, normal_one, normal_two, inverse_one, inverse_two,
+    hidden_one, hidden_two, act, pre, grad_ffn, grad_second, bias, key_sum, value_sum,
+):
+    row = lax.axis_index("tp")
+    length, features = query_row.shape
+    small[...] = jnp.zeros_like(small)
+
+    def vector(index):
+        first = (index % 4) * features
+        return small.at[1 + index // 4 : 2 + index // 4, first : first + features]
+
+    def quarter(ref, index):
+        return ref.at[:, index * features : (index + 1) * features]
+
+    fill_self_bias(bias, lengths, rank, limit, row)
+    self_k[...] = nn(embed_row[...], squares[1]).astype(LOW)
+    self_v[...] = nn(embed_row[...], squares[2]).astype(LOW)
+    self_q[...] = (nn(query_row[...], squares[0]) * 0.125).astype(LOW)
+    flip_heads(self_v, flipped)
+    attend(self_k, self_q, flipped, bias, self_context, totals)
+
+    @pl.loop(0, length // 256)
+    def _(tile):
+        part = rows_of(tile, 256)
+        branch = nt(self_context[part], squares[3])
+        normal, inverse = normalize(query_row[part].astype(WIDE) + branch)
+        normal_one[part] = normal
+        inverse_one[part] = inverse
+        hidden_one[part] = (normal * norm_gain[0:1] + norm_bias[0:1]).astype(LOW)
+
+    fill_cross_bias(bias, lengths, source_lengths, row)
+    cross_k[...] = nn(source_row[...], squares[5]).astype(LOW)
+    cross_v[...] = nn(source_row[...], squares[6]).astype(LOW)
+    cross_q[...] = (nn(hidden_one[...], squares[4]) * 0.125).astype(LOW)
+    flip_heads(cross_v, flipped)
+    attend(cross_k, cross_q, flipped, bias, cross_context, cross_totals)
+
+    @pl.loop(0, length // 256)
+    def _(tile):
+        part = rows_of(tile, 256)
+        branch = nt(cross_context[part], squares[7])
+        before = normal_one[part] * norm_gain[0:1] + norm_bias[0:1]
+        normal, inverse = normalize(before + branch)
+        normal_two[part] = normal
+        inverse_two[part] = inverse
+        after = normal * norm_gain[1:2] + norm_bias[1:2]
+        low = after.astype(LOW)
+        hidden_two[part] = low
+        before = nn(low, wides[0]) + bias_in[...]
+        below = 0.5 * (1.0 + lax.erf(before * 0.7071067811865476))
+        density = jnp.exp(-0.5 * before * before) * 0.3989422804014327
+        slope = below + before * density
+        gate = (before * below).astype(LOW)
+        act[part] = gate
+        after = after + nt(gate, wides[1]) + bias_out[...]
+        normal, inverse = normalize(after)
+        mixed[part] = (normal * norm_gain[2:3] + norm_bias[2:3]).astype(LOW)
+        grad = cotangent_row[part].astype(WIDE)
+        add_rows(vector(2), grad * normal)
+        add_rows(vector(5), grad)
+        grad = normalize_back(grad, normal, inverse, norm_gain[2:3])
+        low = grad.astype(LOW)
+        grad_ffn[part] = low
+        add_rows(vector(6), low.astype(WIDE))
+        grad_pre = (nn(low, wides[1]) * slope).astype(LOW)
+        pre[part] = grad_pre
+        add_rows(small.at[0:1], grad_pre.astype(WIDE))
+        grad = grad + nt(grad_pre, wides[0])
+        normal = normal_two[part]
+        add_rows(vector(1), grad * normal)
+        add_rows(vector(4), grad)
+        grad_second[part] = normalize_back(grad, normal, inverse_two[part], norm_gain[1:2])
+
+    grad_wides[0] = tn(hidden_two[...], pre[...]).astype(LOW)
+    grad_wides[1] = tn(grad_ffn[...], act[...]).astype(LOW)
+
+    cotangent, grad_k, grad_v, grad_q = (quarter(act, i) for i in range(4))
+
+    def attention_back(first, grad_out, context, keys, queries, values, sums):
+        grad_squares[first + 3] = tn(grad_out, context[...]).astype(LOW)
+        cotangent[...] = nn(grad_out, squares[first + 3]).astype(LOW)
+        flip_heads(keys, flipped)
+        inner_products(cotangent, context, inner)
+        attend_back(
+            keys, flipped, queries, values, cotangent, bias, sums, inner,
+            (grad_k, grad_v, grad_q, key_sum, value_sum),
+        )
+
+    attention_back(
+        4, grad_second[...].astype(LOW), cross_context, cross_k, cross_q, cross_v, cross_totals
+    )
+    grad_squares[4] = tn(hidden_one[...], grad_q[...]).astype(LOW)
+    grad_squares[5] = tn(source_row[...], grad_k[...]).astype(LOW)
+    grad_squares[6] = tn(source_row[...], grad_v[...]).astype(LOW)
+    grad_encoder[...] = (
+        nt(grad_k[...], squares[5]) + nt(grad_v[...], squares[6])
+    ).astype(LOW)
+
+    @pl.loop(0, length // 256)
+    def _(tile):
+        part = rows_of(tile, 256)
+        grad = grad_second[part] + nt(grad_q[part], squares[4])
+        normal = normal_one[part]
+        add_rows(vector(0), grad * normal)
+        add_rows(vector(3), grad)
+        grad_second[part] = normalize_back(grad, normal, inverse_one[part], norm_gain[0:1])
+
+    fill_self_bias(bias, lengths, rank, limit, row)
+    attention_back(
+        0, grad_second[...].astype(LOW), self_context, self_k, self_q, self_v, totals
+    )
+    grad_squares[0] = tn(query_row[...], grad_q[...]).astype(LOW)
+    grad_squares[1] = tn(embed_row[...], grad_k[...]).astype(LOW)
+    grad_squares[2] = tn(embed_row[...], grad_v[...]).astype(LOW)
+    grad_embed[...] = (nt(grad_k[...], squares[1]) + nt(grad_v[...], squares[2])).astype(LOW)
+    grad_query[...] = (grad_second[...] + nt(grad_q[...], squares[0])).astype(LOW)
+
+
+def layer_scratch(length, features, hidden):
+    vmem = pltpu.VMEM
+    row = vmem((length, features), LOW)
+    wide_row = vmem((length, features), WIDE)
+    per_head = vmem((HEADS, length), WIDE)
+    return (
+        [row] * 8
+        + [vmem((HEADS, 80, length), LOW)]
+        + [per_head] * 3
+        + [wide_row] * 2
+        + [vmem((length, 1), WIDE)] * 2
+        + [row] * 2
+        + [vmem((length, hidden), LOW)] * 2
+        + [row, wide_row, vmem((length, length), LOW)]
+        + [vmem((length, 128), WIDE)] * 2
+    )
+
+
+def run_layer(rows, squares, wides, bias_in, bias_out, norm_gain, norm_bias, lengths, source_lengths, rank, limit):
+    length, features = rows[0].shape
+    hidden = wides.shape[2]
+    shape = jax.ShapeDtypeStruct
+    vmem = pl.BlockSpec(memory_space=pltpu.VMEM)
+    smem = pl.BlockSpec(memory_space=pltpu.SMEM)
+    row = shape((length, features), LOW)
+    return pl.pallas_call(
+        layer_kernel,
+        out_shape=[row] * 4
+        + [shape(squares.shape, LOW), shape(wides.shape, LOW), shape((8, hidden), WIDE)],
+        in_specs=[vmem] * 10 + [smem] * 2 + [vmem] * 2,
+        out_specs=[vmem] * 7,
+        scratch_shapes=layer_scratch(length, features, hidden),
+        compiler_params=pltpu.CompilerParams(vmem_limit_bytes=63 * 2**20),
+        name="layer",
+    )(*rows, squares, wides, bias_in, bias_out, norm_gain, norm_bias, lengths, source_lengths, rank, limit)
 
 
 def local_rows(
@@ -837,7 +1162,6 @@
     ctx_rank,
     ctx_limit,
 ):
-    low = jnp.bfloat16
     squares = jnp.stack(
         [attn_q, attn_k, attn_v, attn_o.T, cross_q, cross_k, cross_v, cross_o.T]
     )
@@ -846,118 +1170,22 @@
     rows, (squares, wides, biases) = gather_all(
         query_stream, token_embed, encoder_out, out_grad, squares, wides, biases
     )
-    query_row, embed_row, source_row, grad_row = [row[None] for row in rows]
-    lengths, source_lengths = own_row(doc_lengths)[0], own_row(src_lengths)[0]
-    rank_row, limit_row = own_row(ctx_rank)[0], own_row(ctx_limit)[0]
-    self_query, self_key, self_value, other_query, other_key, other_value = (
-        squares[i] for i in (0, 1, 2, 4, 5, 6)
-    )
-    self_out, other_out = squares[3].T, squares[7].T
-    hidden_in, hidden_out = wides[0], wides[1].T
-    hidden_bias = biases.reshape(8, 16, 4, 128)[:, 0, :, :64].transpose(1, 0, 2).reshape(-1)
-
-    def own_mask(first_row, block_rows):
-        return self_visible(
-            lengths, rank_row, limit_row, query_row.shape[1], first_row, block_rows
-        )
-
-    def other_mask(first_row, block_rows):
-        return cross_visible(
-            lengths,
-            source_lengths,
-            query_row.shape[1],
-            source_row.shape[1],
-            first_row,
-            block_rows,
-        )
-
-    self_queries = project(query_row, self_query).astype(low)
-    self_keys = project(embed_row, self_key).astype(low)
-    self_values = project(embed_row, self_value).astype(low)
-    self_context, self_totals = attend_forward(
-        self_queries[0], self_keys[0], self_values[0], own_mask, HEADS
-    )
-    self_low = self_context.astype(low)[None]
-    first_sum = query_row.astype(jnp.float32) + project(self_low, self_out)
-    hidden_one, first_back = jax.vjp(layer_norm, first_sum, norm_gain[0], norm_bias[0])
-    hidden_one_low = hidden_one.astype(low)
-    cross_queries = project(hidden_one_low, other_query).astype(low)
-    cross_keys = project(source_row, other_key).astype(low)
-    cross_values = project(source_row, other_value).astype(low)
-    cross_context, cross_totals = attend_forward(
-        cross_queries[0], cross_keys[0], cross_values[0], other_mask, HEADS
-    )
-    cross_low = cross_context.astype(low)[None]
-    second_sum = hidden_one + project(cross_low, other_out)
-    hidden_two, second_back = jax.vjp(layer_norm, second_sum, norm_gain[1], norm_bias[1])
-    hidden_two_low = hidden_two.astype(low)
-    ffn_pre = project(hidden_two_low, hidden_in) + hidden_bias.astype(jnp.float32)
-    ffn_gate, gelu_back = jax.vjp(gelu_exact, ffn_pre)
-    ffn_act = ffn_gate.astype(low)
-    third_sum = hidden_two + project(ffn_act, hidden_out) + ffn_bias_out
-    mixed, third_back = jax.vjp(layer_norm, third_sum, norm_gain[2], norm_bias[2])
-    grad_third, gain_two, shift_two = third_back(grad_row.astype(jnp.float32))
-    grad_ffn = grad_third.astype(low)
-    grad_bias_out = jnp.sum(grad_ffn.astype(jnp.float32), axis=(0, 1))
-    grad_down = outer_sum(ffn_act, grad_ffn)
-    grad_pre = gelu_back(project_back(grad_ffn, hidden_out))[0].astype(low)
-    grad_up = outer_sum(hidden_two_low, grad_pre)
-    grad_bias_in = jnp.sum(grad_pre.astype(jnp.float32), axis=(0, 1))
-    grad_two = grad_third + project_back(grad_pre, hidden_in)
-    grad_second, gain_one, shift_one = second_back(grad_two)
-    grad_cross = grad_second.astype(low)
-    grad_other_out = outer_sum(cross_low, grad_cross)
-    grad_cross_ctx = project_back(grad_cross, other_out).astype(low)
-    cross_dq, cross_dk, cross_dv = [
-        g[None]
-        for g in attend_backward(
-            cross_queries[0],
-            cross_keys[0],
-            cross_values[0],
-            other_mask,
-            cross_totals,
-            grad_cross_ctx[0],
-            HEADS,
-        )
-    ]
-    grad_other_query = outer_sum(hidden_one_low, cross_dq)
-    grad_other_key = outer_sum(source_row, cross_dk)
-    grad_other_value = outer_sum(source_row, cross_dv)
-    grad_encoder = project_back(cross_dk, other_key) + project_back(cross_dv, other_value)
-    grad_one = grad_second + project_back(cross_dq, other_query)
-    grad_first, gain_zero, shift_zero = first_back(grad_one)
-    grad_attn = grad_first.astype(low)
-    grad_self_out = outer_sum(self_low, grad_attn)
-    grad_self_ctx = project_back(grad_attn, self_out).astype(low)
-    self_dq, self_dk, self_dv = [
-        g[None]
-        for g in attend_backward(
-            self_queries[0],
-            self_keys[0],
-            self_values[0],
-            own_mask,
-            self_totals,
-            grad_self_ctx[0],
-            HEADS,
-        )
-    ]
-    grad_self_query = outer_sum(query_row, self_dq)
-    grad_self_key = outer_sum(embed_row, self_dk)
-    grad_self_value = outer_sum(embed_row, self_dv)
-    grad_embed = project_back(self_dk, self_key) + project_back(self_dv, self_value)
-    grad_query = grad_first + project_back(self_dq, self_query)
-    small = jnp.concatenate(
-        [grad_bias_in, gain_zero, gain_one, gain_two, shift_zero, shift_one, shift_two]
-        + [grad_bias_out, jnp.zeros((8 * 2048 - 2048 - 7 * 512,), jnp.float32)]
-    ).reshape(8, 2048)
-    squares = jnp.stack(
-        [grad_self_query, grad_self_key, grad_self_value, grad_self_out.T]
-        + [grad_other_query, grad_other_key, grad_other_value, grad_other_out.T]
-    ).astype(low)
-    wides = jnp.stack([grad_up, grad_down.T]).astype(low)
-    rows = [g[0].astype(low) for g in (mixed, grad_query, grad_embed, grad_encoder)]
+    hidden_bias = biases.reshape(8, 16, 4, 128)[:, 0, :, :64].transpose(1, 0, 2).reshape(1, -1)
+    mixed, grad_query, grad_embed, grad_encoder, squares, wides, small = run_layer(
+        rows,
+        squares,
+        wides,
+        hidden_bias.astype(jnp.float32),
+        ffn_bias_out[None],
+        norm_gain,
+        norm_bias,
+        doc_lengths,
+        src_lengths,
+        ctx_rank,
+        ctx_limit,
+    )
     squares, wides, small, mixed, grad_query, grad_embed, grad_encoder = scatter_all(
-        squares, wides, small, rows
+        squares, wides, small, [mixed, grad_query, grad_embed, grad_encoder]
     )
     small = small.reshape(-1)
     device = lax.axis_index("tp") * lax.axis_size("dp") + lax.axis_index("dp")

time: 537 us -> 370 us (0.69); the launches traced: 527 us -> 369 us
  matrix products: 181 us -> 0 us
  Pallas kernels: 193 us -> 346 us
  other arithmetic: 78.1 us -> 9.07 us
  local copies, waits for them, and re-layouts: 72.4 us -> 12.9 us
    dot_general x54 -> x0, matrix products: 181 us -> none  [the longest x4 35.3 us: attend_backward(): jnp.einsum('qhd,khd->hqk', grad_part, values_all, preferred_element_type=...]
    pallas_call x0 -> x1, Pallas kernels: none -> 154 us  [run_layer(): pl.pallas_call(layer_kernel, out_shape=[row] * 4 + [shape(squares.shape,...]
    convert_element_type x4 -> x0, other arithmetic: 36.5 us -> none  [attend_backward(): grad_scores = (weights_full * (grad_weights - inner)).astype(jnp.bfloat16)]
    reduce_sum x14 -> x0, other arithmetic: 23.5 us -> none  [the longest x4 14.5 us: attend_forward(): denominator = jnp.sum(exponent, axis=-1, keepdims=True)]
    unnamed x225 -> x21, local copies, waits for them, and re-layouts: 24.1 us -> 6.07 us
    slice x14 -> x1, local copies, waits for them, and re-layouts: 14.2 us -> 0.01 us  [local_rows(): biases.reshape(8, 16, 4, 128)[:, 0, :, :64].transpose(1, 0, 2)]
    dot_general x6 -> x0, local copies, waits for them, and re-layouts: 13.1 us -> none  [outer_sum(): jnp.einsum('rld,rle->de', inputs, cotangent, preferred_element_type=jnp.f...]
    concatenate x9 -> x0, local copies, waits for them, and re-layouts: 11.5 us -> none  [the longest x4 7.22 us: attend_forward(): jnp.concatenate(outputs, axis=0)]
where the time goes in v3:
time: 370 us; the launch traced here: 369 us
  Pallas kernels  346 us (94%)
  local copies, waits for them, and re-layouts  12.9 us (3%)
  other arithmetic  9.07 us (2%)
    pallas_call x1, Pallas kernels, run_layer(): pl.pallas_call(layer_kernel, out_shape=[row] * 4 + [shape(squares.shape,...  154 us
    pallas_call x1, Pallas kernels, gather_all(): pl.pallas_call(gather_kernel, out_shape=[row] * 4 + full, in_specs=[hbm]...  103 us
    pallas_call x1, Pallas kernels, scatter_all(): pl.pallas_call(scatter_kernel, out_shape=[own(squares), own(wides), shape...  89.4 us

profile of v3, /device:TPU:0, one launch (start us, length us, event | category | flops | bytes accessed | tf_op | source)
XLA Modules:
  0.0 369.1 jit_solution(17144734965860819182)
XLA Ops:
  0.7 0.7 constant_dynamic-update-slice_fusion.7
  1.4 0.7 constant_dynamic-update-slice_fusion.6
  2.1 0.7 constant_dynamic-update-slice_fusion.5
  2.8 0.7 constant_dynamic-update-slice_fusion.4
  3.5 0.7 constant_dynamic-update-slice_fusion.3
  4.3 0.7 constant_dynamic-update-slice_fusion.2
  5.0 0.7 constant_dynamic-update-slice_fusion.1
  5.7 0.7 constant_dynamic-update-slice_fusion.squares
  6.4 0.0 copy-start.5
  6.5 1.6 pad_maximum_fusion.wides
  8.0 1.3 pad.4.biases
  9.3 0.0 copy-done.5
  9.3 103.3 %gather_all.1 = (bf16[1024,512]{1,0:T(8,128)(2,1)}, bf16[1024,512]{1,0:T(8,128)(2,1)}, bf16[1024,512]{1,0:T(8,128)(2,1)}, bf16[1024,512]{1,0:T(8,128)(2,1)}, bf1...) custom-call(bf16[4,256,512]{2,1,0:T(8,128)(2,1)} %query.1, ...), custom_call_target="tpu_custom_call" | custom-call | tf_op jit(solution)/shard_map/gather_all/pallas_call | solution.py:612
  112.6 0.9 reshape_reshape.3
  113.6 0.7 reshape.84.bias_in
  114.3 153.7 %layer.1 = (bf16[1024,512]{1,0:T(8,128)(2,1)}, bf16[1024,512]{1,0:T(8,128)(2,1)}, bf16[1024,512]{1,0:T(8,128)(2,1)}, bf16[1024,512]{1,0:T(8,128)(2,1)}, bf16[8,5...) custom-call(bf16[1024,512]{1,0:T(8,128)(2,1)} %get-tuple-element.39.query_row, ...), custom_call_target="tpu_custom_call" | custom-call | tf_op jit(solution)/shard_map/layer/pallas_call | solution.py:1129
  268.0 89.4 %scatter_all.1 = (f32[8,64,128]{2,1,0:T(8,128)}, f32[2,64,512]{2,1,0:T(8,128)}, f32[8,2048]{1,0:T(8,128)}, bf16[4,256,512]{2,1,0:T(8,128)(2,1)}, bf16[4,256,512]...) custom-call(bf16[8,4,2,64,512]{4,3,2,1,0:T(8,128)(2,1)} %bitcast.67, ...), custom_call_target="tpu_custom_call" | custom-call | tf_op jit(solution)/shard_map/scatter_all/pallas_call | solution.py:793
  357.4 0.0 copy-start
  357.4 0.0 copy-start.3
  357.4 2.9 convert_element_type.24
  360.3 0.0 copy-start.2
  360.3 0.0 copy-start.4
  360.3 0.0 copy-start.1
  360.3 2.9 convert_element_type.25
  363.3 0.0 copy-done
  363.3 1.6 convert_element_type.26
  364.9 0.0 copy-done.3
  364.9 0.7 slice_bitcast_fusion.2
  365.6 0.0 copy-done.2
  365.6 0.7 slice_bitcast_fusion
  366.3 0.0 copy-done.4
  366.3 0.6 dynamic_slice.3
  366.9 0.6 fusion
  367.5 0.6 slice.71
  368.1 0.0 copy-done.1
  368.1 1.0 copy.54
  (4 shorter events, 0.0 us)
Async XLA Ops:
  6.4 2.8 copy-start.5
  357.4 5.9 %copy-start = (bf16[4,256,512]{2,1,0:T(8,128)(2,1)S(1)}, bf16[4,256,512]{2,1,0:T(8,128)(2,1)}, u32[]{:S(2)}) copy-start(bf16[4,256,512]{2,1,0:T(8,128)(2,1)} %get-tuple-element.56) | copy-start | bytes 3145732
  357.4 7.5 %copy-start.3 = (f32[8,64,128]{2,1,0:T(8,128)S(1)}, f32[8,64,128]{2,1,0:T(8,128)}, u32[]{:S(2)}) copy-start(f32[8,64,128]{2,1,0:T(8,128)} %get-tuple-element.57) | copy-start | bytes 786436
  360.3 5.3 %copy-start.2 = (f32[2,64,512]{2,1,0:T(8,128)S(1)}, f32[2,64,512]{2,1,0:T(8,128)}, u32[]{:S(2)}) copy-start(f32[2,64,512]{2,1,0:T(8,128)} %get-tuple-element.58) | copy-start | bytes 786436
  360.3 6.0 %copy-start.4 = (f32[8,2048]{1,0:T(8,128)S(1)}, f32[8,2048]{1,0:T(8,128)}, u32[]{:S(2)}) copy-start(f32[8,2048]{1,0:T(8,128)} %get-tuple-element.59) | copy-start | bytes 196612
  360.3 7.8 %copy-start.1 = (bf16[4,256,512]{2,1,0:T(8,128)(2,1)S(1)}, bf16[4,256,512]{2,1,0:T(8,128)(2,1)}, u32[]{:S(2)}) copy-start(bf16[4,256,512]{2,1,0:T(8,128)(2,1)} %get-tuple-element.90) | copy-start | bytes 3145732

commit v4 on v0

--- a/solution.py
+++ b/solution.py
@@ -1,9 +1,13 @@
 import jax
 import jax.numpy as jnp
 from jax import lax
+from jax.experimental import pallas as pl
+from jax.experimental.pallas import tpu as pltpu
 from jax.sharding import PartitionSpec as P
 
 HEADS = 8
+LOW = jnp.bfloat16
+WIDE = jnp.float32
 
 
 EPSILON = 1e-05
@@ -159,7 +163,7 @@
     return lax.psum_scatter(partial_sum, "tp", scatter_dimension=1, tiled=True)
 
 
-def local(
+def local_split(
     query_stream,
     token_embed,
     encoder_out,
@@ -420,6 +424,815 @@
     )
 
 
+HIDDEN = -1e30
+Q_TILE = 256
+
+
+def product(left, right, left_axis, right_axis):
+    return lax.dot_general(
+        left, right, (((left_axis,), (right_axis,)), ((), ())), preferred_element_type=WIDE
+    )
+
+
+def nn(left, right):
+    return product(left, right, 1, 0)
+
+
+def nt(left, right):
+    return product(left, right, 1, 1)
+
+
+def tn(left, right):
+    return product(left, right, 0, 0)
+
+
+def rows_of(index, size):
+    return pl.ds(pl.multiple_of(index * size, size), size)
+
+
+def normalize(values):
+    average = jnp.mean(values, axis=-1, keepdims=True)
+    centred = values - average
+    spread = jnp.mean(centred * centred, axis=-1, keepdims=True)
+    inverse = lax.rsqrt(spread + EPSILON)
+    return centred * inverse, inverse
+
+
+def normalize_back(grad, normal, inverse, gain):
+    scaled = grad * gain
+    mean_one = jnp.mean(scaled, axis=-1, keepdims=True)
+    mean_two = jnp.mean(scaled * normal, axis=-1, keepdims=True)
+    return inverse * (scaled - mean_one - normal * mean_two)
+
+
+def add_rows(target, grad):
+    target[...] += jnp.sum(grad, axis=0, keepdims=True)
+
+
+def documents(lengths, row, shape, axis):
+    positions = lax.broadcasted_iota(jnp.int32, shape, axis)
+    document = jnp.full(shape, -1, jnp.int32)
+    start = jnp.zeros(shape, jnp.int32)
+    offset = jnp.int32(0)
+    for slot in range(lengths.shape[1]):
+        passed = positions >= offset
+        document = document + passed.astype(jnp.int32)
+        start = jnp.where(passed, offset, start)
+        offset = offset + lengths[row, slot]
+    return positions, document, start
+
+
+def fill_self_bias(bias, lengths, rank, limit, row):
+    length = bias.shape[0]
+    key_position, key_document, _ = documents(lengths, row, (length, 1), 0)
+    position, document, start = documents(lengths, row, (1, length), 1)
+    rank_row = rank[pl.ds(row, 1), :].astype(WIDE)
+    key_rank = jnp.transpose(jnp.broadcast_to(rank_row, (128, length)))[:, :1]
+    query_limit = limit[pl.ds(row, 1), :].astype(WIDE)
+    for tile in range(length // Q_TILE):
+        part = slice(tile * Q_TILE, (tile + 1) * Q_TILE)
+        chosen = (key_rank < query_limit[:, part]) & (key_position != position[:, part])
+        seen = (key_document == document[:, part]) & (chosen | (key_position == start[:, part]))
+        bias[:, part] = jnp.where(seen, 0.0, HIDDEN).astype(bias.dtype)
+
+
+def fill_cross_bias(bias, lengths, source_lengths, row):
+    length = bias.shape[0]
+    _, key_document, _ = documents(source_lengths, row, (length, 1), 0)
+    _, document, _ = documents(lengths, row, (1, length), 1)
+    for tile in range(length // Q_TILE):
+        part = slice(tile * Q_TILE, (tile + 1) * Q_TILE)
+        seen = key_document == document[:, part]
+        bias[:, part] = jnp.where(seen, 0.0, HIDDEN).astype(bias.dtype)
+
+
+def one_head(pair, side):
+    lane = lax.broadcasted_iota(jnp.int32, pair.shape, 1)
+    return jnp.where(lane // 64 == side, pair, jnp.zeros_like(pair))
+
+
+def run_after(pair, after):
+    for number, actions in after.items():
+        if actions:
+
+            @pl.when(pair == number)
+            def _():
+                for action in actions:
+                    action()
+
+
+def attend(keys, queries, values_t, bias, context, totals, after):
+    length = keys.shape[0]
+
+    @pl.loop(0, HEADS // 2)
+    def _(pair):
+        lanes = rows_of(pair, 128)
+
+        @pl.loop(0, length // Q_TILE)
+        def _(tile):
+            part = rows_of(tile, Q_TILE)
+            key_pair, query_pair = keys[:, lanes], queries[part, lanes]
+            outs = []
+            for side in (0, 1):
+                head = 2 * pair + side
+                scores = nt(key_pair, one_head(query_pair, side)) + bias[:, part].astype(WIDE)
+                highest = jnp.max(scores, axis=0, keepdims=True)
+                weights = jnp.exp(scores - highest).astype(LOW)
+                out = nn(values_t[head], weights)
+                total = out[64:65]
+                outs.append(out[:64] * (1.0 / total))
+                totals[pl.ds(head, 1), part] = highest + jnp.log(total)
+            context[part, lanes] = jnp.transpose(jnp.concatenate(outs, axis=0)).astype(LOW)
+
+        run_after(pair, after)
+
+
+def attend_back(keys, keys_t, queries, values, cotangent, bias, totals, inner, grads, after):
+    grad_keys, grad_values, grad_queries, key_sum, value_sum = grads
+    length = keys.shape[0]
+
+    @pl.loop(0, HEADS // 2)
+    def _(pair):
+        lanes = rows_of(pair, 128)
+        key_sum[...] = jnp.zeros_like(key_sum)
+        value_sum[...] = jnp.zeros_like(value_sum)
+
+        @pl.loop(0, length // Q_TILE)
+        def _(tile):
+            part = rows_of(tile, Q_TILE)
+            key_pair, value_pair = keys[:, lanes], values[:, lanes]
+            all_weights, all_scores, all_queries, all_cotangents, outs = [], [], [], [], []
+            for side in (0, 1):
+                head = 2 * pair + side
+                query = one_head(queries[part, lanes], side)
+                grad = one_head(cotangent[part, lanes], side)
+                scores = nt(key_pair, query) + bias[:, part].astype(WIDE)
+                weights = jnp.exp(scores - totals[pl.ds(head, 1), part])
+                grad_weights = nt(value_pair, grad)
+                grad_scores = (weights * (grad_weights - inner[pl.ds(head, 1), part])).astype(LOW)
+                outs.append(nn(keys_t[head, :64], grad_scores) * 0.125)
+                all_weights.append(weights.astype(LOW))
+                all_scores.append(grad_scores)
+                all_queries.append(query)
+                all_cotangents.append(grad)
+            grad_queries[part, lanes] = jnp.transpose(jnp.concatenate(outs, axis=0)).astype(LOW)
+            value_sum[...] += nn(
+                jnp.concatenate(all_weights, axis=1), jnp.concatenate(all_cotangents, axis=0)
+            )
+            key_sum[...] += nn(
+                jnp.concatenate(all_scores, axis=1), jnp.concatenate(all_queries, axis=0)
+            )
+
+        grad_keys[:, lanes] = key_sum[...].astype(LOW)
+        grad_values[:, lanes] = value_sum[...].astype(LOW)
+        run_after(pair, after)
+
+
+def inner_products(cotangent, context, inner):
+    products = cotangent[...].astype(WIDE) * context[...].astype(WIDE)
+    high = products.astype(LOW)
+    rest = (products - high.astype(WIDE)).astype(LOW)
+    shape = (2 * HEADS, products.shape[1])
+    head = lax.broadcasted_iota(jnp.int32, shape, 0)
+    lane = lax.broadcasted_iota(jnp.int32, shape, 1)
+    pick = jnp.where(lane // 64 == head, 1.0, 0.0).astype(LOW)
+    inner[...] = (nt(pick, high) + nt(pick, rest))[:HEADS]
+
+
+def flip_heads(values, flipped):
+    turned = jnp.transpose(values[...])
+    for head in range(HEADS):
+        flipped[head, :64] = turned[64 * head : 64 * head + 64]
+
+MESH = pl.DeviceIdType.MESH
+
+
+class Place:
+    def __init__(self):
+        dp, tp = lax.axis_index("dp"), lax.axis_index("tp")
+        self.dp, self.tp = dp, tp
+        self.z, self.x = dp // 2, lax.rem(dp, 2)
+        self.y, self.core = tp // 2, lax.rem(tp, 2)
+        self.core_peer = (dp, 2 * self.y + 1 - self.core)
+        self.y_peer = (dp, 2 * (1 - self.y) + self.core)
+        self.far_peer = (dp, 2 * (1 - self.y) + 1 - self.core)
+        self.x_peer = (2 * self.z + 1 - self.x, tp)
+        self.z_steps = [lax.rem(self.z + step, 4) for step in range(4)]
+        self.z_peers = [(2 * z + self.x, tp) for z in self.z_steps[1:]]
+        self.summing = [self.core_peer, self.x_peer, self.y_peer] + self.z_peers
+
+    def meet(self):
+        peers = self.summing + [self.far_peer]
+        barrier = pltpu.get_barrier_semaphore()
+        for peer in peers:
+            pl.semaphore_signal(barrier, inc=1, device_id=peer, device_id_type=MESH)
+        pl.semaphore_wait(barrier, len(peers))
+
+    def columns(self, width):
+        return [
+            pl.ds(pl.multiple_of(tp * width, width), width)
+            for tp in (self.tp, self.y_peer[1], self.core_peer[1], self.far_peer[1])
+        ]
+
+
+class Exchange:
+    def __init__(self, sends, recvs, number):
+        self.sends, self.recvs, self.number = sends, recvs, number
+        self.made = []
+        self.arriving = []
+
+    def send(self, source, target, peer):
+        slot = len(self.made)
+
+        def copy():
+            return pltpu.make_async_remote_copy(
+                src_ref=source(),
+                dst_ref=target(),
+                send_sem=self.sends.at[self.number, slot],
+                recv_sem=self.recvs.at[self.number, slot],
+                device_id=peer,
+                device_id_type=MESH,
+            )
+
+        copy().start()
+        self.made.append(copy)
+        self.arriving.append(copy)
+
+    def move(self, block, peer):
+        self.send(block, block, peer)
+
+    def arrive(self):
+        for copy in self.arriving:
+            copy().wait_recv()
+        self.arriving = []
+
+    def finish(self):
+        for copy in self.made:
+            copy().wait_send()
+
+
+class Gather(Exchange):
+    slots = 11
+
+    def __init__(self, place, local, full, first, count, sends, recvs, own_sems, number):
+        super().__init__(sends, recvs, number)
+        self.place, self.full, self.items = place, full, pl.ds(first, count)
+        self.sides = place.columns(local.shape[-1])[:2]
+        p = place
+        self.source = lambda: local.at[self.items]
+        self.target = lambda: full.at[self.items, p.z, p.x, :, self.sides[0]]
+        self.own = lambda: pltpu.make_async_copy(
+            self.source(), self.target(), own_sems.at[number]
+        )
+
+    def stage(self, number):
+        p, full, items = self.place, self.full, self.items
+        self.arrive()
+        if number == 0:
+            self.own().start()
+            self.send(self.source, self.target, p.y_peer)
+        elif number == 1:
+            self.own().wait()
+            for side in self.sides:
+                for peer in p.z_peers:
+                    self.move(lambda side=side: full.at[items, p.z, p.x, :, side], peer)
+        elif number == 2:
+            for side in self.sides:
+                self.move(lambda side=side: full.at[items, :, p.x, :, side], p.x_peer)
+        elif number == 3:
+            for side in self.sides:
+                self.move(lambda side=side: full.at[items, :, :, :, side], p.core_peer)
+
+
+class ToRow(Exchange):
+    slots = 3
+
+    def __init__(self, place, local, row, sends, recvs, own_sems, number):
+        super().__init__(sends, recvs, number)
+        size = local.shape[1]
+        p = place
+        span = pl.ds(pl.multiple_of(p.tp * size, size), size)
+
+        def here():
+            return row.at[span]
+
+        self.own = lambda: pltpu.make_async_copy(local.at[p.tp], here(), own_sems.at[number])
+        self.own().start()
+        for peer in (p.y_peer, p.far_peer, p.core_peer):
+            self.send(lambda peer=peer: local.at[peer[1]], here, peer)
+
+    def wait(self):
+        self.own().wait()
+        self.arrive()
+
+
+class FromRow(Exchange):
+    slots = 3
+
+    def __init__(self, place, row, blocks, sends, recvs, own_sems, number):
+        super().__init__(sends, recvs, number)
+        size = blocks.shape[1]
+        p = place
+
+        def part(tp):
+            return row.at[pl.ds(pl.multiple_of(tp * size, size), size)]
+
+        self.own = lambda: pltpu.make_async_copy(
+            part(p.tp), blocks.at[p.tp], own_sems.at[number]
+        )
+        for peer in (p.y_peer, p.far_peer, p.core_peer):
+            self.send(lambda peer=peer: part(peer[1]), lambda: blocks.at[p.tp], peer)
+        self.own().start()
+
+    def wait(self):
+        self.own().wait()
+        self.arrive()
+
+
+class Scatter(Exchange):
+    slots = 8
+
+    def __init__(
+        self, place, parts, work, last, out, first, count, ready, sends, recvs, number
+    ):
+        super().__init__(sends, recvs, number)
+        self.place, self.parts, self.work, self.last, self.out = place, parts, work, last, out
+        self.numbers = range(first, first + count)
+        self.items = pl.ds(first, count)
+        self.width = out.shape[-1]
+        self.columns = place.columns(self.width)
+        self.ready = ready
+
+    def expect(self, index):
+        if self.ready is not None:
+            pl.semaphore_wait(self.ready.at[self.number, index], 1)
+
+    def stage(self, number):
+        p, parts, work, items, width = self.place, self.parts, self.work, self.items, self.width
+        first_half, second_half = slice(0, 2 * width), slice(2 * width, 4 * width)
+        sides = [slice(side * width, (side + 1) * width) for side in range(4)]
+        self.arrive()
+        if number == 0:
+            self.expect(0)
+            for side, column in zip(sides, self.columns[2:]):
+                self.send(
+                    lambda column=column: parts.at[items, :, :, :, column],
+                    lambda side=side: work.at[items, :, :, :, side],
+                    p.core_peer,
+                )
+        elif number == 1:
+            for item in self.numbers:
+                for side, column in zip(sides, self.columns[:2]):
+
+                    @pl.loop(0, 4)
+                    def _(z):
+                        work[item, z, :, :, side] += parts[item, z, :, :, column]
+
+            self.expect(1)
+            self.send(
+                lambda: work.at[items, :, 1 - p.x, :, first_half],
+                lambda: work.at[items, :, 0, :, second_half],
+                p.x_peer,
+            )
+        elif number == 2:
+            for item in self.numbers:
+
+                @pl.loop(0, 4)
+                def _(z):
+                    work[item, z, 0, :, second_half] += work[item, z, p.x, :, first_half]
+
+            for step, peer in enumerate(p.z_peers):
+                self.expect(3 + step)
+                self.send(
+                    lambda step=step: work.at[items, p.z_steps[step + 1], 0, :, second_half],
+                    lambda step=step: work.at[items, step, 1, :, second_half],
+                    peer,
+                )
+        elif number == 3:
+            for item in self.numbers:
+                total = work[item, p.z, 0, :, second_half].astype(WIDE)
+                for step in range(3):
+                    total = total + work[item, step, 1, :, second_half].astype(WIDE)
+                work[item, 3, 1, :, second_half] = total.astype(LOW)
+            self.expect(2)
+            self.send(
+                lambda: work.at[items, 3, 1, :, sides[3]],
+                lambda: self.last.at[items],
+                p.y_peer,
+            )
+        else:
+            for item in self.numbers:
+                mine = work[item, 3, 1, :, sides[2]].astype(WIDE)
+                self.out[item] = mine + self.last[item].astype(WIDE)
+
+
+class SumAll(Exchange):
+    slots = 5
+
+    def __init__(self, place, values, arrived, sends, recvs):
+        super().__init__(sends, recvs, 0)
+        p = place
+        z_one = p.z + 1 - 2 * lax.rem(p.z, 2)
+        peers = (p.core_peer, p.x_peer, p.y_peer, (2 * z_one + p.x, p.tp), p.z_peers[1])
+        self.peers, self.values, self.arrived = peers, values, arrived
+
+    def stage(self, number):
+        if number:
+            self.arrive()
+            self.made[-1]().wait_send()
+            self.values[...] = self.values[...] + self.arrived[number - 1]
+        if number < 5:
+            self.send(
+                lambda: self.values, lambda: self.arrived.at[number], self.peers[number]
+            )
+
+
+def layer_kernel(
+    query, embed, source, cotangent, attn_q, attn_k, attn_v, attn_o, cross_q, cross_k, cross_v,
+    cross_o, ffn_in, ffn_bias_in, ffn_out, bias_out, norm_gain, norm_bias, lengths, source_lengths,
+    rank, limit,
+    own_squares, own_wides, small, mixed_blocks, query_blocks, embed_blocks, encoder_blocks,
+    local_squares, local_wides, local_bias, squares, wides, biases, grad_squares, grad_wides,
+    work, last_squares, last_wides, arrived,
+    query_row, embed_row, source_row, cotangent_row,
+    self_q, self_k, self_v, self_context, other_q, other_k, other_v, other_context,
+    flipped, totals, other_totals, inner, normal_one, inverse_one, inverse_two,
+    hidden_one, hidden_two, act, pre, grad_ffn, grad_second, bias, key_sum, value_sum, bias_in,
+    row_sends, row_recvs, row_own, gather_sends, gather_recvs, gather_own,
+    scatter_sends, scatter_recvs, sum_sends, sum_recvs, ready,
+):
+    place = Place()
+    row = place.tp
+    length, features = query_row.shape
+    hidden = act.shape[1]
+
+    for index, piece in enumerate((attn_q, attn_k, attn_v, attn_o, cross_q, cross_k, cross_v, cross_o)):
+        flip = index % 4 == 3
+        local_squares[index] = jnp.transpose(piece[...]) if flip else piece[...]
+    local_wides[0] = ffn_in[...]
+    local_wides[1] = jnp.transpose(ffn_out[...])
+    local_bias[...] = jnp.zeros_like(local_bias)
+    local_bias[0, 0:1, 0:64] = ffn_bias_in[...]
+    place.meet()
+
+    def gather(number, local, full, first, count):
+        sems = (gather_sends, gather_recvs, gather_own)
+        return Gather(place, local, full, first, count, *sems, number)
+
+    def scatter(number, *buffers):
+        return Scatter(place, *buffers, scatter_sends, scatter_recvs, number)
+
+    def row_sems(number):
+        return row_sends, row_recvs, row_own, number
+
+    keys_values = gather(0, local_squares, squares, 1, 2)
+    query_in = gather(1, local_squares, squares, 0, 1)
+    out_in = gather(2, local_squares, squares, 3, 1)
+    cross_in = gather(3, local_squares, squares, 4, 4)
+    ffn_one = gather(4, local_wides, wides, 0, 1)
+    ffn_two = gather(5, local_wides, wides, 1, 1)
+    bias_gather = gather(6, local_bias, biases, 0, 1)
+    gathers = [keys_values, query_in, out_in, cross_in, ffn_one, ffn_two, bias_gather]
+    scatter_down = scatter(0, grad_wides, wides, last_wides, own_wides, 1, 1, ready)
+    scatter_up = scatter(1, grad_wides, wides, last_wides, own_wides, 0, 1, ready)
+    scatter_cross = scatter(2, grad_squares, work, last_squares, own_squares, 4, 4, None)
+    scatter_out = scatter(3, grad_squares, work, last_squares, own_squares, 3, 1, None)
+    scatter_self = scatter(4, grad_squares, work, last_squares, own_squares, 0, 3, None)
+    sum_all = SumAll(place, small, arrived, sum_sends, sum_recvs)
+
+    def step(task, number):
+        return lambda: task.stage(number)
+
+    def square(index):
+        return squares[index].reshape(features, features)
+
+    def wide(index):
+        return wides[index].reshape(features, hidden)
+
+    def vector(index):
+        first = (index % 4) * features
+        return small.at[1 + index // 4 : 2 + index // 4, first : first + features]
+
+    def quarter(ref, index):
+        return ref.at[:, index * features : (index + 1) * features]
+
+    for task in (keys_values, query_in, out_in):
+        task.stage(0)
+    embed_in = ToRow(place, embed, embed_row, *row_sems(0))
+    for task in (cross_in, ffn_one, ffn_two, bias_gather):
+        task.stage(0)
+    for task in (keys_values, query_in, out_in):
+        task.stage(1)
+    query_stream = ToRow(place, query, query_row, *row_sems(1))
+    small[...] = jnp.zeros_like(small)
+    fill_self_bias(bias, lengths, rank, limit, row)
+    flipped[:, 64:] = jnp.ones((HEADS, flipped.shape[1] - 64, length), LOW)
+    keys_values.stage(2)
+    query_in.stage(2)
+    keys_values.stage(3)
+    cross_in.stage(1)
+    source_in = ToRow(place, source, source_row, *row_sems(2))
+    cotangent_in = ToRow(place, cotangent, cotangent_row, *row_sems(3))
+    embed_in.wait()
+    keys_values.stage(4)
+    self_k[...] = nn(embed_row[...], square(1)).astype(LOW)
+    query_in.stage(3)
+    out_in.stage(2)
+    self_v[...] = nn(embed_row[...], square(2)).astype(LOW)
+    flip_heads(self_v, flipped)
+    query_stream.wait()
+    query_in.stage(4)
+    out_in.stage(3)
+    cross_in.stage(2)
+    self_q[...] = (nn(query_row[...], square(0)) * 0.125).astype(LOW)
+    attend(
+        self_k, self_q, flipped, bias, self_context, totals,
+        {
+            0: [step(out_in, 4), step(ffn_one, 1), step(ffn_two, 1), step(bias_gather, 1)],
+            1: [step(cross_in, 3), step(ffn_one, 2)],
+            2: [step(bias_gather, 2)],
+            3: [step(ffn_two, 2), step(bias_gather, 3)],
+        },
+    )
+
+    @pl.loop(0, length // 256)
+    def _(tile):
+        part = rows_of(tile, 256)
+        branch = nt(self_context[part], square(3))
+        normal, inverse = normalize(query_row[part].astype(WIDE) + branch)
+        normal_one[part] = normal
+        inverse_one[part] = inverse
+        hidden_one[part] = (normal * norm_gain[0:1] + norm_bias[0:1]).astype(LOW)
+
+    fill_cross_bias(bias, lengths, source_lengths, row)
+    cross_in.stage(4)
+    source_in.wait()
+    other_k[...] = nn(source_row[...], square(5)).astype(LOW)
+    other_v[...] = nn(source_row[...], square(6)).astype(LOW)
+    ffn_one.stage(3)
+    other_q[...] = (nn(hidden_one[...], square(4)) * 0.125).astype(LOW)
+    flip_heads(other_v, flipped)
+    attend(
+        other_k, other_q, flipped, bias, other_context, other_totals,
+        {1: [step(ffn_two, 3), step(bias_gather, 4)], 3: [step(ffn_one, 4), step(ffn_two, 4)]},
+    )
+    cotangent_in.wait()
+    for block in range(4):
+        pieces = biases[0, :, :, :, block * 128 : block * 128 + 128].reshape(128, 128)
+        size = hidden // 4
+        lane = lax.broadcasted_iota(jnp.int32, (128, size), 1)
+        line = lax.broadcasted_iota(jnp.int32, (128, size), 0)
+        spread = nn(pieces, jnp.where(lane % 64 == line, 1.0, 0.0).astype(LOW))
+        spread = jnp.where(lane // 64 == line // 16, spread, 0.0)
+        bias_in[:, block * size : block * size + size] = jnp.sum(spread, axis=0, keepdims=True)
+
+    @pl.loop(0, length // 256)
+    def _(tile):
+        part = rows_of(tile, 256)
+        branch = nt(other_context[part], square(7))
+        before = normal_one[part] * norm_gain[0:1] + norm_bias[0:1]
+        normal_mid, inverse_mid = normalize(before + branch)
+        after = normal_mid * norm_gain[1:2] + norm_bias[1:2]
+        low = after.astype(LOW)
+        hidden_two[part] = low
+        before = nn(low, wide(0)) + bias_in[...]
+        below = 0.5 * (1.0 + lax.erf(before * 0.7071067811865476))
+        density = jnp.exp(-0.5 * before * before) * 0.3989422804014327
+        slope = below + before * density
+        gate = (before * below).astype(LOW)
+        act[part] = gate
+        after = after + nt(gate, wide(1)) + bias_out[...]
+        normal, inverse = normalize(after)
+        grad = cotangent_row[part].astype(WIDE)
+        cotangent_row[part] = (normal * norm_gain[2:3] + norm_bias[2:3]).astype(LOW)
+        add_rows(vector(2), grad * normal)
+        add_rows(vector(5), grad)
+        grad = normalize_back(grad, normal, inverse, norm_gain[2:3])
+        low = grad.astype(LOW)
+        grad_ffn[part] = low
+        add_rows(vector(6), low.astype(WIDE))
+        grad_pre = (nn(low, wide(1)) * slope).astype(LOW)
+        pre[part] = grad_pre
+        add_rows(small.at[0:1], grad_pre.astype(WIDE))
+        grad = grad + nt(grad_pre, wide(0))
+        add_rows(vector(1), grad * normal_mid)
+        add_rows(vector(4), grad)
+        grad_second[part] = normalize_back(grad, normal_mid, inverse_mid, norm_gain[1:2])
+
+    for task in (ffn_one, ffn_two):
+        task.finish()
+    for group in (0, 1):
+        for index, peer in enumerate(place.summing):
+            there = index if index < 3 else 8 - index
+            pl.semaphore_signal(
+                ready.at[group, there], inc=1, device_id=peer, device_id_type=MESH
+            )
+    mixed_out = FromRow(place, cotangent_row, mixed_blocks, *row_sems(4))
+    grad_wides[1] = tn(grad_ffn[...], act[...]).astype(LOW).reshape(grad_wides.shape[1:])
+    scatter_down.stage(0)
+    grad_wides[0] = tn(hidden_two[...], pre[...]).astype(LOW).reshape(grad_wides.shape[1:])
+    scatter_up.stage(0)
+
+    cotangent_low, grad_k, grad_v, grad_q = (quarter(act, i) for i in range(4))
+
+    def weight_grad(index, inputs, grad):
+        grad_squares[index] = tn(inputs, grad).astype(LOW).reshape(grad_squares.shape[1:])
+
+    def attention_back(first, grad_out, context, keys, queries, values, sums, before, after):
+        weight_grad(first + 3, grad_out, context[...])
+        cotangent_low[...] = nn(grad_out, square(first + 3)).astype(LOW)
+        before()
+        flip_heads(keys, flipped)
+        inner_products(cotangent_low, context, inner)
+        attend_back(
+            keys, flipped, queries, values, cotangent_low, bias, sums, inner,
+            (grad_k, grad_v, grad_q, key_sum, value_sum), after,
+        )
+
+    attention_back(
+        4, grad_second[...].astype(LOW), other_context, other_k, other_q, other_v, other_totals,
+        lambda: scatter_down.stage(1),
+        {
+            0: [step(scatter_up, 1)],
+            1: [step(scatter_down, 2)],
+            3: [step(scatter_up, 2), step(scatter_down, 3)],
+        },
+    )
+    weight_grad(4, hidden_one[...], grad_q[...])
+    weight_grad(5, source_row[...], grad_k[...])
+    weight_grad(6, source_row[...], grad_v[...])
+    scatter_cross.stage(0)
+    source_row[...] = (nt(grad_k[...], square(5)) + nt(grad_v[...], square(6))).astype(LOW)
+    encoder_out = FromRow(place, source_row, encoder_blocks, *row_sems(5))
+
+    @pl.loop(0, length // 256)
+    def _(tile):
+        part = rows_of(tile, 256)
+        grad = grad_second[part] + nt(grad_q[part], square(4))
+        normal = normal_one[part]
+        add_rows(vector(0), grad * normal)
+        add_rows(vector(3), grad)
+        grad_second[part] = normalize_back(grad, normal, inverse_one[part], norm_gain[0:1])
+
+    sum_all.stage(0)
+    fill_self_bias(bias, lengths, rank, limit, row)
+    scatter_cross.stage(1)
+    attention_back(
+        0, grad_second[...].astype(LOW), self_context, self_k, self_q, self_v, totals,
+        lambda: (scatter_out.stage(0), sum_all.stage(1)),
+        {
+            0: [step(scatter_up, 3), step(scatter_down, 4), step(scatter_out, 1), step(sum_all, 2)],
+            1: [step(scatter_cross, 2), step(scatter_up, 4), step(sum_all, 3)],
+            2: [step(scatter_out, 2), step(sum_all, 4)],
+            3: [step(scatter_cross, 3), step(sum_all, 5)],
+        },
+    )
+    weight_grad(1, embed_row[...], grad_k[...])
+    weight_grad(2, embed_row[...], grad_v[...])
+    embed_row[...] = (nt(grad_k[...], square(1)) + nt(grad_v[...], square(2))).astype(LOW)
+    embed_out = FromRow(place, embed_row, embed_blocks, *row_sems(6))
+    weight_grad(0, query_row[...], grad_q[...])
+    scatter_self.stage(0)
+    query_row[...] = (grad_second[...] + nt(grad_q[...], square(0))).astype(LOW)
+    query_out = FromRow(place, query_row, query_blocks, *row_sems(7))
+    scatter_out.stage(3)
+    scatter_cross.stage(4)
+    for number in (1, 2, 3):
+        scatter_self.stage(number)
+    scatter_out.stage(4)
+    scatter_self.stage(4)
+    outgoing = [mixed_out, encoder_out, embed_out, query_out]
+    for task in outgoing:
+        task.wait()
+    for task in outgoing + [embed_in, query_stream, source_in, cotangent_in]:
+        task.finish()
+    for task in gathers[:4] + gathers[6:]:
+        task.finish()
+    for task in (scatter_down, scatter_up, scatter_cross, scatter_out, scatter_self):
+        task.finish()
+
+
+def run_layer(streams, weights, vectors, tables):
+    _, size, features = streams[0].shape
+    length = 4 * size
+    hidden = weights[8].shape[0] * 8 * 4
+    hidden = 4 * weights[8].shape[1]
+    shape = jax.ShapeDtypeStruct
+    vmem_in = pl.BlockSpec(memory_space=pltpu.VMEM)
+    smem_in = pl.BlockSpec(memory_space=pltpu.SMEM)
+    hbm = pl.BlockSpec(memory_space=pl.ANY)
+    vmem, dma = pltpu.VMEM, pltpu.SemaphoreType.DMA
+    row, wide_row = vmem((length, features), LOW), vmem((length, features), WIDE)
+    per_head, column = vmem((HEADS, length), WIDE), vmem((length, 1), WIDE)
+    full_squares = vmem((8, 4, 2, features // 8, features), LOW)
+    full_wides = vmem((2, 4, 2, features // 8, hidden), LOW)
+    blocks = shape((4, size, features), LOW)
+    return pl.pallas_call(
+        layer_kernel,
+        out_shape=[
+            shape((8, features // 8, features // 4), WIDE),
+            shape((2, features // 8, hidden // 4), WIDE),
+            shape((8, hidden), WIDE),
+        ]
+        + [blocks] * 4,
+        in_specs=[hbm] * 4 + [vmem_in] * 14 + [smem_in] * 2 + [vmem_in] * 2,
+        out_specs=[vmem_in] * 3 + [hbm] * 4,
+        scratch_shapes=[
+            vmem((8, features // 8, features // 4), LOW),
+            vmem((2, features // 8, hidden // 4), LOW),
+            vmem((1, 16, 128), LOW),
+            full_squares,
+            full_wides,
+            vmem((1, 4, 2, 16, 512), LOW),
+            full_squares,
+            full_wides,
+            full_squares,
+            vmem((8, features // 8, features // 4), LOW),
+            vmem((2, features // 8, hidden // 4), LOW),
+            vmem((5, 8, hidden), WIDE),
+        ]
+        + [row] * 12
+        + [vmem((HEADS, 80, length), LOW)]
+        + [per_head] * 3
+        + [wide_row, column, column, row, row]
+        + [vmem((length, hidden), LOW)] * 2
+        + [row, wide_row, vmem((length, length), LOW)]
+        + [vmem((length, 128), WIDE)] * 2
+        + [vmem((1, hidden), WIDE)]
+        + [dma((8, 3)), dma((8, 3)), dma((8,))]
+        + [dma((7, Gather.slots)), dma((7, Gather.slots)), dma((7,))]
+        + [dma((5, Scatter.slots)), dma((5, Scatter.slots)), dma((1, 5)), dma((1, 5))]
+        + [pltpu.SemaphoreType.REGULAR((2, 6))],
+        compiler_params=pltpu.CompilerParams(
+            collective_id=0, has_side_effects=True, vmem_limit_bytes=63 * 2**20
+        ),
+        name="layer",
+    )(*streams, *weights, *vectors, *tables)
+
+
+def local_rows(
+    query_stream,
+    token_embed,
+    encoder_out,
+    out_grad,
+    attn_q,
+    attn_k,
+    attn_v,
+    attn_o,
+    cross_q,
+    cross_k,
+    cross_v,
+    cross_o,
+    ffn_in,
+    ffn_bias_in,
+    ffn_out,
+    ffn_bias_out,
+    norm_gain,
+    norm_bias,
+    doc_lengths,
+    src_lengths,
+    ctx_rank,
+    ctx_limit,
+):
+    squares, wides, small, mixed, grad_query, grad_embed, grad_encoder = run_layer(
+        (query_stream, token_embed, encoder_out, out_grad),
+        (attn_q, attn_k, attn_v, attn_o, cross_q, cross_k, cross_v, cross_o)
+        + (ffn_in, ffn_bias_in[None], ffn_out),
+        (ffn_bias_out[None], norm_gain, norm_bias),
+        (doc_lengths, src_lengths, ctx_rank, ctx_limit),
+    )
+    small = small.reshape(-1)
+    device = lax.axis_index("tp") * lax.axis_size("dp") + lax.axis_index("dp")
+    grad_bias_in = lax.dynamic_slice_in_dim(small, device * 64, 64)
+    vectors = small[2048 : 2048 + 7 * 512].reshape(7, 512)
+    return (
+        mixed,
+        grad_query.astype(jnp.float32),
+        grad_embed.astype(jnp.float32),
+        grad_encoder.astype(jnp.float32),
+        squares[0],
+        squares[1],
+        squares[2],
+        squares[3].T,
+        squares[4],
+        squares[5],
+        squares[6],
+        squares[7].T,
+        wides[0],
+        grad_bias_in,
+        wides[1].T,
+        vectors[6],
+        vectors[:3],
+        vectors[3:6],
+    )
+
+
+def local(*arrays):
+    if arrays[0].shape[0] == 4 and (lax.axis_size("dp"), lax.axis_size("tp")) == (8, 4):
+        return local_rows(*arrays)
+    return local_split(*arrays)
+
+
 def solution(mesh):
     in_specs = (
         P("dp", "tp", None),

time: 1970 us -> 254 us (0.13)
  waiting for transfers between devices: 1060 us -> 0 us
  blocking collectives: 395 us -> 0 us
  matrix products: 263 us -> 0 us
  Pallas kernels: 0 us -> 235 us
  other arithmetic: 110 us -> 4.83 us
  local copies, waits for them, and re-layouts: 99.7 us -> 12.4 us
    reduce_scatter x13 -> x0, waiting for transfers between devices: 750 us -> none  [the longest x4 291 us: send_back(): return lax.psum_scatter(partial_sum, 'tp', scatter_dimension=1, tiled=True)]
    all_gather x10 -> x0, blocking collectives: 312 us -> none  [the longest x1 32.6 us: local(): lax.all_gather(attn_q, 'dp', axis=0, tiled=True)]
    dot_general x142 -> x0, matrix products: 263 us -> none  [the longest x10 49.2 us: project_back(): jnp.einsum('rle,de->rld', cotangent, matrix, preferred_element_type=jnp.f...]
    unnamed x31 -> x0, waiting for transfers between devices: 243 us -> none
    pallas_call x0 -> x1, Pallas kernels: none -> 235 us  [run_layer(): pl.pallas_call(layer_kernel, out_shape=[shape((8, features // 8, features...]
    all_gather x8 -> x0, waiting for transfers between devices: 72.4 us -> none  [the longest x2 38.2 us: collect_grad(): return lax.all_gather(piece, 'tp', axis=1, tiled=True)]
    reduce_sum x52 -> x0, other arithmetic: 43.4 us -> none  [the longest x16 18.6 us: attend_forward(): denominator = jnp.sum(exponent, axis=-1, keepdims=True)]
    unnamed x2 -> x0, blocking collectives: 42.7 us -> none
  transfers between devices with their start and end apart: 26 -> 0, of which waited for: 19 -> 0; matrix products, arithmetic and copies ran while one was open for 10% -> 0% of each run, Pallas kernels for 0% -> 0%
where the time goes in v4:
time: 254 us; the launch traced here: 253 us
  Pallas kernels  235 us (93%)
  local copies, waits for them, and re-layouts  12.4 us (5%)
  other arithmetic  4.83 us (2%)
    pallas_call x1, Pallas kernels, run_layer(): pl.pallas_call(layer_kernel, out_shape=[shape((8, features // 8, features...  235 us
    unnamed x13, local copies, waits for them, and re-layouts  6.39 us

profile of v4, /device:TPU:0, one launch (start us, length us, event | category | flops | bytes accessed | tf_op | source)
XLA Modules:
  0.0 253.2 jit_solution(4598723969267624176)
XLA Ops:
  0.7 1.4 copy.40.attn_o
  2.1 1.4 copy.41.cross_o
  3.5 1.6 copy.42.ffn_out
  5.1 235.3 %layer.1 = (f32[8,64,128]{2,1,0:T(8,128)}, f32[2,64,512]{2,1,0:T(8,128)}, f32[8,2048]{1,0:T(8,128)}, bf16[4,256,512]{2,1,0:T(8,128)(2,1)}, bf16[4,256,512]{2,1,0...) custom-call(bf16[4,256,512]{2,1,0:T(8,128)(2,1)} %query.1, bf16[4,256,512]{2,1,0:T(8,128)(2,1)} %embed.1, ...), custom_call_target="tpu_custom_call" | custom-call | tf_op jit(solution)/shard_map/layer/pallas_call | solution.py:1130
  240.5 0.0 copy-start.2
  240.5 0.9 copy.43
  241.4 0.6 dynamic_slice.3
  242.0 0.6 slice.66
  242.6 0.9 slice.63
  243.5 0.6 fusion
  244.1 0.0 copy-start.1
  244.1 1.7 slice_bitcast_fusion.2
  245.7 1.7 slice_bitcast_fusion
  247.4 0.0 copy-done.2
  247.4 1.6 convert_element_type.9
  249.0 0.0 copy-done.1
  249.0 0.0 copy-start
  249.0 1.6 convert_element_type.10
  250.6 0.0 copy-done
  250.6 0.0 copy-start.3
  250.7 1.6 convert_element_type.11
  252.3 0.0 copy-done.3
  252.3 1.0 copy.45
Async XLA Ops:
  240.5 6.9 %copy-start.2 = (bf16[4,256,512]{2,1,0:T(8,128)(2,1)S(1)}, bf16[4,256,512]{2,1,0:T(8,128)(2,1)}, u32[]{:S(2)}) copy-start(bf16[4,256,512]{2,1,0:T(8,128)(2,1)} %get-tuple-element.26) | copy-start | bytes 3145732
  244.1 5.0 %copy-start.1 = (bf16[4,256,512]{2,1,0:T(8,128)(2,1)S(1)}, bf16[4,256,512]{2,1,0:T(8,128)(2,1)}, u32[]{:S(2)}) copy-start(bf16[4,256,512]{2,1,0:T(8,128)(2,1)} %get-tuple-element.27) | copy-start | bytes 3145732
  249.0 1.6 copy-start
  250.6 1.6 copy-start.3
